TPU v7x, 512 devices: a whole 4x4x16 slice. The times are simulated.
512 devices in a mesh: feat: 32 (over x, y, core), dp: 16 (over z).
Axes of the slice: x: 4, y: 4, z: 16, core: 2. Of those that a mesh axis runs over, the one named last changes fastest.
Arguments:
- feature_table: bfloat16 [65536, 256], P('feat'), may hold values from -6 to 6
- row_state: float32 [65536], P('feat'), may hold values from 0.01 to 1
- rel_diag: bfloat16 [4096, 256], replicated, may hold values from -103 to 103
- slot_rows: int32 [512, 32, 128], P(('feat', 'dp')), may hold values from 0 to 2047
- slot_counts: int32 [512, 32], P(('feat', 'dp')), may hold values from 1 to 128, as said below
- head_bags: int32 [131072, 16], P(('feat', 'dp')), may hold values from 0 to 4095, as said below
- tail_bags: int32 [131072, 16], P(('feat', 'dp')), may hold values from 0 to 4095, as said below
- negative_bags: int32 [8192, 16], P(('feat', 'dp')), may hold values from 0 to 4095, as said below
- relation_ids: int32 [131072], P(('feat', 'dp')), may hold values from 0 to 4095
Outputs:
- triple_loss: float32 [131072], P(('feat', 'dp'))
- new_table: bfloat16 [65536, 256], P('feat')
- new_state: float32 [65536], P('feat')
Inputs may be any that keep to these rules, and one draw needn't show every extreme that they name: `slot_counts`: for every device some owner has exactly 128 live slots. `head_bags`: each entry o * 128 + c names a live slot of its device: c < slot_counts[d, o]. `tail_bags`: each entry o * 128 + c names a live slot of its device: c < slot_counts[d, o]. `negative_bags`: each entry o * 128 + c names a live slot of its device: c < slot_counts[d, o].
All inputs are finite; a program needn't handle non-finite values.
Results may differ from a plain program's by a relative error of at most 0.007.
Values may be sent and summed in bfloat16 or wider, within the bound.
No kernel may reach another device: no remote copies, remote signals or barrier semaphores. Data moves between devices by JAX's collectives and lax.ppermute only.
A program may use at most 64 MiB of HBM per device.

v0:
```python
import jax
import jax.numpy as jnp
from jax import lax
from jax.sharding import PartitionSpec as P

score_scale = 4.0
learn_rate = 0.1


def adagrad(table_part, state_part, gradient):
    fresh_state = state_part + jnp.mean(gradient * gradient, axis=1)
    updated = (
        table_part.astype(jnp.float32) - learn_rate * gradient / jnp.sqrt(fresh_state)[:, None]
    )
    return (updated.astype(jnp.bfloat16), fresh_state)


def on_device(
    feature_table,
    row_state,
    rel_diag,
    slot_rows,
    slot_counts,
    head_bags,
    tail_bags,
    negative_bags,
    relation_ids,
):
    n_feat = lax.axis_size("feat")
    cap = slot_rows.shape[2]
    width = feature_table.shape[1]
    local_rows = feature_table.shape[0]
    trip = head_bags.shape[0]
    slot_total = n_feat * cap
    asked = lax.all_to_all(slot_rows[0], "feat", split_axis=0, concat_axis=0, tiled=True)
    served = jnp.take(feature_table, asked.reshape(-1), axis=0).reshape(asked.shape + (width,))
    returned = lax.all_to_all(served, "feat", split_axis=0, concat_axis=0, tiled=True)
    fetched = returned
    live_mask = (
        lax.broadcasted_iota(jnp.int32, (n_feat, cap), 1) < slot_counts[0][:, None]
    ).reshape(slot_total)
    fetched = jnp.where(
        live_mask[:, None], fetched.reshape(slot_total, width), jnp.zeros((), jnp.bfloat16)
    )
    all_bags = jnp.concatenate([head_bags, tail_bags, negative_bags], axis=0)
    bag_size = all_bags.shape[1]
    pooled = jnp.sum(jnp.take(fetched, all_bags, axis=0), axis=1, dtype=jnp.float32)
    entity = (pooled / bag_size).astype(jnp.bfloat16)
    heads = entity[:trip]
    tails = entity[trip : 2 * trip]
    own_negs = entity[2 * trip :]
    negs = lax.all_gather(own_negs, "feat", axis=0, tiled=True)
    rel_pick = (
        relation_ids[:, None] == lax.broadcasted_iota(jnp.int32, (trip, rel_diag.shape[0]), 1)
    ).astype(jnp.bfloat16)
    scaling = jnp.dot(rel_pick, rel_diag, preferred_element_type=jnp.float32)
    tails_f = tails.astype(jnp.float32)
    query = (heads.astype(jnp.float32) * scaling).astype(jnp.bfloat16)
    query_f = query.astype(jnp.float32)
    positive = score_scale * jnp.sum(query_f * tails_f, axis=1)
    negative_score = score_scale * jnp.einsum(
        "td,nd->tn", query, negs, preferred_element_type=jnp.float32
    )
    highest = jnp.maximum(jnp.max(negative_score, axis=1), positive)
    total = jnp.exp(positive - highest) + jnp.sum(
        jnp.exp(negative_score - highest[:, None]), axis=1
    )
    log_total = highest + jnp.log(total)
    triple_loss = log_total - positive
    p_pos = jnp.exp(positive - log_total)
    p_neg = jnp.exp(negative_score - log_total[:, None]).astype(jnp.bfloat16)
    grad_query = score_scale * (
        (p_pos - 1.0)[:, None] * tails_f + jnp.dot(p_neg, negs, preferred_element_type=jnp.float32)
    )
    grad_head = grad_query * scaling
    grad_tail = score_scale * (p_pos - 1.0)[:, None] * query_f
    grad_negative = lax.psum_scatter(
        (
            score_scale * jnp.einsum("tn,td->nd", p_neg, query, preferred_element_type=jnp.float32)
        ).astype(jnp.bfloat16),
        "feat",
        scatter_dimension=0,
        tiled=True,
    ).astype(jnp.float32)
    entity_grad = jnp.concatenate([grad_head, grad_tail, grad_negative], axis=0) / bag_size
    slot_grad = (
        jnp.zeros((slot_total, width), jnp.float32)
        .at[all_bags]
        .add(jnp.broadcast_to(entity_grad[:, None, :], (entity_grad.shape[0], bag_size, width)))
    )
    slot_grad = (
        jnp.where(live_mask[:, None], slot_grad, jnp.zeros((), jnp.float32))
        .astype(jnp.bfloat16)
        .reshape(n_feat, cap, width)
    )
    owner_grads = lax.all_to_all(slot_grad, "feat", split_axis=0, concat_axis=0, tiled=True)
    partial_value = jax.ops.segment_sum(
        owner_grads.reshape(slot_total, width).astype(jnp.float32),
        asked.reshape(-1),
        num_segments=local_rows,
    )
    whole = lax.psum(partial_value.astype(jnp.bfloat16), "dp").astype(jnp.float32)
    new_table, new_state = adagrad(feature_table, row_state, whole)
    return (triple_loss, new_table, new_state)


def solution(mesh):
    in_specs = (
        P("feat", None),
        P("feat"),
        P(),
        P(("feat", "dp"), None, None),
        P(("feat", "dp"), None),
        P(("feat", "dp"), None),
        P(("feat", "dp"), None),
        P(("feat", "dp"), None),
        P(("feat", "dp")),
    )
    out_specs = (P(("feat", "dp")), P("feat", None), P("feat"))
    return jax.shard_map(
        on_device, mesh=mesh, in_specs=in_specs, out_specs=out_specs, check_vma=False
    )
```

profile of v0, /device:TPU:2, one launch (start us, length us, event | category | flops | bytes accessed | tf_op | source)
XLA Modules:
  0.0 496.0 jit_solution(13791528045355781160)
XLA Ops:
  7.2 15.7 %all_to_all.19 = s32[32,1,128]{2,1,0:T(1,128)S(1)} all-to-all(s32[32,1,128]{2,1,0:T(1,128)} %bitcast.38), channel_id=1, replica_groups=mesh['feat'=32,'dp'=16] {'feat'}, dimensions={0} | all-to-all | bytes 32768 | tf_op jit(solution)/shard_map/all_to_all | solution.py:35
  23.0 17.2 %gather_fusion = bf16[4096,256]{1,0:T(8,128)(2,1)} fusion(bf16[2048,256]{1,0:T(8,128)(2,1)} %param.9, s32[4096]{0:T(1024)S(1)} %broadcast_clamp_fusion), kind=kCustom, calls=%fused_computation | custom fusion | bytes 4210688 | tf_op jit(solution)/shard_map/jit(_take)/gather | solution.py:36
  40.2 2.9 broadcast_select_fusion
  43.1 5.9 %all-to-all-start.1 = ((bf16[32,128,256]{2,1,0:T(8,128)(2,1)}), bf16[32,128,256]{2,1,0:T(8,128)(2,1)}, u32[]{:S(2)}, u32[]{:S(2)}) async-start(bf16[32,128,256]{2,1,0:T(8,128)(2,1)} %broadcast_select_fusion), calls=%async_computation.1 | async-start | bytes 4194304 | tf_op jit(solution)/shard_map/all_to_all | solution.py:37
  49.3 0.2 copy.20
  49.5 0.1 copy.22
  49.6 0.1 reshape.288
  49.9 25.2 %all-to-all-done.1 = bf16[32,128,256]{2,1,0:T(8,128)(2,1)} async-done(((bf16[32,128,256]{2,1,0:T(8,128)(2,1)}), bf16[32,128,256]{2,1,0:T(8,128)(2,1)}, u32[]{:S(2)}, u32[]{:S(2)}) %all-to-all-start.1) | async-done | bytes 2097184 | tf_op jit(solution)/shard_map/all_to_all | solution.py:37
  75.0 2.9 bitcast_select_fusion
  78.0 21.8 %gather_fusion.1 = bf16[8448,256]{1,0:T(8,128)(2,1)} fusion(bf16[4096,256]{1,0:T(8,128)(2,1)} %bitcast_select_fusion, s32[9216]{0:T(1024)S(1)} %pad_clamp_fusion), kind=kCustom, calls=%fused_computation.1 | custom fusion | bytes 8684544 | tf_op jit(solution)/shard_map/jit(_take)/gather | solution.py:47
  99.7 7.0 %convert_reduce_fusion = f32[528,256]{1,0:T(8,128)S(1)} fusion(bf16[528,16,256]{2,1,0:T(8,128)(2,1)} %bitcast.27, pred[528,16]{1,0:T(8,128)(4,1)S(1)} %copy.20), kind=kLoop, calls=%fused_computation.4 | loop fusion | flops 6352896 | bytes 4874496 | tf_op jit(solution)/shard_map/reduce_sum | solution.py:47
  106.8 25.0 %all_gather.3 = bf16[512,256]{1,0:T(8,128)(2,1)S(1)} all-gather(bf16[16,256]{1,0:T(8,128)(2,1)S(1)} %slice.17), channel_id=1, replica_groups=mesh['feat'=32,'dp'=16] {'feat'}, dimensions={0}, use_global_device_ids=true | all-gather | bytes 270336 | tf_op jit(solution)/shard_map/all_gather | solution.py:52
  131.8 1.5 fusion.14
  133.3 0.3 fusion.19
  133.6 0.2 exponential_reduce_fusion
  133.9 0.6 broadcast_multiply_fusion
  134.5 1.1 fusion.10
  135.6 0.1 convert_multiply_fusion.4
  135.7 1.3 fusion.12
  137.0 98.8 %reduce-scatter.2.cloned.1.call-done = bf16[16,256]{1,0:T(8,128)(2,1)} async-done(((bf16[512,256]{1,0:T(8,128)(2,1)}), bf16[16,256]{1,0:T(8,128)(2,1)}) %reduce-scatter.2.cloned.1.call-update) | async-done | bytes 8208 | tf_op jit(solution)/shard_map/reduce_scatter | solution.py:77
  235.9 0.7 convert_element_type.58
  236.6 4.0 broadcast_in_dim.67
  240.6 45.2 %scatter_custom_fusion = f32[4096,256]{1,0:T(8,128)} fusion(s32[8448]{0:T(1024)} %copy-done.3, f32[8448,256]{1,0:T(8,128)} %bitcast.28, f32[]{:T(128)} %constant.29.clone.1), kind=kCustom, calls=%fused_computation.17 | custom fusion | flops 2162688 | bytes 4194816 | tf_op jit(solution)/shard_map/scatter-add | solution.py:89
  285.8 2.6 select_convert_fusion
  288.4 31.4 %all_to_all.20 = bf16[32,128,256]{2,1,0:T(8,128)(2,1)} all-to-all(bf16[32,128,256]{2,1,0:T(8,128)(2,1)S(1)} %bitcast.30), channel_id=1, replica_groups=mesh['feat'=32,'dp'=16] {'feat'}, dimensions={0} | all-to-all | bytes 4194304 | tf_op jit(solution)/shard_map/all_to_all | solution.py:96
  319.9 22.3 %scatter_custom_fusion.1 = f32[2048,256]{1,0:T(8,128)} fusion(s32[4096]{0:T(1024)S(1)} %bitcast.33, bf16[4096,256]{1,0:T(8,128)(2,1)} %bitcast.29, f32[]{:T(128)} %constant.29.clone.1), kind=kCustom, calls=%fused_computation.5 | custom fusion | flops 2097152 | bytes 4194308 | tf_op jit(solution)/shard_map/scatter-add | solution.py:97
  342.1 2.8 convert_element_type.62
  344.9 0.6 fusion.16
  345.5 138.8 %all-reduce.2.cloned.1.call-done = bf16[2048,256]{1,0:T(8,128)(2,1)} async-done(((bf16[2048,256]{1,0:T(8,128)(2,1)}), bf16[2048,256]{1,0:T(8,128)(2,1)}) %all-reduce.2.cloned.1.call-update) | async-done | bytes 1048592 | tf_op jit(solution)/shard_map/psum | solution.py:102
  484.3 1.6 fusion.6
  485.8 0.6 fusion.18
  486.4 2.7 fusion.5
  (49 shorter events, 0.6 us)
Async XLA Ops:
  7.2 124.7 %copy-start = (bf16[4096,256]{1,0:T(8,128)(2,1)S(1)}, bf16[4096,256]{1,0:T(8,128)(2,1)}, u32[]{:S(2)}) copy-start(bf16[4096,256]{1,0:T(8,128)(2,1)} %param.11) | copy-start | bytes 6291460
  43.1 6.0 %copy-start.8 = (s32[16,16]{1,0:T(8,128)S(1)}, s32[16,16]{1,0:T(8,128)}, u32[]{:S(2)}) copy-start(s32[16,16]{1,0:T(8,128)} %param.16) | copy-start | bytes 3076
  43.1 6.2 %copy-start.4 = (s32[256,16]{0,1:T(8,128)S(1)}, s32[256,16]{0,1:T(8,128)}, u32[]{:S(2)}) copy-start(s32[256,16]{0,1:T(8,128)} %param.15) | copy-start | bytes 49156
  43.1 6.2 %copy-start.5 = (s32[256,16]{0,1:T(8,128)S(1)}, s32[256,16]{0,1:T(8,128)}, u32[]{:S(2)}) copy-start(s32[256,16]{0,1:T(8,128)} %param.14) | copy-start | bytes 49156
  43.1 6.7 %copy-start.14 = (s32[1,32]{1,0:T(1,128)S(1)}, s32[1,32]{1,0:T(1,128)}, u32[]{:S(2)}) copy-start(s32[1,32]{1,0:T(1,128)} %param.13) | copy-start | bytes 388
  43.1 31.9 %all-to-all-start.1 = ((bf16[32,128,256]{2,1,0:T(8,128)(2,1)}), bf16[32,128,256]{2,1,0:T(8,128)(2,1)}, u32[]{:S(2)}, u32[]{:S(2)}) async-start(bf16[32,128,256]{2,1,0:T(8,128)(2,1)} %broadcast_select_fusion), calls=%async_computation.1 | async-start | bytes 4194304 | tf_op jit(solution)/shard_map/all_to_all | solution.py:37
  49.0 186.8 %reduce-scatter.2.cloned.1.call-start = ((), (), s32[]{:S(2)}) async-start(), calls=%async_computation.4 | async-start | bytes 270336 | tf_op jit(solution)/shard_map/reduce_scatter | solution.py:77
  49.7 28.2 %copy-start.3 = (s32[8448]{0:T(1024)}, s32[8448]{0:T(1024)S(1)}, u32[]{:S(2)}) copy-start(s32[8448]{0:T(1024)S(1)} %reshape.288) | copy-start | bytes 101380
  49.8 28.1 %copy-start.6 = (pred[4096]{0:T(1024)(128)(4,1)}, pred[4096]{0:T(1024)(128)(4,1)S(1)}, u32[]{:S(2)}) copy-start(pred[4096]{0:T(1024)(128)(4,1)S(1)} %fusion.15) | copy-start | bytes 12292
  99.7 32.1 %copy-start.15 = (s32[256]{0:T(256)S(1)}, s32[256]{0:T(256)}, u32[]{:S(2)}) copy-start(s32[256]{0:T(256)} %param.17) | copy-start | bytes 3076
  106.8 26.5 %copy-start.2 = (bf16[528,256]{1,0:T(8,128)(2,1)}, bf16[528,256]{1,0:T(8,128)(2,1)S(1)}, u32[]{:S(2)}) copy-start(bf16[528,256]{1,0:T(8,128)(2,1)S(1)} %multiply_convert_fusion) | copy-start | bytes 811012
  133.3 2.3 copy-start.11
  134.5 1.2 copy-start.9
  135.6 348.7 %all-reduce.2.cloned.1.call-start = ((), (), s32[]{:S(2)}) async-start(), calls=%async_computation.5 | async-start | bytes 2097152 | tf_op jit(solution)/shard_map/psum | solution.py:102
  240.6 45.2 %copy-start.7 = (pred[4096]{0:T(1024)(128)(4,1)S(1)}, pred[4096]{0:T(1024)(128)(4,1)}, u32[]{:S(2)}) copy-start(pred[4096]{0:T(1024)(128)(4,1)} %copy-done.6) | copy-start | bytes 12292
  342.1 2.8 copy-start.10
  342.1 2.8 copy-start.12
  342.1 143.7 %copy-start.13 = (f32[2048]{0:T(1024)S(1)}, f32[2048]{0:T(1024)}, u32[]{:S(2)}) copy-start(f32[2048]{0:T(1024)} %param.10) | copy-start | bytes 24580
  342.1 144.3 %copy-start.1 = (bf16[2048,256]{1,0:T(8,128)(2,1)S(1)}, bf16[2048,256]{1,0:T(8,128)(2,1)}, u32[]{:S(2)}) copy-start(bf16[2048,256]{1,0:T(8,128)(2,1)} %param.9) | copy-start | bytes 3145732
Sparse Core Ops, SparseCore 0:
  135.7 100.1 reduce-scatter.1
  345.0 139.1 all-reduce.1
where the time goes:
time: 497 us; the launch traced here: 496 us
  waiting for transfers between devices  263 us (53%)
  other arithmetic  92.9 us (19%)
  blocking collectives  72.2 us (15%)
  local copies, waits for them, and re-layouts  43.6 us (9%)
  between operations  14.3 us (3%)
  starting transfers between devices  6.02 us (1%)
    psum x1, waiting for transfers between devices, on_device(): lax.psum(partial_value.astype(jnp.bfloat16), 'dp').astype(jnp.float32)  139 us
    reduce_scatter x1, waiting for transfers between devices, on_device(): lax.psum_scatter((score_scale * jnp.einsum('tn,td->nd', p_neg, query, pre...  98.8 us
    scatter-add x1, other arithmetic, on_device(): slot_grad = jnp.zeros((slot_total, width), jnp.float32).at[all_bags].add(...  45.2 us
    all_to_all x1, blocking collectives, on_device(): lax.all_to_all(slot_grad, 'feat', split_axis=0, concat_axis=0, tiled=True)  31.4 us
    all_to_all x1, waiting for transfers between devices, on_device(): lax.all_to_all(served, 'feat', split_axis=0, concat_axis=0, tiled=True)  25.2 us
    all_gather x1, blocking collectives, on_device(): negs = lax.all_gather(own_negs, 'feat', axis=0, tiled=True)  25 us
    scatter-add x1, other arithmetic, on_device(): jax.ops.segment_sum(owner_grads.reshape(slot_total, width).astype(jnp.flo...  22.3 us
    gather x1, local copies, waits for them, and re-layouts, on_device(): jnp.take(fetched, all_bags, axis=0)  21.8 us
  transfers between devices with their start and end apart: 3, of which 3 were waited for; matrix products, arithmetic and copies ran while one was open for 1% of the time, Pallas kernels for 0%

commit v1 on v0

v1 whole, which is shorter than its diff:
```python
import jax
import jax.numpy as jnp
from jax import lax
from jax.experimental import pallas as pl
from jax.experimental.pallas import tpu as pltpu
from jax.sharding import PartitionSpec as P

score_scale = 4.0
learn_rate = 0.1
f32 = jnp.float32
bf16 = jnp.bfloat16
i32 = jnp.int32
i16 = jnp.int16

VM = pl.BlockSpec(memory_space=pltpu.VMEM)
SM = pl.BlockSpec(memory_space=pltpu.SMEM)
MIB = 1 << 20


def call(body, out_shape, in_specs, scratch=(), flops=0, moved=0, limit=48):
    outs = jax.tree.map(lambda _: VM, out_shape)
    return pl.pallas_call(
        body,
        out_shape=out_shape,
        in_specs=in_specs,
        out_specs=outs,
        scratch_shapes=list(scratch),
        compiler_params=pltpu.CompilerParams(vmem_limit_bytes=limit * MIB),
        cost_estimate=pl.CostEstimate(flops=flops, bytes_accessed=moved, transcendentals=0),
    )


def shape(dims, dtype):
    return jax.ShapeDtypeStruct(dims, dtype)


def ones_where(mask):
    return jnp.where(mask, jnp.ones((), bf16), jnp.zeros((), bf16))


def narrow_iota(dims, axis):
    return lax.broadcasted_iota(i32, dims, axis).astype(i16)


def gather_rows(asked_ref, table_ref, out_ref):
    sources, cap, width = out_ref.shape
    rows = table_ref.shape[0]
    columns = asked_ref[...].T
    lanes = narrow_iota((cap, rows), 1)
    group = 8
    for first in range(0, sources, group):
        picks = [
            ones_where(lanes == columns[:, s : s + 1].astype(i16))
            for s in range(first, first + group)
        ]
        got = jnp.dot(jnp.concatenate(picks, axis=0), table_ref[...], preferred_element_type=f32)
        out_ref[first : first + group] = got.astype(bf16).reshape(group, cap, width)


def count_entries(counts_ref, bags_ref, bags_t_ref, by_item_ref, by_slot_ref):
    items, bag = bags_ref.shape
    slots = by_slot_ref.shape[0]
    cap = slots // counts_ref.shape[1]
    lane = narrow_iota((items, cap), 1)
    sub = narrow_iota((cap, items), 0)
    lane_at = lax.broadcasted_iota(i32, (1, cap), 1)
    sub_at = lax.broadcasted_iota(i32, (cap, 1), 0)

    def step(owner, carry):
        live = counts_ref[0, owner]
        base = owner * cap
        at = pl.ds(pl.multiple_of(base, cap), cap)
        total = jnp.zeros((items, cap), bf16)
        for b in range(bag):
            entry = (bags_ref[:, b : b + 1] - base).astype(i16)
            total = total + ones_where(lane == entry)
        by_item_ref[:, at] = total * jnp.where(lane_at < live, 1.0, 0.0).astype(bf16)
        total = jnp.zeros((cap, items), bf16)
        for b in range(bag):
            entry = (bags_t_ref[b : b + 1, :] - base).astype(i16)
            total = total + ones_where(sub == entry)
        by_slot_ref[at, :] = total * jnp.where(sub_at < live, 1.0, 0.0).astype(bf16)
        return carry

    lax.fori_loop(0, counts_ref.shape[1], step, 0)


def pool_negatives(counts_ref, fetched_ref, out_ref):
    bag = 16
    trip = counts_ref.shape[0] - out_ref.shape[1]
    pooled = jnp.dot(counts_ref[trip:, :], fetched_ref[...], preferred_element_type=f32)
    entity = (pooled * (1.0 / bag)).astype(bf16)
    out_ref[...] = jnp.broadcast_to(entity[None], out_ref.shape)


def pool_triples(counts_ref, fetched_ref, scaling_ref, query_ref, tails_ref, positive_ref):
    bag = 16
    trip = query_ref.shape[0]
    pooled = jnp.dot(counts_ref[: 2 * trip, :], fetched_ref[...], preferred_element_type=f32)
    entity = (pooled * (1.0 / bag)).astype(bf16)
    tails = entity[trip:]
    query = (entity[:trip].astype(f32) * scaling_ref[...]).astype(bf16)
    query_ref[...] = query
    tails_ref[...] = tails
    positive_ref[...] = score_scale * jnp.sum(
        query.astype(f32) * tails.astype(f32), axis=1, keepdims=True
    )


def score(query_ref, tails_ref, positive_ref, scaling_ref, negs_ref, loss_ref, gneg_ref, grads_ref):
    bag = 16
    trip, width = query_ref.shape
    query = query_ref[...]
    query_f = query.astype(f32)
    tails_f = tails_ref[...].astype(f32)
    negs = negs_ref[...].reshape(-1, width)
    positive = positive_ref[...]
    scores = score_scale * lax.dot_general(
        query, negs, (((1,), (1,)), ((), ())), preferred_element_type=f32
    )
    highest = jnp.maximum(jnp.max(scores, axis=1, keepdims=True), positive)
    total = jnp.exp(positive - highest) + jnp.sum(
        jnp.exp(scores - highest), axis=1, keepdims=True
    )
    log_total = highest + jnp.log(total)
    loss_ref[...] = log_total - positive
    p_pos = jnp.exp(positive - log_total)
    p_neg_f = jnp.exp(scores - log_total)
    p_neg = p_neg_f.astype(bf16)
    gneg = score_scale * jnp.dot(p_neg_f.T.astype(bf16), query, preferred_element_type=f32)
    gneg_ref[...] = gneg.astype(bf16).reshape(gneg_ref.shape)
    grad_query = score_scale * (
        (p_pos - 1.0) * tails_f + jnp.dot(p_neg, negs, preferred_element_type=f32)
    )
    grads_ref[:trip] = (grad_query * scaling_ref[...] * (1.0 / bag)).astype(bf16)
    grads_ref[trip:] = (score_scale * (p_pos - 1.0) * query_f * (1.0 / bag)).astype(bf16)


def spread(counts_ref, grads_ref, gneg_ref, out_ref):
    bag = 16
    blocks, cap, half = out_ref.shape
    gneg = jnp.sum(gneg_ref[...].astype(f32), axis=0) * (1.0 / bag)
    grads = jnp.concatenate([grads_ref[...], gneg.astype(bf16)], axis=0)
    group = 8
    for first in range(0, blocks // 2, group):
        slot = jnp.dot(
            counts_ref[first * cap : (first + group) * cap, :], grads, preferred_element_type=f32
        ).astype(bf16)
        for s in range(group):
            for h in range(2):
                out_ref[2 * (first + s) + h] = slot[
                    s * cap : (s + 1) * cap, h * half : (h + 1) * half
                ]


def flip(p):
    return ((p & 1) << 2) | (p & 2) | (p >> 2)


def collect(place_ref, own_ref, other_ref, grads_ref, out_ref, acc_ref):
    blocks, cap, half = grads_ref.shape
    rows = acc_ref.shape[0]
    chunk = rows // 8
    place = place_ref[0]
    even = (place & 1) == 0
    asked = (
        jnp.where(even, own_ref[...], other_ref[...]),
        jnp.where(even, other_ref[...], own_ref[...]),
    )
    sub = narrow_iota((rows, cap), 0)
    group = 8
    for first in range(0, blocks, group):
        picks = [
            ones_where(sub == asked[b % 2][b // 2 : b // 2 + 1, :].astype(i16))
            for b in range(first, first + group)
        ]
        part = jnp.dot(
            jnp.concatenate(picks, axis=1),
            grads_ref[first : first + group].reshape(group * cap, half),
            preferred_element_type=f32,
        )
        acc_ref[...] = part if first == 0 else acc_ref[...] + part
    for p in range(8):
        c = flip(p) ^ (place >> 1)
        out_ref[p] = acc_ref[pl.ds(pl.multiple_of(c * chunk, chunk), chunk), :].astype(bf16)


def update(place_ref, table_ref, state_ref, own_ref, other_ref, table_out_ref, state_out_ref):
    chunk, half = own_ref.shape[1:]
    place = place_ref[0]
    even = (place & 1) == 0
    for c in range(8):
        turned = c ^ (place >> 1)
        p = flip(turned)
        own, other = own_ref[p].astype(f32), other_ref[p].astype(f32)
        gradient = jnp.concatenate(
            [jnp.where(even, own, other), jnp.where(even, other, own)], axis=1
        )
        at = slice(c * chunk, (c + 1) * chunk)
        square = jnp.sum(gradient * gradient, axis=1, keepdims=True) * (1.0 / (2 * half))
        fresh = state_ref[at, :] + square
        state_out_ref[at, :] = fresh
        table_out_ref[at, :] = (
            table_ref[at, :].astype(f32) - learn_rate * gradient / jnp.sqrt(fresh)
        ).astype(bf16)


def on_device(
    feature_table,
    row_state,
    rel_diag,
    slot_rows,
    slot_counts,
    head_bags,
    tail_bags,
    negative_bags,
    relation_ids,
):
    n_feat = lax.axis_size("feat")
    n_dp = lax.axis_size("dp")
    cap = slot_rows.shape[2]
    rows, width = feature_table.shape
    trip = head_bags.shape[0]
    n_neg = negative_bags.shape[0]
    items = 2 * trip + n_neg
    slots = n_feat * cap
    half = width // 2
    place = lax.axis_index("dp").astype(i32).reshape(1)

    def swap(value, bit):
        return lax.ppermute(value, "dp", [(i, i ^ bit) for i in range(n_dp)])

    asked = lax.all_to_all(slot_rows[0], "feat", split_axis=0, concat_axis=0, tiled=True)
    asked_other = swap(asked, 1)
    served = call(
        gather_rows,
        shape((n_feat, cap, width), bf16),
        [VM, VM],
        flops=2 * slots * rows * width,
        moved=rows * width * 2 + slots * width * 2,
    )(asked, feature_table)
    fetched = lax.all_to_all(served, "feat", split_axis=0, concat_axis=0, tiled=True)
    fetched = fetched.reshape(slots, width)

    bags = jnp.concatenate([head_bags, tail_bags, negative_bags], axis=0)
    by_item, by_slot = call(
        count_entries,
        (shape((items, slots), bf16), shape((slots, items), bf16)),
        [SM, VM, VM],
        flops=8 * items * slots * 32,
        moved=4 * items * slots,
    )(slot_counts, bags, bags.T)
    rel_pick = (
        relation_ids[:, None] == lax.broadcasted_iota(i32, (trip, rel_diag.shape[0]), 1)
    ).astype(bf16)
    scaling = jnp.dot(rel_pick, rel_diag, preferred_element_type=f32)

    own_negs = call(
        pool_negatives, shape((n_feat, n_neg, width), bf16), [VM, VM], flops=2 * n_neg * slots * width
    )(by_item, fetched)
    negs = lax.all_to_all(own_negs, "feat", split_axis=0, concat_axis=0, tiled=True)
    query, tails, positive = call(
        pool_triples,
        (shape((trip, width), bf16), shape((trip, width), bf16), shape((trip, 1), f32)),
        [VM, VM, VM],
        flops=4 * trip * slots * width,
        moved=2 * slots * width,
    )(by_item, fetched, scaling)
    loss, gneg, grads = call(
        score,
        (
            shape((trip, 1), f32),
            shape((n_feat, n_neg, width), bf16),
            shape((2 * trip, width), bf16),
        ),
        [VM] * 5,
        flops=6 * trip * n_feat * n_neg * width,
    )(query, tails, positive, scaling, negs)
    gneg = lax.all_to_all(gneg, "feat", split_axis=0, concat_axis=0, tiled=True)
    slot_grad = call(
        spread,
        shape((2 * n_feat, cap, half), bf16),
        [VM, VM, VM],
        flops=2 * items * slots * width,
    )(by_slot, grads, gneg)
    pairs = [
        [f * n_dp + 2 * p + h for f in range(n_feat) for h in range(2)] for p in range(n_dp // 2)
    ]
    arrived = lax.all_to_all(
        slot_grad,
        ("feat", "dp"),
        split_axis=0,
        concat_axis=0,
        tiled=True,
        axis_index_groups=pairs,
    )
    part = call(
        collect,
        shape((8, rows // 8, half), bf16),
        [SM, VM, VM, VM],
        scratch=[pltpu.VMEM((rows, half), f32)],
        flops=4 * slots * rows * half,
    )(place, asked, asked_other, arrived)
    kept = part
    for bit in (2, 4, 8):
        n = kept.shape[0] // 2
        kept = (kept[:n].astype(f32) + swap(kept[n:], bit).astype(f32)).astype(bf16)
    for bit in (8, 4, 2):
        kept = jnp.concatenate([kept, swap(kept, bit)], axis=0)
    across = swap(kept, 1)
    new_table, new_state = call(
        update,
        (shape((rows, width), bf16), shape((rows, 1), f32)),
        [SM, VM, VM, VM, VM],
    )(place, feature_table, row_state.reshape(rows, 1), kept, across)
    return (loss.reshape(trip), new_table, new_state.reshape(rows))


def solution(mesh):
    in_specs = (
        P("feat", None),
        P("feat"),
        P(),
        P(("feat", "dp"), None, None),
        P(("feat", "dp"), None),
        P(("feat", "dp"), None),
        P(("feat", "dp"), None),
        P(("feat", "dp"), None),
        P(("feat", "dp")),
    )
    out_specs = (P(("feat", "dp")), P("feat", None), P("feat"))
    return jax.shard_map(
        on_device, mesh=mesh, in_specs=in_specs, out_specs=out_specs, check_vma=False
    )
```

time: 497 us -> 269 us (0.54)
  the two profiles are of different devices: /device:TPU:2 before, /device:TPU:1 now
where the time goes in v1:
time: 269 us; the launch traced here: 268 us
  waiting for transfers between devices  93.2 us (35%)
  Pallas kernels  66.2 us (25%)
  starting transfers between devices  64.4 us (24%)
  blocking collectives  29.9 us (11%)
  local copies, waits for them, and re-layouts  8.86 us (3%)
  other arithmetic  3.88 us (1%)
    ppermute x8, waiting for transfers between devices, swap(): return lax.ppermute(value, 'dp', [(i, i ^ bit) for i in range(n_dp)])  85.9 us
    ppermute x8, starting transfers between devices, swap(): return lax.ppermute(value, 'dp', [(i, i ^ bit) for i in range(n_dp)])  46.7 us
    pallas_call x1, Pallas kernels, on_device(): call(count_entries, (shape((items, slots), bf16), shape((slots, items), b...  34.4 us
    all_to_all x1, blocking collectives, on_device(): lax.all_to_all(slot_rows[0], 'feat', split_axis=0, concat_axis=0, tiled=T...  17.5 us
    all_to_all x1, blocking collectives, on_device(): gneg = lax.all_to_all(gneg, 'feat', split_axis=0, concat_axis=0, tiled=True)  12.5 us
    pallas_call x1, Pallas kernels, on_device(): call(collect, shape((8, rows // 8, half), bf16), [SM, VM, VM, VM], scratc...  10.7 us
    unnamed x27, local copies, waits for them, and re-layouts  8.33 us
    all_to_all x1, starting transfers between devices, on_device(): lax.all_to_all(own_negs, 'feat', split_axis=0, concat_axis=0, tiled=True)  7.49 us
  transfers between devices with their start and end apart: 11, of which 10 were waited for; matrix products, arithmetic and copies ran while one was open for 1% of the time, Pallas kernels for 14%

profile of v1, /device:TPU:1, one launch (start us, length us, event | category | flops | bytes accessed | tf_op | source)
XLA Modules:
  0.0 268.2 jit_solution(4702724904981152678)
XLA Ops:
  0.6 17.5 %all_to_all.31 = s32[32,1,128]{2,1,0:T(1,128)S(1)} all-to-all(s32[32,1,128]{2,1,0:T(1,128)} %bitcast.11), channel_id=1, replica_groups=mesh['feat'=32,'dp'=16] {'feat'}, dimensions={0} | all-to-all | bytes 32768 | tf_op jit(solution)/shard_map/all_to_all | solution.py:233
  19.3 4.6 %shard_map.113 = bf16[32,128,256]{2,1,0:T(8,128)(2,1)S(1)} custom-call(s32[32,128]{1,0:T(8,128)S(1)} %bitcast.8, bf16[2048,256]{1,0:T(8,128)(2,1)S(1)} %copy-done.4), custom_call_target="tpu_custom_call" | custom-call | flops 4294967296 | bytes 3145728 | tf_op jit(solution)/shard_map/pallas_call | solution.py:235
  25.3 5.1 %all-to-all-start.1 = ((bf16[32,128,256]{2,1,0:T(8,128)(2,1)}), bf16[32,128,256]{2,1,0:T(8,128)(2,1)}, u32[]{:S(2)}, u32[]{:S(2)}) async-start(bf16[32,128,256]{2,1,0:T(8,128)(2,1)} %copy-done.3), calls=%async_computation.1 | async-start | bytes 4194304 | tf_op jit(solution)/shard_map/all_to_all | solution.py:242
  30.7 34.4 %shard_map.112 = (bf16[528,4096]{1,0:T(8,128)(2,1)S(1)}, bf16[4096,528]{1,0:T(8,128)(2,1)}) custom-call(s32[1,32]{1,0:T(1,128)S(1)} %copy-done.7, s32[528,16]{1,0:T(8,128)S(1)} %copy.18.bags_ref, s32[16,528]{1,0:T(8,128)S(1)} %get-tuple-element.23.bags_t_ref), custom_call_target="tpu_custom_call" | custom-call | flops 553648128 | bytes 8650752 | tf_op jit(solution)/shard_map/pallas_call | solution.py:246
  65.2 2.1 copy-done.1
  67.2 4.0 %shard_map.115 = bf16[32,16,256]{2,1,0:T(8,128)(2,1)} custom-call(bf16[528,4096]{1,0:T(8,128)(2,1)} %copy-done.1, bf16[4096,256]{1,0:T(8,128)(2,1)} %bitcast.3.fetched_ref), custom_call_target="tpu_custom_call" | custom-call | flops 33554432 | tf_op jit(solution)/shard_map/pallas_call | solution.py:258
  71.3 7.5 %all-to-all-start.2 = ((bf16[32,16,256]{2,1,0:T(8,128)(2,1)}), bf16[32,16,256]{2,1,0:T(8,128)(2,1)S(1)}, u32[]{:S(2)}, u32[]{:S(2)}) async-start(bf16[32,16,256]{2,1,0:T(8,128)(2,1)} %shard_map.115), calls=%async_computation.2 | async-start | bytes 524288 | tf_op jit(solution)/shard_map/all_to_all | solution.py:261
  79.6 4.2 %shard_map.114 = (bf16[256,256]{1,0:T(8,128)(2,1)S(1)}, bf16[256,256]{1,0:T(8,128)(2,1)S(1)}, f32[256,1]{1,0:T(8,128)S(1)}) custom-call(bf16[528,4096]{1,0:T(8,128)(2,1)} %copy-done.1, bf16[4096,256]{1,0:T(8,128)(2,1)} %bitcast.3.fetched_ref, f32[256,256]{1,0:T(8,128)S(1)} %fusion.scaling_ref), custom_call_target="tpu_custom_call" | custom-call | flops 1073741824 | bytes 2097152 | tf_op jit(solution)/shard_map/pallas_call | solution.py:262
  83.8 4.0 %all-to-all-done.2.negs_ref = bf16[32,16,256]{2,1,0:T(8,128)(2,1)S(1)} async-done(((bf16[32,16,256]{2,1,0:T(8,128)(2,1)}), bf16[32,16,256]{2,1,0:T(8,128)(2,1)S(1)}, u32[]{:S(2)}, u32[]{:S(2)}) %all-to-all-start.2) | async-done | bytes 262176 | tf_op jit(solution)/shard_map/all_to_all | solution.py:261
  88.7 12.5 %all_to_all.32.gneg_ref = bf16[32,16,256]{2,1,0:T(8,128)(2,1)S(1)} all-to-all(bf16[32,16,256]{2,1,0:T(8,128)(2,1)S(1)} %get-tuple-element.20), channel_id=1, replica_groups=mesh['feat'=32,'dp'=16] {'feat'}, dimensions={0} | all-to-all | bytes 524288 | tf_op jit(solution)/shard_map/all_to_all | solution.py:279
  101.1 4.3 %shard_map.117 = bf16[64,128,128]{2,1,0:T(8,128)(2,1)S(1)} custom-call(bf16[4096,528]{1,0:T(8,128)(2,1)} %get-tuple-element.18.counts_ref, bf16[512,256]{1,0:T(8,128)(2,1)S(1)} %get-tuple-element.19.grads_ref, bf16[32,16,256]{2,1,0:T(8,128)(2,1)S(1)} %all_to_all.32.gneg_ref), custom_call_target="tpu_custom_call" | custom-call | flops 1107296256 | tf_op jit(solution)/shard_map/pallas_call | solution.py:280
  106.7 5.1 %all-to-all-start.4 = ((bf16[64,128,128]{2,1,0:T(8,128)(2,1)}), bf16[64,128,128]{2,1,0:T(8,128)(2,1)}, u32[]{:S(2)}, u32[]{:S(2)}) async-start(bf16[64,128,128]{2,1,0:T(8,128)(2,1)} %copy-done.2), calls=%async_computation.4 | async-start | bytes 4194304 | tf_op jit(solution)/shard_map/all_to_all | solution.py:289
  111.9 3.5 %collective-permute-start = (s32[32,128]{1,0:T(8,128)S(1)}, s32[32,128]{1,0:T(8,128)S(1)}, u32[]{:S(2)}, u32[]{:S(2)}) collective-permute-start(s32[32,128]{1,0:T(8,128)S(1)} %bitcast.9), channel_id=1, source_target_pairs={{0,1},{1,0},{2,3},{3,2},{4,5},{5,4},{6,7},{7,6},{8,9},{9,8},{10,11... | collective-permute-start | bytes 49160 | tf_op jit(solution)/shard_map/ppermute | solution.py:231
  115.3 21.4 %collective-permute-done.other_ref = s32[32,128]{1,0:T(8,128)S(1)} collective-permute-done((s32[32,128]{1,0:T(8,128)S(1)}, s32[32,128]{1,0:T(8,128)S(1)}, u32[]{:S(2)}, u32[]{:S(2)}) %collective-permute-start) | collective-permute-done | bytes 16416 | tf_op jit(solution)/shard_map/ppermute | solution.py:231
  136.7 3.3 %all-to-all-done.4.grads_ref = bf16[64,128,128]{2,1,0:T(8,128)(2,1)} async-done(((bf16[64,128,128]{2,1,0:T(8,128)(2,1)}), bf16[64,128,128]{2,1,0:T(8,128)(2,1)}, u32[]{:S(2)}, u32[]{:S(2)}) %all-to-all-start.4) | async-done | bytes 2097184 | tf_op jit(solution)/shard_map/all_to_all | solution.py:289
  140.0 10.7 %shard_map.118 = bf16[8,256,128]{2,1,0:T(8,128)(2,1)S(1)} custom-call(s32[1]{0:T(128)} %bitcast.4.place_ref, s32[32,128]{1,0:T(8,128)S(1)} %bitcast.10, s32[32,128]{1,0:T(8,128)S(1)} %collective-permute-done.other_ref, bf16[64,128,128]{2,1,0:T(8,128)(2,1)} %all-to-all-done.4.grads_ref), custom_call_target="tpu_custom_call" | custom-call | flops 4294967296 | tf_op jit(solution)/shard_map/pallas_call | solution.py:297
  150.7 3.4 %collective-permute-start.1 = (bf16[4,256,128]{2,1,0:T(8,128)(2,1)S(1)}, bf16[4,256,128]{2,1,0:T(8,128)(2,1)S(1)}, u32[]{:S(2)}, u32[]{:S(2)}) collective-permute-start(bf16[4,256,128]{2,1,0:T(8,128)(2,1)S(1)} %slice.25), channel_id=1, source_target_pairs={{0,2},{1,3},{2,0},{3,1},{4,6},{5,7},{6,4},{7,5},{8,10},{9,11},{10,... | collective-permute-start | bytes 786440 | tf_op jit(solution)/shard_map/ppermute | solution.py:231
  154.1 13.2 %collective-permute-done.1 = bf16[4,256,128]{2,1,0:T(8,128)(2,1)S(1)} collective-permute-done((bf16[4,256,128]{2,1,0:T(8,128)(2,1)S(1)}, bf16[4,256,128]{2,1,0:T(8,128)(2,1)S(1)}, u32[]{:S(2)}, u32[]{:S(2)}) %collective-permute-start.1) | collective-permute-done | bytes 262176 | tf_op jit(solution)/shard_map/ppermute | solution.py:231
  167.4 8.0 %collective-permute-start.2 = (bf16[2,256,128]{2,1,0:T(8,128)(2,1)S(1)}, bf16[2,256,128]{2,1,0:T(8,128)(2,1)S(1)}, u32[]{:S(2)}, u32[]{:S(2)}) collective-permute-start(bf16[2,256,128]{2,1,0:T(8,128)(2,1)S(1)} %slice.27), channel_id=1, source_target_pairs={{0,4},{1,5},{2,6},{3,7},{4,0},{5,1},{6,2},{7,3},{8,12},{9,13},{10,... | collective-permute-start | bytes 393224 | tf_op jit(solution)/shard_map/ppermute | solution.py:231
  175.4 10.6 %collective-permute-done.2 = bf16[2,256,128]{2,1,0:T(8,128)(2,1)S(1)} collective-permute-done((bf16[2,256,128]{2,1,0:T(8,128)(2,1)S(1)}, bf16[2,256,128]{2,1,0:T(8,128)(2,1)S(1)}, u32[]{:S(2)}, u32[]{:S(2)}) %collective-permute-start.2) | collective-permute-done | bytes 131104 | tf_op jit(solution)/shard_map/ppermute | solution.py:231
  186.1 12.9 %collective-permute-start.3 = (bf16[1,256,128]{2,1,0:T(8,128)(2,1)S(1)}, bf16[1,256,128]{2,1,0:T(8,128)(2,1)S(1)}, u32[]{:S(2)}, u32[]{:S(2)}) collective-permute-start(bf16[1,256,128]{2,1,0:T(8,128)(2,1)S(1)} %slice.29), channel_id=1, source_target_pairs={{0,8},{1,9},{2,10},{3,11},{4,12},{5,13},{6,14},{7,15},{8,0},{9,1},... | collective-permute-start | bytes 196616 | tf_op jit(solution)/shard_map/ppermute | solution.py:231
  199.0 1.6 collective-permute-done.3
  200.7 12.1 %collective-permute-start.4 = (bf16[1,256,128]{2,1,0:T(8,128)(2,1)S(1)}, bf16[1,256,128]{2,1,0:T(8,128)(2,1)S(1)}, u32[]{:S(2)}, u32[]{:S(2)}) collective-permute-start(bf16[1,256,128]{2,1,0:T(8,128)(2,1)S(1)} %add_convert_fusion.2), channel_id=1, source_target_pairs={{0,8},{1,9},{2,10},{3,11},{4,12},{5,13},{6,14},{7,15},{8,0},{9,1},... | collective-permute-start | bytes 196616 | tf_op jit(solution)/shard_map/ppermute | solution.py:231
  212.7 1.6 collective-permute-done.4
  214.4 3.0 %collective-permute-start.5 = (bf16[2,256,128]{2,1,0:T(8,128)(2,1)S(1)}, bf16[2,256,128]{2,1,0:T(8,128)(2,1)S(1)}, u32[]{:S(2)}, u32[]{:S(2)}) collective-permute-start(bf16[2,256,128]{2,1,0:T(8,128)(2,1)S(1)} %pad_maximum_fusion.2), channel_id=1, source_target_pairs={{0,4},{1,5},{2,6},{3,7},{4,0},{5,1},{6,2},{7,3},{8,12},{9,13},{10,... | collective-permute-start | bytes 393224 | tf_op jit(solution)/shard_map/ppermute | solution.py:231
  217.4 13.7 %collective-permute-done.5 = bf16[2,256,128]{2,1,0:T(8,128)(2,1)S(1)} collective-permute-done((bf16[2,256,128]{2,1,0:T(8,128)(2,1)S(1)}, bf16[2,256,128]{2,1,0:T(8,128)(2,1)S(1)}, u32[]{:S(2)}, u32[]{:S(2)}) %collective-permute-start.5) | collective-permute-done | bytes 131104 | tf_op jit(solution)/shard_map/ppermute | solution.py:231
  231.1 1.9 collective-permute-start.6
  233.0 11.7 %collective-permute-done.6 = bf16[4,256,128]{2,1,0:T(8,128)(2,1)S(1)} collective-permute-done((bf16[4,256,128]{2,1,0:T(8,128)(2,1)S(1)}, bf16[4,256,128]{2,1,0:T(8,128)(2,1)S(1)}, u32[]{:S(2)}, u32[]{:S(2)}) %collective-permute-start.6) | collective-permute-done | bytes 262176 | tf_op jit(solution)/shard_map/ppermute | solution.py:231
  245.6 1.9 collective-permute-start.7
  248.6 12.0 %collective-permute-done.7.other_ref = bf16[8,256,128]{2,1,0:T(8,128)(2,1)} collective-permute-done((bf16[8,256,128]{2,1,0:T(8,128)(2,1)}, bf16[8,256,128]{2,1,0:T(8,128)(2,1)}, u32[]{:S(2)}, u32[]{:S(2)}) %collective-permute-start.7) | collective-permute-done | bytes 524320 | tf_op jit(solution)/shard_map/ppermute | solution.py:231
  261.9 3.1 %shard_map.119 = (bf16[2048,256]{1,0:T(8,128)(2,1)}, f32[2048,1]{1,0:T(8,128)S(1)}) custom-call(s32[1]{0:T(128)} %bitcast.4.place_ref, bf16[2048,256]{1,0:T(8,128)(2,1)S(1)} %copy-done.5, f32[2048,1]{1,0:T(8,128)S(1)} %copy.19.state_ref, bf16[8,256,128]{2,1,0:T(8,128)(2,1)} %pad_maximum_fusion.own_ref, bf16[8,256,128]{2,1,0:T(8,128)(2,1)} %collective-permute-done.7.other_ref), custom_call_target="tpu_custom_call" | custom-call | tf_op jit(solution)/shard_map/pallas_call | solution.py:311
  266.1 2.2 reduce.1
  (42 shorter events, 10.2 us)
Async XLA Ops:
  0.6 78.1 %copy-start = (bf16[4096,256]{1,0:T(8,128)(2,1)S(1)}, bf16[4096,256]{1,0:T(8,128)(2,1)}, u32[]{:S(2)}) copy-start(bf16[4096,256]{1,0:T(8,128)(2,1)} %param.11) | copy-start | bytes 6291460
  18.1 1.2 copy-start.4
  23.9 1.4 copy-start.3
  25.3 5.2 %copy-start.11 = (s32[16,16]{1,0:T(8,128)S(1)}, s32[16,16]{1,0:T(8,128)}, u32[]{:S(2)}) copy-start(s32[16,16]{1,0:T(8,128)} %param.16) | copy-start | bytes 3076
  25.3 5.2 %copy-start.8 = (s32[256,16]{0,1:T(8,128)S(1)}, s32[256,16]{0,1:T(8,128)}, u32[]{:S(2)}) copy-start(s32[256,16]{0,1:T(8,128)} %param.15) | copy-start | bytes 49156
  25.3 5.2 %copy-start.9 = (s32[256,16]{0,1:T(8,128)S(1)}, s32[256,16]{0,1:T(8,128)}, u32[]{:S(2)}) copy-start(s32[256,16]{0,1:T(8,128)} %param.14) | copy-start | bytes 49156
  25.3 5.4 %copy-start.7 = (s32[1,32]{1,0:T(1,128)S(1)}, s32[1,32]{1,0:T(1,128)}, u32[]{:S(2)}) copy-start(s32[1,32]{1,0:T(1,128)} %counts_ref.1) | copy-start | bytes 388
  25.3 41.9 %all-to-all-start.1 = ((bf16[32,128,256]{2,1,0:T(8,128)(2,1)}), bf16[32,128,256]{2,1,0:T(8,128)(2,1)}, u32[]{:S(2)}, u32[]{:S(2)}) async-start(bf16[32,128,256]{2,1,0:T(8,128)(2,1)} %copy-done.3), calls=%async_computation.1 | async-start | bytes 4194304 | tf_op jit(solution)/shard_map/all_to_all | solution.py:242
  65.2 2.1 copy-start.1
  67.2 11.5 %copy-start.12 = (s32[256]{0:T(256)S(1)}, s32[256]{0:T(256)}, u32[]{:S(2)}) copy-start(s32[256]{0:T(256)} %param.17) | copy-start | bytes 3076
  71.3 16.5 %all-to-all-start.2 = ((bf16[32,16,256]{2,1,0:T(8,128)(2,1)}), bf16[32,16,256]{2,1,0:T(8,128)(2,1)S(1)}, u32[]{:S(2)}, u32[]{:S(2)}) async-start(bf16[32,16,256]{2,1,0:T(8,128)(2,1)} %shard_map.115), calls=%async_computation.2 | async-start | bytes 524288 | tf_op jit(solution)/shard_map/all_to_all | solution.py:261
  105.4 1.3 copy-start.2
  106.7 33.3 %all-to-all-start.4 = ((bf16[64,128,128]{2,1,0:T(8,128)(2,1)}), bf16[64,128,128]{2,1,0:T(8,128)(2,1)}, u32[]{:S(2)}, u32[]{:S(2)}) async-start(bf16[64,128,128]{2,1,0:T(8,128)(2,1)} %copy-done.2), calls=%async_computation.4 | async-start | bytes 4194304 | tf_op jit(solution)/shard_map/all_to_all | solution.py:289
  111.9 24.9 %collective-permute-start = (s32[32,128]{1,0:T(8,128)S(1)}, s32[32,128]{1,0:T(8,128)S(1)}, u32[]{:S(2)}, u32[]{:S(2)}) collective-permute-start(s32[32,128]{1,0:T(8,128)S(1)} %bitcast.9), channel_id=1, source_target_pairs={{0,1},{1,0},{2,3},{3,2},{4,5},{5,4},{6,7},{7,6},{8,9},{9,8},{10,11... | collective-permute-start | bytes 49160 | tf_op jit(solution)/shard_map/ppermute | solution.py:231
  150.7 96.9 %copy-start.10 = (f32[2048]{0:T(1024)S(1)}, f32[2048]{0:T(1024)}, u32[]{:S(2)}) copy-start(f32[2048]{0:T(1024)} %param.10) | copy-start | bytes 24580
  150.7 16.6 %collective-permute-start.1 = (bf16[4,256,128]{2,1,0:T(8,128)(2,1)S(1)}, bf16[4,256,128]{2,1,0:T(8,128)(2,1)S(1)}, u32[]{:S(2)}, u32[]{:S(2)}) collective-permute-start(bf16[4,256,128]{2,1,0:T(8,128)(2,1)S(1)} %slice.25), channel_id=1, source_target_pairs={{0,2},{1,3},{2,0},{3,1},{4,6},{5,7},{6,4},{7,5},{8,10},{9,11},{10,... | collective-permute-start | bytes 786440 | tf_op jit(solution)/shard_map/ppermute | solution.py:231
  167.4 18.6 %collective-permute-start.2 = (bf16[2,256,128]{2,1,0:T(8,128)(2,1)S(1)}, bf16[2,256,128]{2,1,0:T(8,128)(2,1)S(1)}, u32[]{:S(2)}, u32[]{:S(2)}) collective-permute-start(bf16[2,256,128]{2,1,0:T(8,128)(2,1)S(1)} %slice.27), channel_id=1, source_target_pairs={{0,4},{1,5},{2,6},{3,7},{4,0},{5,1},{6,2},{7,3},{8,12},{9,13},{10,... | collective-permute-start | bytes 393224 | tf_op jit(solution)/shard_map/ppermute | solution.py:231
  186.1 14.6 %collective-permute-start.3 = (bf16[1,256,128]{2,1,0:T(8,128)(2,1)S(1)}, bf16[1,256,128]{2,1,0:T(8,128)(2,1)S(1)}, u32[]{:S(2)}, u32[]{:S(2)}) collective-permute-start(bf16[1,256,128]{2,1,0:T(8,128)(2,1)S(1)} %slice.29), channel_id=1, source_target_pairs={{0,8},{1,9},{2,10},{3,11},{4,12},{5,13},{6,14},{7,15},{8,0},{9,1},... | collective-permute-start | bytes 196616 | tf_op jit(solution)/shard_map/ppermute | solution.py:231
  200.7 13.7 %collective-permute-start.4 = (bf16[1,256,128]{2,1,0:T(8,128)(2,1)S(1)}, bf16[1,256,128]{2,1,0:T(8,128)(2,1)S(1)}, u32[]{:S(2)}, u32[]{:S(2)}) collective-permute-start(bf16[1,256,128]{2,1,0:T(8,128)(2,1)S(1)} %add_convert_fusion.2), channel_id=1, source_target_pairs={{0,8},{1,9},{2,10},{3,11},{4,12},{5,13},{6,14},{7,15},{8,0},{9,1},... | collective-permute-start | bytes 196616 | tf_op jit(solution)/shard_map/ppermute | solution.py:231
  214.4 16.7 %collective-permute-start.5 = (bf16[2,256,128]{2,1,0:T(8,128)(2,1)S(1)}, bf16[2,256,128]{2,1,0:T(8,128)(2,1)S(1)}, u32[]{:S(2)}, u32[]{:S(2)}) collective-permute-start(bf16[2,256,128]{2,1,0:T(8,128)(2,1)S(1)} %pad_maximum_fusion.2), channel_id=1, source_target_pairs={{0,4},{1,5},{2,6},{3,7},{4,0},{5,1},{6,2},{7,3},{8,12},{9,13},{10,... | collective-permute-start | bytes 393224 | tf_op jit(solution)/shard_map/ppermute | solution.py:231
  231.1 13.7 %collective-permute-start.6 = (bf16[4,256,128]{2,1,0:T(8,128)(2,1)S(1)}, bf16[4,256,128]{2,1,0:T(8,128)(2,1)S(1)}, u32[]{:S(2)}, u32[]{:S(2)}) collective-permute-start(bf16[4,256,128]{2,1,0:T(8,128)(2,1)S(1)} %pad_maximum_fusion.1), channel_id=1, source_target_pairs={{0,2},{1,3},{2,0},{3,1},{4,6},{5,7},{6,4},{7,5},{8,10},{9,11},{10,... | collective-permute-start | bytes 786440 | tf_op jit(solution)/shard_map/ppermute | solution.py:231
  245.6 15.0 %collective-permute-start.7 = (bf16[8,256,128]{2,1,0:T(8,128)(2,1)}, bf16[8,256,128]{2,1,0:T(8,128)(2,1)}, u32[]{:S(2)}, u32[]{:S(2)}) collective-permute-start(bf16[8,256,128]{2,1,0:T(8,128)(2,1)} %pad_maximum_fusion.own_ref), channel_id=1, source_target_pairs={{0,1},{1,0},{2,3},{3,2},{4,5},{5,4},{6,7},{7,6},{8,9},{9,8},{10,11... | collective-permute-start | bytes 1572872 | tf_op jit(solution)/shard_map/ppermute | solution.py:231
  260.7 1.2 copy-start.5
  265.0 1.0 copy-start.6

commit v2 on v1

--- a/solution.py
+++ b/solution.py
@@ -57,48 +57,38 @@
         out_ref[first : first + group] = got.astype(bf16).reshape(group, cap, width)
 
 
-def count_entries(counts_ref, bags_ref, bags_t_ref, by_item_ref, by_slot_ref):
-    items, bag = bags_ref.shape
-    slots = by_slot_ref.shape[0]
-    cap = slots // counts_ref.shape[1]
-    lane = narrow_iota((items, cap), 1)
-    sub = narrow_iota((cap, items), 0)
-    lane_at = lax.broadcasted_iota(i32, (1, cap), 1)
+def count_entries(counts_ref, bags_ref, by_item_ref, by_slot_ref):
+    bag, items = bags_ref.shape
+    owners = counts_ref.shape[1]
+    cap = by_slot_ref.shape[0] // owners
     sub_at = lax.broadcasted_iota(i32, (cap, 1), 0)
-
-    def step(owner, carry):
-        live = counts_ref[0, owner]
-        base = owner * cap
-        at = pl.ds(pl.multiple_of(base, cap), cap)
-        total = jnp.zeros((items, cap), bf16)
-        for b in range(bag):
-            entry = (bags_ref[:, b : b + 1] - base).astype(i16)
-            total = total + ones_where(lane == entry)
-        by_item_ref[:, at] = total * jnp.where(lane_at < live, 1.0, 0.0).astype(bf16)
-        total = jnp.zeros((cap, items), bf16)
-        for b in range(bag):
-            entry = (bags_t_ref[b : b + 1, :] - base).astype(i16)
-            total = total + ones_where(sub == entry)
-        by_slot_ref[at, :] = total * jnp.where(sub_at < live, 1.0, 0.0).astype(bf16)
-        return carry
-
-    lax.fori_loop(0, counts_ref.shape[1], step, 0)
-
-
-def pool_negatives(counts_ref, fetched_ref, out_ref):
-    bag = 16
-    trip = counts_ref.shape[0] - out_ref.shape[1]
-    pooled = jnp.dot(counts_ref[trip:, :], fetched_ref[...], preferred_element_type=f32)
-    entity = (pooled * (1.0 / bag)).astype(bf16)
-    out_ref[...] = jnp.broadcast_to(entity[None], out_ref.shape)
-
-
-def pool_triples(counts_ref, fetched_ref, scaling_ref, query_ref, tails_ref, positive_ref):
+    for first in range(0, items, cap):
+        wide = min(cap, items - first)
+        span = slice(first, first + wide)
+        entries = [bags_ref[b : b + 1, span].astype(i16) for b in range(bag)]
+        sub = narrow_iota((cap, wide), 0)
+
+        def step(owner, carry):
+            at = pl.ds(pl.multiple_of(owner * cap, cap), cap)
+            here = sub + (owner * cap).astype(i16)
+            total = ones_where(here == entries[0])
+            for b in range(1, bag):
+                total = total + ones_where(here == entries[b])
+            total = total * jnp.where(sub_at < counts_ref[0, owner], 1.0, 0.0).astype(bf16)
+            by_slot_ref[at, span] = total
+            by_item_ref[span, at] = total.T
+            return carry
+
+        lax.fori_loop(0, owners, step, 0)
+
+
+def pool(counts_ref, fetched_ref, scaling_ref, query_ref, tails_ref, positive_ref, negs_ref):
     bag = 16
     trip = query_ref.shape[0]
-    pooled = jnp.dot(counts_ref[: 2 * trip, :], fetched_ref[...], preferred_element_type=f32)
+    pooled = jnp.dot(counts_ref[...], fetched_ref[...], preferred_element_type=f32)
     entity = (pooled * (1.0 / bag)).astype(bf16)
-    tails = entity[trip:]
+    negs_ref[...] = jnp.broadcast_to(entity[None, 2 * trip :], negs_ref.shape)
+    tails = entity[trip : 2 * trip]
     query = (entity[:trip].astype(f32) * scaling_ref[...]).astype(bf16)
     query_ref[...] = query
     tails_ref[...] = tails
@@ -153,11 +143,7 @@
                 ]
 
 
-def flip(p):
-    return ((p & 1) << 2) | (p & 2) | (p >> 2)
-
-
-def collect(place_ref, own_ref, other_ref, grads_ref, out_ref, acc_ref):
+def collect(place_ref, own_ref, other_ref, grads_ref, kept_ref, up_ref, down_ref, acc_ref):
     blocks, cap, half = grads_ref.shape
     rows = acc_ref.shape[0]
     chunk = rows // 8
@@ -180,29 +166,42 @@
             preferred_element_type=f32,
         )
         acc_ref[...] = part if first == 0 else acc_ref[...] + part
-    for p in range(8):
-        c = flip(p) ^ (place >> 1)
-        out_ref[p] = acc_ref[pl.ds(pl.multiple_of(c * chunk, chunk), chunk), :].astype(bf16)
-
-
-def update(place_ref, table_ref, state_ref, own_ref, other_ref, table_out_ref, state_out_ref):
-    chunk, half = own_ref.shape[1:]
-    place = place_ref[0]
-    even = (place & 1) == 0
+    parity = (place >> 1) & 1
+
+    def take(c):
+        return acc_ref[pl.ds(pl.multiple_of(c * chunk, chunk), chunk), :].astype(bf16)
+
+    for j in range(4):
+        kept_ref[j] = take(2 * j + parity)
+    for j in range(2):
+        up_ref[j] = take(2 * j + 1 - parity)
+        down_ref[j] = take(2 * j + 5 - parity)
+
+
+def update(table_ref, state_ref, sums_ref, table_out_ref, state_out_ref):
+    chunk, half = sums_ref.shape[2:]
+    step = state_ref.shape[1]
+    eye = lax.broadcasted_iota(i32, (step, step), 0) == lax.broadcasted_iota(i32, (step, step), 1)
     for c in range(8):
-        turned = c ^ (place >> 1)
-        p = flip(turned)
-        own, other = own_ref[p].astype(f32), other_ref[p].astype(f32)
-        gradient = jnp.concatenate(
-            [jnp.where(even, own, other), jnp.where(even, other, own)], axis=1
-        )
-        at = slice(c * chunk, (c + 1) * chunk)
-        square = jnp.sum(gradient * gradient, axis=1, keepdims=True) * (1.0 / (2 * half))
-        fresh = state_ref[at, :] + square
-        state_out_ref[at, :] = fresh
-        table_out_ref[at, :] = (
-            table_ref[at, :].astype(f32) - learn_rate * gradient / jnp.sqrt(fresh)
-        ).astype(bf16)
+        at = 2 * (c % 2)
+        whole = jnp.concatenate(
+            [sums_ref[at, c // 2], sums_ref[at + 1, c // 2]], axis=1
+        ).astype(f32)
+        for q in range(chunk // step):
+            gradient = whole[q * step : (q + 1) * step]
+            line = c * (chunk // step) + q
+            at = slice(line * step, (line + 1) * step)
+            square = jnp.sum(gradient * gradient, axis=1, keepdims=True) * (1.0 / (2 * half))
+            before = jnp.sum(
+                jnp.where(eye, state_ref[line : line + 1, :], 0.0), axis=1, keepdims=True
+            )
+            fresh = before + square
+            state_out_ref[line : line + 1, :] = jnp.sum(
+                jnp.where(eye, fresh, 0.0), axis=0, keepdims=True
+            )
+            table_out_ref[at, :] = (
+                table_ref[at, :].astype(f32) - learn_rate * gradient / jnp.sqrt(fresh)
+            ).astype(bf16)
 
 
 def on_device(
@@ -227,11 +226,14 @@
     half = width // 2
     place = lax.axis_index("dp").astype(i32).reshape(1)
 
-    def swap(value, bit):
-        return lax.ppermute(value, "dp", [(i, i ^ bit) for i in range(n_dp)])
+    def swap(value):
+        return lax.ppermute(value, "dp", [(i, i ^ 1) for i in range(n_dp)])
+
+    def shift(value, by):
+        return lax.ppermute(value, "dp", [(i, (i + by) % n_dp) for i in range(n_dp)])
 
     asked = lax.all_to_all(slot_rows[0], "feat", split_axis=0, concat_axis=0, tiled=True)
-    asked_other = swap(asked, 1)
+    asked_other = swap(asked)
     served = call(
         gather_rows,
         shape((n_feat, cap, width), bf16),
@@ -242,30 +244,32 @@
     fetched = lax.all_to_all(served, "feat", split_axis=0, concat_axis=0, tiled=True)
     fetched = fetched.reshape(slots, width)
 
-    bags = jnp.concatenate([head_bags, tail_bags, negative_bags], axis=0)
+    bags = jnp.concatenate([head_bags.T, tail_bags.T, negative_bags.T], axis=1)
     by_item, by_slot = call(
         count_entries,
         (shape((items, slots), bf16), shape((slots, items), bf16)),
-        [SM, VM, VM],
+        [SM, VM],
         flops=8 * items * slots * 32,
         moved=4 * items * slots,
-    )(slot_counts, bags, bags.T)
+    )(slot_counts, bags)
     rel_pick = (
         relation_ids[:, None] == lax.broadcasted_iota(i32, (trip, rel_diag.shape[0]), 1)
     ).astype(bf16)
     scaling = jnp.dot(rel_pick, rel_diag, preferred_element_type=f32)
 
-    own_negs = call(
-        pool_negatives, shape((n_feat, n_neg, width), bf16), [VM, VM], flops=2 * n_neg * slots * width
-    )(by_item, fetched)
+    query, tails, positive, own_negs = call(
+        pool,
+        (
+            shape((trip, width), bf16),
+            shape((trip, width), bf16),
+            shape((trip, 1), f32),
+            shape((n_feat, n_neg, width), bf16),
+        ),
+        [VM, VM, VM],
+        flops=2 * items * slots * width,
+        moved=2 * slots * (width + items),
+    )(by_item, fetched, scaling)
     negs = lax.all_to_all(own_negs, "feat", split_axis=0, concat_axis=0, tiled=True)
-    query, tails, positive = call(
-        pool_triples,
-        (shape((trip, width), bf16), shape((trip, width), bf16), shape((trip, 1), f32)),
-        [VM, VM, VM],
-        flops=4 * trip * slots * width,
-        moved=2 * slots * width,
-    )(by_item, fetched, scaling)
     loss, gneg, grads = call(
         score,
         (
@@ -294,25 +298,44 @@
         tiled=True,
         axis_index_groups=pairs,
     )
-    part = call(
+    chunk = rows // 8
+    kept, up, down = call(
         collect,
-        shape((8, rows // 8, half), bf16),
+        (
+            shape((4, chunk, half), bf16),
+            shape((2, chunk, half), bf16),
+            shape((2, chunk, half), bf16),
+        ),
         [SM, VM, VM, VM],
         scratch=[pltpu.VMEM((rows, half), f32)],
         flops=4 * slots * rows * half,
     )(place, asked, asked_other, arrived)
-    kept = part
-    for bit in (2, 4, 8):
-        n = kept.shape[0] // 2
-        kept = (kept[:n].astype(f32) + swap(kept[n:], bit).astype(f32)).astype(bf16)
-    for bit in (8, 4, 2):
-        kept = jnp.concatenate([kept, swap(kept, bit)], axis=0)
-    across = swap(kept, 1)
+    nearby = jnp.concatenate([shift(up, 2), shift(down, -2)], axis=0)
+    kept = (kept.astype(f32) + nearby.astype(f32)).astype(bf16)
+    apart = [[h + 4 * j for j in range(4)] for h in range(4)]
+    quarter = lax.all_to_all(
+        kept,
+        "dp",
+        split_axis=0,
+        concat_axis=0,
+        tiled=True,
+        axis_index_groups=apart,
+    )
+    summed = jnp.sum(quarter.astype(f32), axis=0).astype(bf16)
+    quad = lax.all_gather(summed, "dp", axis=0, axis_index_groups=apart)
+    whole = lax.all_to_all(
+        jnp.broadcast_to(quad[None], (4,) + quad.shape),
+        "dp",
+        split_axis=0,
+        concat_axis=0,
+        tiled=True,
+        axis_index_groups=[[4 * j + h for h in range(4)] for j in range(4)],
+    )
     new_table, new_state = call(
         update,
-        (shape((rows, width), bf16), shape((rows, 1), f32)),
-        [SM, VM, VM, VM, VM],
-    )(place, feature_table, row_state.reshape(rows, 1), kept, across)
+        (shape((rows, width), bf16), shape((rows // 128, 128), f32)),
+        [VM] * 3,
+    )(feature_table, row_state.reshape(rows // 128, 128), whole)
     return (loss.reshape(trip), new_table, new_state.reshape(rows))
 
 

time: 269 us -> 234 us (0.87)
  the two profiles are of different devices: /device:TPU:1 before, /device:TPU:4 now
where the time goes in v2:
time: 234 us; the launch traced here: 233 us
  blocking collectives  88.2 us (38%)
  waiting for transfers between devices  50.5 us (22%)
  Pallas kernels  48.7 us (21%)
  starting transfers between devices  34.6 us (15%)
  local copies, waits for them, and re-layouts  8.52 us (4%)
    all_to_all x1, blocking collectives, on_device(): lax.all_to_all(kept, 'dp', split_axis=0, concat_axis=0, tiled=True, axis_...  29.6 us
    pallas_call x1, Pallas kernels, on_device(): call(count_entries, (shape((items, slots), bf16), shape((slots, items), b...  21.9 us
    ppermute x1, waiting for transfers between devices, swap(): return lax.ppermute(value, 'dp', [(i, i ^ 1) for i in range(n_dp)])  21.5 us
    all_to_all x1, waiting for transfers between devices, on_device(): lax.all_to_all(jnp.broadcast_to(quad[None], (4,) + quad.shape), 'dp', spl...  21.4 us
    all_gather x1, blocking collectives, on_device(): quad = lax.all_gather(summed, 'dp', axis=0, axis_index_groups=apart)  18.1 us
    all_to_all x1, blocking collectives, on_device(): lax.all_to_all(slot_rows[0], 'feat', split_axis=0, concat_axis=0, tiled=T...  14.8 us
    all_to_all x1, blocking collectives, on_device(): lax.all_to_all(own_negs, 'feat', split_axis=0, concat_axis=0, tiled=True)  13.2 us
    all_to_all x1, blocking collectives, on_device(): gneg = lax.all_to_all(gneg, 'feat', split_axis=0, concat_axis=0, tiled=True)  12.5 us
  transfers between devices with their start and end apart: 6, of which 6 were waited for; matrix products, arithmetic and copies ran while one was open for 1% of the time, Pallas kernels for 9%

profile of v2, /device:TPU:4, one launch (start us, length us, event | category | flops | bytes accessed | tf_op | source)
XLA Modules:
  0.0 232.8 jit_solution(10529632594622088996)
XLA Ops:
  0.6 14.8 %all_to_all.41 = s32[32,1,128]{2,1,0:T(1,128)S(1)} all-to-all(s32[32,1,128]{2,1,0:T(1,128)} %bitcast.19), channel_id=1, replica_groups=mesh['feat'=32,'dp'=16] {'feat'}, dimensions={0} | all-to-all | bytes 32768 | tf_op jit(solution)/shard_map/all_to_all | solution.py:235
  15.5 1.2 copy-done.4
  16.7 4.6 %shard_map.113 = bf16[32,128,256]{2,1,0:T(8,128)(2,1)S(1)} custom-call(s32[32,128]{1,0:T(8,128)S(1)} %bitcast.11, bf16[2048,256]{1,0:T(8,128)(2,1)S(1)} %copy-done.4), custom_call_target="tpu_custom_call" | custom-call | flops 4294967296 | bytes 3145728 | tf_op jit(solution)/shard_map/pallas_call | solution.py:237
  21.3 1.4 copy-done.3
  22.7 6.9 %all-to-all-start.1 = ((bf16[32,128,256]{2,1,0:T(8,128)(2,1)}), bf16[32,128,256]{2,1,0:T(8,128)(2,1)}, u32[]{:S(2)}, u32[]{:S(2)}) async-start(bf16[32,128,256]{2,1,0:T(8,128)(2,1)} %copy-done.3), calls=%async_computation.1 | async-start | bytes 4194304 | tf_op jit(solution)/shard_map/all_to_all | solution.py:244
  29.8 21.9 %shard_map.112 = (bf16[528,4096]{1,0:T(8,128)(2,1)S(1)}, bf16[4096,528]{1,0:T(8,128)(2,1)}) custom-call(s32[1,32]{1,0:T(1,128)S(1)} %copy-done.7, s32[16,528]{1,0:T(8,128)S(1)} %pad_add_fusion.bags_ref), custom_call_target="tpu_custom_call" | custom-call | flops 553648128 | bytes 8650752 | tf_op jit(solution)/shard_map/pallas_call | solution.py:248
  51.7 2.1 copy-done.2
  53.7 0.8 fusion.scaling_ref
  54.5 1.0 all-to-all-done.1
  55.5 4.3 %shard_map.114 = (bf16[256,256]{1,0:T(8,128)(2,1)S(1)}, bf16[256,256]{1,0:T(8,128)(2,1)S(1)}, f32[256,1]{1,0:T(8,128)S(1)}, bf16[32,16,256]{2,1,0:T(8,128)(2,1)S(1)}) custom-call(bf16[528,4096]{1,0:T(8,128)(2,1)} %copy-done.2, bf16[4096,256]{1,0:T(8,128)(2,1)} %bitcast.5.fetched_ref, f32[256,256]{1,0:T(8,128)S(1)} %fusion.scaling_ref), custom_call_target="tpu_custom_call" | custom-call | flops 1107296256 | bytes 6422528 | tf_op jit(solution)/shard_map/pallas_call | solution.py:260
  59.8 13.2 %all_to_all.42.negs_ref = bf16[32,16,256]{2,1,0:T(8,128)(2,1)S(1)} all-to-all(bf16[32,16,256]{2,1,0:T(8,128)(2,1)S(1)} %get-tuple-element.21), channel_id=1, replica_groups=mesh['feat'=32,'dp'=16] {'feat'}, dimensions={0} | all-to-all | bytes 524288 | tf_op jit(solution)/shard_map/all_to_all | solution.py:272
  73.0 0.9 shard_map.115
  73.9 12.5 %all_to_all.43.gneg_ref = bf16[32,16,256]{2,1,0:T(8,128)(2,1)S(1)} all-to-all(bf16[32,16,256]{2,1,0:T(8,128)(2,1)S(1)} %get-tuple-element.25), channel_id=1, replica_groups=mesh['feat'=32,'dp'=16] {'feat'}, dimensions={0} | all-to-all | bytes 524288 | tf_op jit(solution)/shard_map/all_to_all | solution.py:283
  86.3 4.3 %shard_map.116 = bf16[64,128,128]{2,1,0:T(8,128)(2,1)S(1)} custom-call(bf16[4096,528]{1,0:T(8,128)(2,1)} %get-tuple-element.23.counts_ref, bf16[512,256]{1,0:T(8,128)(2,1)S(1)} %get-tuple-element.24.grads_ref, bf16[32,16,256]{2,1,0:T(8,128)(2,1)S(1)} %all_to_all.43.gneg_ref), custom_call_target="tpu_custom_call" | custom-call | flops 1107296256 | tf_op jit(solution)/shard_map/pallas_call | solution.py:284
  90.6 1.3 copy-done.1
  91.9 7.3 %all-to-all-start.4 = ((bf16[64,128,128]{2,1,0:T(8,128)(2,1)}), bf16[64,128,128]{2,1,0:T(8,128)(2,1)}, u32[]{:S(2)}, u32[]{:S(2)}) async-start(bf16[64,128,128]{2,1,0:T(8,128)(2,1)} %copy-done.1), calls=%async_computation.4 | async-start | bytes 4194304 | tf_op jit(solution)/shard_map/all_to_all | solution.py:293
  99.3 3.6 %collective-permute-start = (s32[32,128]{1,0:T(8,128)S(1)}, s32[32,128]{1,0:T(8,128)S(1)}, u32[]{:S(2)}, u32[]{:S(2)}) collective-permute-start(s32[32,128]{1,0:T(8,128)S(1)} %bitcast.12), channel_id=1, source_target_pairs={{0,1},{1,0},{2,3},{3,2},{4,5},{5,4},{6,7},{7,6},{8,9},{9,8},{10,11... | collective-permute-start | bytes 49160 | tf_op jit(solution)/shard_map/ppermute | solution.py:230
  102.8 21.5 %collective-permute-done.other_ref = s32[32,128]{1,0:T(8,128)S(1)} collective-permute-done((s32[32,128]{1,0:T(8,128)S(1)}, s32[32,128]{1,0:T(8,128)S(1)}, u32[]{:S(2)}, u32[]{:S(2)}) %collective-permute-start) | collective-permute-done | bytes 16416 | tf_op jit(solution)/shard_map/ppermute | solution.py:230
  124.3 1.4 all-to-all-done.4.grads_ref
  125.7 10.8 %shard_map.117 = (bf16[4,256,128]{2,1,0:T(8,128)(2,1)S(1)}, bf16[2,256,128]{2,1,0:T(8,128)(2,1)S(1)}, bf16[2,256,128]{2,1,0:T(8,128)(2,1)S(1)}) custom-call(s32[1]{0:T(128)} %bitcast.7.place_ref, s32[32,128]{1,0:T(8,128)S(1)} %bitcast.13, s32[32,128]{1,0:T(8,128)S(1)} %collective-permute-done.other_ref, bf16[64,128,128]{2,1,0:T(8,128)(2,1)} %all-to-all-done.4.grads_ref), custom_call_target="tpu_custom_call" | custom-call | flops 4294967296 | tf_op jit(solution)/shard_map/pallas_call | solution.py:302
  136.5 3.7 %collective-permute-start.1 = (bf16[2,256,128]{2,1,0:T(8,128)(2,1)S(1)}, bf16[2,256,128]{2,1,0:T(8,128)(2,1)S(1)}, u32[]{:S(2)}, u32[]{:S(2)}) collective-permute-start(bf16[2,256,128]{2,1,0:T(8,128)(2,1)S(1)} %get-tuple-element.27), channel_id=1, source_target_pairs={{0,2},{1,3},{2,4},{3,5},{4,6},{5,7},{6,8},{7,9},{8,10},{9,11},{10,... | collective-permute-start | bytes 393224 | tf_op jit(solution)/shard_map/ppermute | solution.py:233
  140.2 8.2 %collective-permute-start.2 = (bf16[2,256,128]{2,1,0:T(8,128)(2,1)S(1)}, bf16[2,256,128]{2,1,0:T(8,128)(2,1)S(1)}, u32[]{:S(2)}, u32[]{:S(2)}) collective-permute-start(bf16[2,256,128]{2,1,0:T(8,128)(2,1)S(1)} %get-tuple-element.28), channel_id=1, source_target_pairs={{0,14},{1,15},{2,0},{3,1},{4,2},{5,3},{6,4},{7,5},{8,6},{9,7},{10,... | collective-permute-start | bytes 393224 | tf_op jit(solution)/shard_map/ppermute | solution.py:233
  148.4 3.0 %collective-permute-done.1 = bf16[2,256,128]{2,1,0:T(8,128)(2,1)S(1)} collective-permute-done((bf16[2,256,128]{2,1,0:T(8,128)(2,1)S(1)}, bf16[2,256,128]{2,1,0:T(8,128)(2,1)S(1)}, u32[]{:S(2)}, u32[]{:S(2)}) %collective-permute-start.1) | collective-permute-done | bytes 131104 | tf_op jit(solution)/shard_map/ppermute | solution.py:233
  151.4 2.2 collective-permute-done.2
  153.7 29.6 %all_to_all.44 = bf16[4,256,128]{2,1,0:T(8,128)(2,1)S(1)} all-to-all(bf16[4,256,128]{2,1,0:T(8,128)(2,1)S(1)} %add_convert_fusion), channel_id=1, replica_groups={{0,4,8,12},{1,5,9,13},{2,6,10,14},{3,7,11,15},{16,20,24,28},{17,21,25,2..., dimensions={0} | all-to-all | bytes 524288 | tf_op jit(solution)/shard_map/all_to_all | solution.py:316
  183.3 18.1 %all-gather = bf16[1024,128]{1,0:T(8,128)(2,1)S(1)} all-gather(bf16[256,128]{1,0:T(8,128)(2,1)S(1)} %reduce_sum.12), channel_id=2, replica_groups={{0,4,8,12},{1,5,9,13},{2,6,10,14},{3,7,11,15},{16,20,24,28},{17,21,25,2..., dimensions={0}, use_global_device_ids=true | all-gather | bytes 327680 | tf_op jit(solution)/shard_map/all_gather | solution.py:325
  201.5 1.2 broadcast_in_dim.2
  202.6 4.9 %all-to-all-start.6 = ((bf16[4,4,256,128]{3,2,1,0:T(8,128)(2,1)}), bf16[4,4,256,128]{3,2,1,0:T(8,128)(2,1)S(1)}, u32[]{:S(2)}, u32[]{:S(2)}) async-start(bf16[4,4,256,128]{3,2,1,0:T(8,128)(2,1)} %broadcast_in_dim.2), calls=%async_computation.6 | async-start | bytes 2097152 | tf_op jit(solution)/shard_map/all_to_all | solution.py:326
  207.6 0.7 reduce.1
  208.2 21.4 %all-to-all-done.6.sums_ref = bf16[4,4,256,128]{3,2,1,0:T(8,128)(2,1)S(1)} async-done(((bf16[4,4,256,128]{3,2,1,0:T(8,128)(2,1)}), bf16[4,4,256,128]{3,2,1,0:T(8,128)(2,1)S(1)}, u32[]{:S(2)}, u32[]{:S(2)}) %all-to-all-start.6) | async-done | bytes 1048608 | tf_op jit(solution)/shard_map/all_to_all | solution.py:326
  229.6 1.2 copy-done.5
  230.8 2.0 shard_map.118
  (23 shorter events, 0.2 us)
Async XLA Ops:
  0.6 53.1 %copy-start = (bf16[4096,256]{1,0:T(8,128)(2,1)S(1)}, bf16[4096,256]{1,0:T(8,128)(2,1)}, u32[]{:S(2)}) copy-start(bf16[4096,256]{1,0:T(8,128)(2,1)} %param.11) | copy-start | bytes 6291460
  15.5 1.2 copy-start.4
  21.3 1.4 copy-start.3
  22.7 6.9 %copy-start.10 = (s32[16,16]{1,0:T(8,128)S(1)}, s32[16,16]{1,0:T(8,128)}, u32[]{:S(2)}) copy-start(s32[16,16]{1,0:T(8,128)} %param.16) | copy-start | bytes 3076
  22.7 7.0 %copy-start.8 = (s32[256,16]{0,1:T(8,128)S(1)}, s32[256,16]{0,1:T(8,128)}, u32[]{:S(2)}) copy-start(s32[256,16]{0,1:T(8,128)} %param.15) | copy-start | bytes 49156
  22.7 7.0 %copy-start.9 = (s32[256,16]{0,1:T(8,128)S(1)}, s32[256,16]{0,1:T(8,128)}, u32[]{:S(2)}) copy-start(s32[256,16]{0,1:T(8,128)} %param.14) | copy-start | bytes 49156
  22.7 7.0 %copy-start.7 = (s32[1,32]{1,0:T(1,128)S(1)}, s32[1,32]{1,0:T(1,128)}, u32[]{:S(2)}) copy-start(s32[1,32]{1,0:T(1,128)} %counts_ref.1) | copy-start | bytes 388
  22.7 32.8 %all-to-all-start.1 = ((bf16[32,128,256]{2,1,0:T(8,128)(2,1)}), bf16[32,128,256]{2,1,0:T(8,128)(2,1)}, u32[]{:S(2)}, u32[]{:S(2)}) async-start(bf16[32,128,256]{2,1,0:T(8,128)(2,1)} %copy-done.3), calls=%async_computation.1 | async-start | bytes 4194304 | tf_op jit(solution)/shard_map/all_to_all | solution.py:244
  29.7 24.1 %copy-start.11 = (s32[256]{0:T(256)S(1)}, s32[256]{0:T(256)}, u32[]{:S(2)}) copy-start(s32[256]{0:T(256)} %param.17) | copy-start | bytes 3076
  51.7 2.1 copy-start.2
  90.6 1.3 copy-start.1
  91.9 33.8 %all-to-all-start.4 = ((bf16[64,128,128]{2,1,0:T(8,128)(2,1)}), bf16[64,128,128]{2,1,0:T(8,128)(2,1)}, u32[]{:S(2)}, u32[]{:S(2)}) async-start(bf16[64,128,128]{2,1,0:T(8,128)(2,1)} %copy-done.1), calls=%async_computation.4 | async-start | bytes 4194304 | tf_op jit(solution)/shard_map/all_to_all | solution.py:293
  99.3 25.1 %collective-permute-start = (s32[32,128]{1,0:T(8,128)S(1)}, s32[32,128]{1,0:T(8,128)S(1)}, u32[]{:S(2)}, u32[]{:S(2)}) collective-permute-start(s32[32,128]{1,0:T(8,128)S(1)} %bitcast.12), channel_id=1, source_target_pairs={{0,1},{1,0},{2,3},{3,2},{4,5},{5,4},{6,7},{7,6},{8,9},{9,8},{10,11... | collective-permute-start | bytes 49160 | tf_op jit(solution)/shard_map/ppermute | solution.py:230
  136.5 14.9 %collective-permute-start.1 = (bf16[2,256,128]{2,1,0:T(8,128)(2,1)S(1)}, bf16[2,256,128]{2,1,0:T(8,128)(2,1)S(1)}, u32[]{:S(2)}, u32[]{:S(2)}) collective-permute-start(bf16[2,256,128]{2,1,0:T(8,128)(2,1)S(1)} %get-tuple-element.27), channel_id=1, source_target_pairs={{0,2},{1,3},{2,4},{3,5},{4,6},{5,7},{6,8},{7,9},{8,10},{9,11},{10,... | collective-permute-start | bytes 393224 | tf_op jit(solution)/shard_map/ppermute | solution.py:233
  140.2 13.4 %collective-permute-start.2 = (bf16[2,256,128]{2,1,0:T(8,128)(2,1)S(1)}, bf16[2,256,128]{2,1,0:T(8,128)(2,1)S(1)}, u32[]{:S(2)}, u32[]{:S(2)}) collective-permute-start(bf16[2,256,128]{2,1,0:T(8,128)(2,1)S(1)} %get-tuple-element.28), channel_id=1, source_target_pairs={{0,14},{1,15},{2,0},{3,1},{4,2},{5,3},{6,4},{7,5},{8,6},{9,7},{10,... | collective-permute-start | bytes 393224 | tf_op jit(solution)/shard_map/ppermute | solution.py:233
  183.3 46.3 %copy-start.6 = (f32[2048]{0:T(1024)S(1)}, f32[2048]{0:T(1024)}, u32[]{:S(2)}) copy-start(f32[2048]{0:T(1024)} %param.10) | copy-start | bytes 24580
  202.6 27.0 %all-to-all-start.6 = ((bf16[4,4,256,128]{3,2,1,0:T(8,128)(2,1)}), bf16[4,4,256,128]{3,2,1,0:T(8,128)(2,1)S(1)}, u32[]{:S(2)}, u32[]{:S(2)}) async-start(bf16[4,4,256,128]{3,2,1,0:T(8,128)(2,1)} %broadcast_in_dim.2), calls=%async_computation.6 | async-start | bytes 2097152 | tf_op jit(solution)/shard_map/all_to_all | solution.py:326
  229.6 1.2 copy-start.5

commit v3 on v2

v3 whole, which is shorter than its diff:
```python
import jax
import jax.numpy as jnp
from jax import lax
from jax.experimental import pallas as pl
from jax.experimental.pallas import tpu as pltpu
from jax.sharding import PartitionSpec as P

score_scale = 4.0
learn_rate = 0.1
f32 = jnp.float32
bf16 = jnp.bfloat16
i32 = jnp.int32
i16 = jnp.int16

VM = pl.BlockSpec(memory_space=pltpu.VMEM)
SM = pl.BlockSpec(memory_space=pltpu.SMEM)
MIB = 1 << 20
LIMIT = 60


def call(
    body, out_shape, in_specs, out_specs=None, grid=(), scratch=(), flops=0, moved=0
):
    if out_specs is None:
        out_specs = jax.tree.map(lambda _: VM, out_shape)
    return pl.pallas_call(
        body,
        out_shape=out_shape,
        grid=grid,
        in_specs=in_specs,
        out_specs=out_specs,
        scratch_shapes=list(scratch),
        compiler_params=pltpu.CompilerParams(vmem_limit_bytes=LIMIT * MIB),
        cost_estimate=pl.CostEstimate(flops=flops, bytes_accessed=moved, transcendentals=0),
    )


def cut(dims, axis):
    return pl.BlockSpec(dims, lambda step: tuple(step if d == axis else 0 for d in range(len(dims))))


def whole(dims):
    return pl.BlockSpec(dims, lambda step: (0,) * len(dims))


def shape(dims, dtype):
    return jax.ShapeDtypeStruct(dims, dtype)


def ones_where(mask):
    return jnp.where(mask, jnp.ones((), bf16), jnp.zeros((), bf16))


def narrow_iota(dims, axis):
    return lax.broadcasted_iota(i32, dims, axis).astype(i16)


def gather_rows(asked_ref, table_ref, out_ref):
    sources, cap, width = out_ref.shape
    columns = asked_ref[...].T
    lanes = narrow_iota((cap, table_ref.shape[0]), 1)
    picks = [ones_where(lanes == columns[:, s : s + 1].astype(i16)) for s in range(sources)]
    got = jnp.dot(jnp.concatenate(picks, axis=0), table_ref[...], preferred_element_type=f32)
    out_ref[...] = got.astype(bf16).reshape(sources, cap, width)


def count_entries(counts_ref, bags_ref, by_item_ref, by_slot_ref):
    bag, items = bags_ref.shape
    owners = counts_ref.shape[1]
    cap = by_slot_ref.shape[0] // owners
    sub_at = lax.broadcasted_iota(i32, (cap, 1), 0)
    for first in range(0, items, cap):
        wide = min(cap, items - first)
        span = slice(first, first + wide)
        entries = [bags_ref[b : b + 1, span].astype(i16) for b in range(bag)]
        sub = narrow_iota((cap, wide), 0)

        def step(owner, carry):
            at = pl.ds(pl.multiple_of(owner * cap, cap), cap)
            here = sub + (owner * cap).astype(i16)
            total = ones_where(here == entries[0])
            for b in range(1, bag):
                total = total + ones_where(here == entries[b])
            total = total * jnp.where(sub_at < counts_ref[0, owner], 1.0, 0.0).astype(bf16)
            by_slot_ref[at, span] = total
            by_item_ref[span, at] = total.T
            return carry

        lax.fori_loop(0, owners, step, 0)


def pool(
    counts_ref, fetched_ref, scaling_ref, query_ref, tails_ref, positive_ref, negs_ref, pooled_ref
):
    bag = 16
    trip = query_ref.shape[0]
    part = jnp.dot(counts_ref[...], fetched_ref[...], preferred_element_type=f32)

    @pl.when(pl.program_id(0) == 0)
    def _():
        pooled_ref[...] = part

    @pl.when(pl.program_id(0) > 0)
    def _():
        pooled_ref[...] += part

    @pl.when(pl.program_id(0) == pl.num_programs(0) - 1)
    def _():
        entity = (pooled_ref[...] * (1.0 / bag)).astype(bf16)
        negs_ref[...] = jnp.broadcast_to(entity[None, 2 * trip :], negs_ref.shape)
        tails = entity[trip : 2 * trip]
        query = (entity[:trip].astype(f32) * scaling_ref[...]).astype(bf16)
        query_ref[...] = query
        tails_ref[...] = tails
        positive_ref[...] = score_scale * jnp.sum(
            query.astype(f32) * tails.astype(f32), axis=1, keepdims=True
        )


def score(query_ref, tails_ref, positive_ref, scaling_ref, negs_ref, loss_ref, gneg_ref, grads_ref):
    bag = 16
    trip, width = query_ref.shape
    query = query_ref[...]
    query_f = query.astype(f32)
    tails_f = tails_ref[...].astype(f32)
    negs = negs_ref[...].reshape(-1, width)
    positive = positive_ref[...]
    scores = score_scale * lax.dot_general(
        query, negs, (((1,), (1,)), ((), ())), preferred_element_type=f32
    )
    highest = jnp.maximum(jnp.max(scores, axis=1, keepdims=True), positive)
    total = jnp.exp(positive - highest) + jnp.sum(
        jnp.exp(scores - highest), axis=1, keepdims=True
    )
    log_total = highest + jnp.log(total)
    loss_ref[...] = log_total - positive
    p_pos = jnp.exp(positive - log_total)
    p_neg_f = jnp.exp(scores - log_total)
    p_neg = p_neg_f.astype(bf16)
    gneg = score_scale * jnp.dot(p_neg_f.T.astype(bf16), query, preferred_element_type=f32)
    gneg_ref[...] = gneg.astype(bf16).reshape(gneg_ref.shape)
    grad_query = score_scale * (
        (p_pos - 1.0) * tails_f + jnp.dot(p_neg, negs, preferred_element_type=f32)
    )
    grads_ref[:trip] = (grad_query * scaling_ref[...] * (1.0 / bag)).astype(bf16)
    grads_ref[trip:] = (score_scale * (p_pos - 1.0) * query_f * (1.0 / bag)).astype(bf16)


def spread(counts_ref, grads_ref, gneg_ref, out_ref, all_ref):
    bag = 16
    trips = grads_ref.shape[0]

    @pl.when(pl.program_id(0) == 0)
    def _():
        gneg = jnp.sum(gneg_ref[...].astype(f32), axis=0) * (1.0 / bag)
        all_ref[:trips] = grads_ref[...]
        all_ref[trips:] = gneg.astype(bf16)

    slot = jnp.dot(counts_ref[...], all_ref[...], preferred_element_type=f32)
    out_ref[...] = slot.astype(bf16).reshape(out_ref.shape)


def collect(asked_ref, grads_ref, out_ref, acc_ref):
    sources, cap, width = grads_ref.shape
    sub = narrow_iota((acc_ref.shape[0], cap), 0)
    picks = [ones_where(sub == asked_ref[s : s + 1, :].astype(i16)) for s in range(sources)]
    part = jnp.dot(
        jnp.concatenate(picks, axis=1),
        grads_ref[...].reshape(sources * cap, width),
        preferred_element_type=f32,
    )
    step, last = pl.program_id(0), pl.num_programs(0) - 1

    @pl.when(step == 0)
    def _():
        acc_ref[...] = part

    @pl.when((step > 0) & (step < last))
    def _():
        acc_ref[...] += part

    @pl.when(step == last)
    def _():
        out_ref[...] = (acc_ref[...] + part).astype(bf16)


def update(table_ref, state_ref, sums_ref, table_out_ref, state_out_ref):
    lines, step = state_ref.shape
    width = table_ref.shape[1]
    eye = lax.broadcasted_iota(i32, (step, step), 0) == lax.broadcasted_iota(i32, (step, step), 1)
    for line in range(lines):
        at = slice(line * step, (line + 1) * step)
        gradient = sums_ref[at, :].astype(f32)
        square = jnp.sum(gradient * gradient, axis=1, keepdims=True) * (1.0 / width)
        before = jnp.sum(
            jnp.where(eye, state_ref[line : line + 1, :], 0.0), axis=1, keepdims=True
        )
        fresh = before + square
        state_out_ref[line : line + 1, :] = jnp.sum(
            jnp.where(eye, fresh, 0.0), axis=0, keepdims=True
        )
        table_out_ref[at, :] = (
            table_ref[at, :].astype(f32) - learn_rate * gradient / jnp.sqrt(fresh)
        ).astype(bf16)


def on_device(
    feature_table,
    row_state,
    rel_diag,
    slot_rows,
    slot_counts,
    head_bags,
    tail_bags,
    negative_bags,
    relation_ids,
):
    n_feat = lax.axis_size("feat")
    n_dp = lax.axis_size("dp")
    cap = slot_rows.shape[2]
    rows, width = feature_table.shape
    trip = head_bags.shape[0]
    n_neg = negative_bags.shape[0]
    items = 2 * trip + n_neg
    slots = n_feat * cap
    steps = 4
    part = n_feat // steps
    asked = lax.all_to_all(slot_rows[0], "feat", split_axis=0, concat_axis=0, tiled=True)
    served = call(
        gather_rows,
        shape((n_feat, cap, width), bf16),
        [cut((part, cap), 0), whole((rows, width))],
        cut((part, cap, width), 0),
        grid=(steps,),
        flops=2 * slots * rows * width,
        moved=rows * width * 2 + slots * width * 2,
    )(asked, feature_table)
    fetched = lax.all_to_all(served, "feat", split_axis=0, concat_axis=0, tiled=True)
    fetched = fetched.reshape(slots, width)

    bags = jnp.concatenate([head_bags.T, tail_bags.T, negative_bags.T], axis=1)
    by_item, by_slot = call(
        count_entries,
        (shape((items, slots), bf16), shape((slots, items), bf16)),
        [SM, VM],
        flops=8 * items * slots * 32,
        moved=4 * items * slots,
    )(slot_counts, bags)
    rel_pick = (
        relation_ids[:, None] == lax.broadcasted_iota(i32, (trip, rel_diag.shape[0]), 1)
    ).astype(bf16)
    scaling = jnp.dot(rel_pick, rel_diag, preferred_element_type=f32)

    query, tails, positive, own_negs = call(
        pool,
        (
            shape((trip, width), bf16),
            shape((trip, width), bf16),
            shape((trip, 1), f32),
            shape((n_feat, n_neg, width), bf16),
        ),
        [cut((items, slots // steps), 1), cut((slots // steps, width), 0), whole((trip, width))],
        (whole((trip, width)), whole((trip, width)), whole((trip, 1)), whole((n_feat, n_neg, width))),
        grid=(steps,),
        scratch=[pltpu.VMEM((items, width), f32)],
        flops=2 * items * slots * width,
        moved=2 * slots * (width + items),
    )(by_item, fetched, scaling)
    negs = lax.all_to_all(own_negs, "feat", split_axis=0, concat_axis=0, tiled=True)
    loss, gneg, grads = call(
        score,
        (
            shape((trip, 1), f32),
            shape((n_feat, n_neg, width), bf16),
            shape((2 * trip, width), bf16),
        ),
        [VM] * 5,
        flops=6 * trip * n_feat * n_neg * width,
    )(query, tails, positive, scaling, negs)
    gneg = lax.all_to_all(gneg, "feat", split_axis=0, concat_axis=0, tiled=True)
    slot_grad = call(
        spread,
        shape((n_feat, cap, width), bf16),
        [
            cut((slots // steps, items), 0),
            whole((2 * trip, width)),
            whole((n_feat, n_neg, width)),
        ],
        cut((part, cap, width), 0),
        grid=(steps,),
        scratch=[pltpu.VMEM((items, width), bf16)],
        flops=2 * items * slots * width,
        moved=2 * slots * (width + items),
    )(by_slot, grads, gneg)
    arrived = lax.all_to_all(slot_grad, "feat", split_axis=0, concat_axis=0, tiled=True)
    sums = call(
        collect,
        shape((rows, width), bf16),
        [cut((part, cap), 0), cut((part, cap, width), 0)],
        whole((rows, width)),
        grid=(steps,),
        scratch=[pltpu.VMEM((rows, width), f32)],
        flops=2 * slots * rows * width,
        moved=2 * (slots + rows) * width,
    )(asked, arrived)
    close = [[4 * j + h for h in range(4)] for j in range(n_dp // 4)]
    apart = [[h + 4 * j for j in range(n_dp // 4)] for h in range(4)]

    def exchange(value, groups):
        return lax.all_to_all(
            value, "dp", split_axis=0, concat_axis=0, tiled=True, axis_index_groups=groups
        )

    for groups in (close, apart):
        pieces = exchange(sums.reshape(4, -1, width), groups)
        sums = jnp.sum(pieces.astype(f32), axis=0).astype(bf16)
    quad = lax.all_gather(sums, "dp", axis=0, axis_index_groups=apart)
    sums = exchange(jnp.broadcast_to(quad[None], (4,) + quad.shape), close).reshape(rows, width)
    lines = rows // cap
    new_table, new_state = call(
        update,
        (shape((rows, width), bf16), shape((lines, cap), f32)),
        [cut((rows // 2, width), 0), cut((lines // 2, cap), 0), cut((rows // 2, width), 0)],
        (cut((rows // 2, width), 0), cut((lines // 2, cap), 0)),
        grid=(2,),
        flops=8 * rows * width,
        moved=6 * rows * width,
    )(feature_table, row_state.reshape(lines, cap), sums)
    return (loss.reshape(trip), new_table, new_state.reshape(rows))


def solution(mesh):
    in_specs = (
        P("feat", None),
        P("feat"),
        P(),
        P(("feat", "dp"), None, None),
        P(("feat", "dp"), None),
        P(("feat", "dp"), None),
        P(("feat", "dp"), None),
        P(("feat", "dp"), None),
        P(("feat", "dp")),
    )
    out_specs = (P(("feat", "dp")), P("feat", None), P("feat"))
    return jax.shard_map(
        on_device, mesh=mesh, in_specs=in_specs, out_specs=out_specs, check_vma=False
    )
```

time: 234 us -> 252 us (1.077)
  the two profiles are of different devices: /device:TPU:4 before, /device:TPU:10 now
where the time goes in v3:
time: 252 us; the launch traced here: 251 us
  blocking collectives  155 us (62%)
  Pallas kernels  56 us (22%)
  waiting for transfers between devices  21.2 us (8%)
  starting transfers between devices  12.2 us (5%)
    all_to_all x2, blocking collectives, exchange(): lax.all_to_all(value, 'dp', split_axis=0, concat_axis=0, tiled=True, axis...  61.1 us
    all_to_all x1, blocking collectives, on_device(): lax.all_to_all(slot_grad, 'feat', split_axis=0, concat_axis=0, tiled=True)  32.9 us
    pallas_call x1, Pallas kernels, on_device(): call(count_entries, (shape((items, slots), bf16), shape((slots, items), b...  23.5 us
    all_to_all x1, waiting for transfers between devices, exchange(): lax.all_to_all(value, 'dp', split_axis=0, concat_axis=0, tiled=True, axis...  21.1 us
    all_gather x1, blocking collectives, on_device(): quad = lax.all_gather(sums, 'dp', axis=0, axis_index_groups=apart)  18.3 us
    all_to_all x1, blocking collectives, on_device(): lax.all_to_all(slot_rows[0], 'feat', split_axis=0, concat_axis=0, tiled=T...  15.3 us
    all_to_all x1, blocking collectives, on_device(): lax.all_to_all(own_negs, 'feat', split_axis=0, concat_axis=0, tiled=True)  14.2 us
    all_to_all x1, blocking collectives, on_device(): gneg = lax.all_to_all(gneg, 'feat', split_axis=0, concat_axis=0, tiled=True)  13.5 us
  transfers between devices with their start and end apart: 2, of which 2 were waited for; matrix products, arithmetic and copies ran while one was open for 1% of the time, Pallas kernels for 9%

profile of v3, /device:TPU:10, one launch (start us, length us, event | category | flops | bytes accessed | tf_op | source)
XLA Modules:
  0.0 250.6 jit_solution(15601485676856454223)
XLA Ops:
  0.6 0.0 copy-start
  0.6 15.3 %all_to_all.46 = s32[32,1,128]{2,1,0:T(1,128)} all-to-all(s32[32,1,128]{2,1,0:T(1,128)} %bitcast.20), channel_id=1, replica_groups=mesh['feat'=32,'dp'=16] {'feat'}, dimensions={0} | all-to-all | bytes 32768 | tf_op jit(solution)/shard_map/all_to_all | solution.py:228
  15.9 7.5 %shard_map.113 = bf16[32,128,256]{2,1,0:T(8,128)(2,1)} custom-call(s32[32,128]{1,0:T(8,128)} %bitcast.21, bf16[2048,256]{1,0:T(8,128)(2,1)} %table_ref.3), custom_call_target="tpu_custom_call" | custom-call | flops 4294967296 | bytes 3145728 | tf_op jit(solution)/shard_map/pallas_call | solution.py:229
  23.5 6.8 %all-to-all-start.1 = ((bf16[32,128,256]{2,1,0:T(8,128)(2,1)}), bf16[32,128,256]{2,1,0:T(8,128)(2,1)}, u32[]{:S(2)}, u32[]{:S(2)}) async-start(bf16[32,128,256]{2,1,0:T(8,128)(2,1)} %shard_map.113), calls=%async_computation.1 | async-start | bytes 4194304 | tf_op jit(solution)/shard_map/all_to_all | solution.py:238
  30.3 0.0 copy-done.5
  30.4 0.0 copy-start.6
  30.4 0.1 copy.15
  30.4 0.0 copy-done.3
  30.4 0.0 copy-done.4
  30.4 0.6 pad_add_fusion.bags_ref
  31.1 23.5 %shard_map.112 = (bf16[528,4096]{1,0:T(8,128)(2,1)}, bf16[4096,528]{1,0:T(8,128)(2,1)}) custom-call(s32[1,32]{1,0:T(1,128)} %counts_ref.1, s32[16,528]{1,0:T(8,128)} %pad_add_fusion.bags_ref), custom_call_target="tpu_custom_call" | custom-call | flops 553648128 | bytes 8650752 | tf_op jit(solution)/shard_map/pallas_call | solution.py:242
  54.6 0.0 copy-done
  54.6 0.0 copy-done.6
  54.6 1.5 fusion.scaling_ref
  56.1 0.1 all-to-all-done.1
  56.2 5.5 %shard_map.114 = (bf16[256,256]{1,0:T(8,128)(2,1)}, bf16[256,256]{1,0:T(8,128)(2,1)}, f32[256,1]{1,0:T(8,128)}, bf16[32,16,256]{2,1,0:T(8,128)(2,1)}) custom-call(bf16[528,4096]{1,0:T(8,128)(2,1)} %get-tuple-element.14.counts_ref, bf16[4096,256]{1,0:T(8,128)(2,1)} %bitcast.5.fetched_ref, f32[256,256]{1,0:T(8,128)} %fusion.scaling_ref), custom_call_target="tpu_custom_call" | custom-call | flops 1107296256 | bytes 6422528 | tf_op jit(solution)/shard_map/pallas_call | solution.py:254
  61.6 14.2 %all_to_all.47.negs_ref = bf16[32,16,256]{2,1,0:T(8,128)(2,1)} all-to-all(bf16[32,16,256]{2,1,0:T(8,128)(2,1)} %get-tuple-element.18), channel_id=1, replica_groups=mesh['feat'=32,'dp'=16] {'feat'}, dimensions={0} | all-to-all | bytes 524288 | tf_op jit(solution)/shard_map/all_to_all | solution.py:269
  75.8 2.9 %shard_map.115 = (f32[256,1]{1,0:T(8,128)}, bf16[32,16,256]{2,1,0:T(8,128)(2,1)}, bf16[512,256]{1,0:T(8,128)(2,1)}) custom-call(bf16[256,256]{1,0:T(8,128)(2,1)} %get-tuple-element.15.query_ref, bf16[256,256]{1,0:T(8,128)(2,1)} %get-tuple-element.16.tails_ref, f32[256,1]{1,0:T(8,128)} %get-tuple-element.17.positive_ref, f32[256,256]{1,0:T(8,128)} %fusion.scaling_ref, ...), custom_call_target="tpu_custom_call" | custom-call | flops 201326592 | tf_op jit(solution)/shard_map/pallas_call | solution.py:270
  78.7 13.5 %all_to_all.48.gneg_ref = bf16[32,16,256]{2,1,0:T(8,128)(2,1)} all-to-all(bf16[32,16,256]{2,1,0:T(8,128)(2,1)} %get-tuple-element.22), channel_id=1, replica_groups=mesh['feat'=32,'dp'=16] {'feat'}, dimensions={0} | all-to-all | bytes 524288 | tf_op jit(solution)/shard_map/all_to_all | solution.py:280
  92.2 5.7 %shard_map.116 = bf16[32,128,256]{2,1,0:T(8,128)(2,1)} custom-call(bf16[4096,528]{1,0:T(8,128)(2,1)} %get-tuple-element.20.counts_ref, bf16[512,256]{1,0:T(8,128)(2,1)} %get-tuple-element.21.grads_ref, bf16[32,16,256]{2,1,0:T(8,128)(2,1)} %all_to_all.48.gneg_ref), custom_call_target="tpu_custom_call" | custom-call | flops 1107296256 | bytes 6422528 | tf_op jit(solution)/shard_map/pallas_call | solution.py:281
  97.9 32.9 %all_to_all.49.grads_ref = bf16[32,128,256]{2,1,0:T(8,128)(2,1)} all-to-all(bf16[32,128,256]{2,1,0:T(8,128)(2,1)} %shard_map.116), channel_id=1, replica_groups=mesh['feat'=32,'dp'=16] {'feat'}, dimensions={0} | all-to-all | bytes 4194304 | tf_op jit(solution)/shard_map/all_to_all | solution.py:295
  130.8 7.8 %shard_map.117 = bf16[2048,256]{1,0:T(8,128)(2,1)} custom-call(s32[32,128]{1,0:T(8,128)} %bitcast.22, bf16[32,128,256]{2,1,0:T(8,128)(2,1)} %all_to_all.49.grads_ref), custom_call_target="tpu_custom_call" | custom-call | flops 4294967296 | bytes 3145728 | tf_op jit(solution)/shard_map/pallas_call | solution.py:296
  138.6 30.1 %all_to_all.50 = bf16[4,512,256]{2,1,0:T(8,128)(2,1)S(1)} all-to-all(bf16[4,512,256]{2,1,0:T(8,128)(2,1)} %bitcast.16), channel_id=1, replica_groups={{0,1,2,3},{4,5,6,7},{8,9,10,11},{12,13,14,15},{16,17,18,19},{20,21,22,2..., dimensions={0} | all-to-all | bytes 2097152 | tf_op jit(solution)/shard_map/all_to_all | solution.py:310
  168.7 0.3 reduce_sum.24
  169.0 31.0 %all_to_all.51 = bf16[4,128,256]{2,1,0:T(8,128)(2,1)S(1)} all-to-all(bf16[4,128,256]{2,1,0:T(8,128)(2,1)S(1)} %bitcast.15), channel_id=1, replica_groups={{0,4,8,12},{1,5,9,13},{2,6,10,14},{3,7,11,15},{16,20,24,28},{17,21,25,2..., dimensions={0} | all-to-all | bytes 524288 | tf_op jit(solution)/shard_map/all_to_all | solution.py:310
  200.1 18.3 %all-gather = bf16[512,256]{1,0:T(8,128)(2,1)S(1)} all-gather(bf16[128,256]{1,0:T(8,128)(2,1)S(1)} %reduce_sum.25), channel_id=2, replica_groups={{0,4,8,12},{1,5,9,13},{2,6,10,14},{3,7,11,15},{16,20,24,28},{17,21,25,2..., dimensions={0}, use_global_device_ids=true | all-gather | bytes 327680 | tf_op jit(solution)/shard_map/all_gather | solution.py:317
  218.3 1.1 broadcast_in_dim.2
  219.4 5.4 %all-to-all-start.7 = ((bf16[4,4,128,256]{3,2,1,0:T(8,128)(2,1)}), bf16[4,4,128,256]{3,2,1,0:T(8,128)(2,1)S(1)}, u32[]{:S(2)}, u32[]{:S(2)}) async-start(bf16[4,4,128,256]{3,2,1,0:T(8,128)(2,1)} %broadcast_in_dim.2), calls=%async_computation.7 | async-start | bytes 2097152 | tf_op jit(solution)/shard_map/all_to_all | solution.py:310
  224.8 0.7 reduce.2
  225.5 21.1 %all-to-all-done.7 = bf16[4,4,128,256]{3,2,1,0:T(8,128)(2,1)S(1)} async-done(((bf16[4,4,128,256]{3,2,1,0:T(8,128)(2,1)}), bf16[4,4,128,256]{3,2,1,0:T(8,128)(2,1)S(1)}, u32[]{:S(2)}, u32[]{:S(2)}) %all-to-all-start.7) | async-done | bytes 1048608 | tf_op jit(solution)/shard_map/all_to_all | solution.py:310
  246.6 1.0 copy-done.1
  247.5 3.1 %shard_map.118 = (bf16[2048,256]{1,0:T(8,128)(2,1)}, f32[16,128]{1,0:T(8,128)}) custom-call(bf16[2048,256]{1,0:T(8,128)(2,1)} %table_ref.3, f32[16,128]{1,0:T(8,128)} %bitcast.23, bf16[2048,256]{1,0:T(8,128)(2,1)} %bitcast.13), custom_call_target="tpu_custom_call" | custom-call | flops 4194304 | bytes 3145728 | tf_op jit(solution)/shard_map/pallas_call | solution.py:320
  (7 shorter events, 0.1 us)
Async XLA Ops:
  0.6 54.0 %copy-start = (bf16[4096,256]{1,0:T(8,128)(2,1)S(1)}, bf16[4096,256]{1,0:T(8,128)(2,1)}, u32[]{:S(2)}) copy-start(bf16[4096,256]{1,0:T(8,128)(2,1)} %param.11) | copy-start | bytes 6291460
  23.5 6.9 %copy-start.5 = (s32[16,16]{1,0:T(8,128)S(1)}, s32[16,16]{1,0:T(8,128)}, u32[]{:S(2)}) copy-start(s32[16,16]{1,0:T(8,128)} %param.16) | copy-start | bytes 3076
  23.5 7.0 %copy-start.3 = (s32[256,16]{0,1:T(8,128)S(1)}, s32[256,16]{0,1:T(8,128)}, u32[]{:S(2)}) copy-start(s32[256,16]{0,1:T(8,128)} %param.15) | copy-start | bytes 49156
  23.5 7.0 %copy-start.4 = (s32[256,16]{0,1:T(8,128)S(1)}, s32[256,16]{0,1:T(8,128)}, u32[]{:S(2)}) copy-start(s32[256,16]{0,1:T(8,128)} %param.14) | copy-start | bytes 49156
  23.5 32.7 %all-to-all-start.1 = ((bf16[32,128,256]{2,1,0:T(8,128)(2,1)}), bf16[32,128,256]{2,1,0:T(8,128)(2,1)}, u32[]{:S(2)}, u32[]{:S(2)}) async-start(bf16[32,128,256]{2,1,0:T(8,128)(2,1)} %shard_map.113), calls=%async_computation.1 | async-start | bytes 4194304 | tf_op jit(solution)/shard_map/all_to_all | solution.py:238
  30.4 24.2 %copy-start.6 = (s32[256]{0:T(256)S(1)}, s32[256]{0:T(256)}, u32[]{:S(2)}) copy-start(s32[256]{0:T(256)} %param.17) | copy-start | bytes 3076
  200.0 24.8 %copy-start.2 = (f32[256,1]{1,0:T(8,128)S(1)}, f32[256,1]{1,0:T(8,128)}, u32[]{:S(2)}) copy-start(f32[256,1]{1,0:T(8,128)} %get-tuple-element.19) | copy-start | bytes 3076
  219.4 27.1 %all-to-all-start.7 = ((bf16[4,4,128,256]{3,2,1,0:T(8,128)(2,1)}), bf16[4,4,128,256]{3,2,1,0:T(8,128)(2,1)S(1)}, u32[]{:S(2)}, u32[]{:S(2)}) async-start(bf16[4,4,128,256]{3,2,1,0:T(8,128)(2,1)} %broadcast_in_dim.2), calls=%async_computation.7 | async-start | bytes 2097152 | tf_op jit(solution)/shard_map/all_to_all | solution.py:310
  246.6 1.0 copy-start.1

commit v4 on v2

--- a/solution.py
+++ b/solution.py
@@ -15,9 +15,10 @@
 VM = pl.BlockSpec(memory_space=pltpu.VMEM)
 SM = pl.BlockSpec(memory_space=pltpu.SMEM)
 MIB = 1 << 20
-
-
-def call(body, out_shape, in_specs, scratch=(), flops=0, moved=0, limit=48):
+LIMIT = 48
+
+
+def call(body, out_shape, in_specs, scratch=(), flops=0, moved=0, limit=LIMIT):
     outs = jax.tree.map(lambda _: VM, out_shape)
     return pl.pallas_call(
         body,
@@ -42,44 +43,81 @@
     return lax.broadcasted_iota(i32, dims, axis).astype(i16)
 
 
-def gather_rows(asked_ref, table_ref, out_ref):
+def gather_rows(place_ref, asked_ref, table_ref, out_ref):
     sources, cap, width = out_ref.shape
     rows = table_ref.shape[0]
+    even = (place_ref[0] & 1) == 0
     columns = asked_ref[...].T
     lanes = narrow_iota((cap, rows), 1)
     group = 8
     for first in range(0, sources, group):
-        picks = [
-            ones_where(lanes == columns[:, s : s + 1].astype(i16))
-            for s in range(first, first + group)
-        ]
+        picks = []
+        for s in range(first, first + group):
+            column = jnp.where(
+                even, columns[:, 2 * s : 2 * s + 1], columns[:, 2 * s + 1 : 2 * s + 2]
+            )
+            picks.append(ones_where(lanes == column.astype(i16)))
         got = jnp.dot(jnp.concatenate(picks, axis=0), table_ref[...], preferred_element_type=f32)
         out_ref[first : first + group] = got.astype(bf16).reshape(group, cap, width)
 
 
-def count_entries(counts_ref, bags_ref, by_item_ref, by_slot_ref):
-    bag, items = bags_ref.shape
+def count_entries(counts_ref, bags_ref, neg_ref, by_item_ref, by_slot_ref):
+    bag, trips = bags_ref.shape
+    negs = neg_ref.shape[0]
     owners = counts_ref.shape[1]
     cap = by_slot_ref.shape[0] // owners
     sub_at = lax.broadcasted_iota(i32, (cap, 1), 0)
-    for first in range(0, items, cap):
-        wide = min(cap, items - first)
-        span = slice(first, first + wide)
+    lane_at = lax.broadcasted_iota(i32, (1, cap), 1)
+    sub = narrow_iota((cap, cap), 0)
+    for first in range(0, trips, cap):
+        span = slice(first, first + cap)
         entries = [bags_ref[b : b + 1, span].astype(i16) for b in range(bag)]
-        sub = narrow_iota((cap, wide), 0)
-
-        def step(owner, carry):
-            at = pl.ds(pl.multiple_of(owner * cap, cap), cap)
-            here = sub + (owner * cap).astype(i16)
-            total = ones_where(here == entries[0])
-            for b in range(1, bag):
-                total = total + ones_where(here == entries[b])
-            total = total * jnp.where(sub_at < counts_ref[0, owner], 1.0, 0.0).astype(bf16)
-            by_slot_ref[at, span] = total
-            by_item_ref[span, at] = total.T
+
+        def step(pair, carry):
+            for owner in (2 * pair, 2 * pair + 1):
+                at = pl.ds(pl.multiple_of(owner * cap, cap), cap)
+                here = sub + (owner * cap).astype(i16)
+                total = ones_where(here == entries[0])
+                for b in range(1, bag):
+                    total = total + ones_where(here == entries[b])
+                total = total * jnp.where(sub_at < counts_ref[0, owner], 1.0, 0.0).astype(bf16)
+                by_slot_ref[at, span] = total
+                by_item_ref[span, at] = total.T
             return carry
 
-        lax.fori_loop(0, owners, step, 0)
+        lax.fori_loop(0, owners // 2, step, 0)
+
+    lane = narrow_iota((negs, cap), 1)
+    columns = [
+        jnp.broadcast_to(neg_ref[:, b : b + 1], (negs, cap)).astype(i16) for b in range(bag)
+    ]
+    span = slice(trips, trips + negs)
+
+    def last(owner, carry):
+        at = pl.ds(pl.multiple_of(owner * cap, cap), cap)
+        here = lane + (owner * cap).astype(i16)
+        total = ones_where(here == columns[0])
+        for b in range(1, bag):
+            total = total + ones_where(here == columns[b])
+        total = total * jnp.where(lane_at < counts_ref[0, owner], 1.0, 0.0).astype(bf16)
+        by_item_ref[span, at] = total
+        by_slot_ref[at, span] = total.T
+        return carry
+
+    lax.fori_loop(0, owners, last, 0)
+
+
+def pick_relations(ids_ref, rel_ref, out_ref):
+    step = ids_ref.shape[1]
+    relations = rel_ref.shape[0]
+    eye = lax.broadcasted_iota(i32, (step, step), 0) == lax.broadcasted_iota(i32, (step, step), 1)
+    lanes = narrow_iota((step, relations), 1)
+    for line in range(ids_ref.shape[0]):
+        column = jnp.sum(jnp.where(eye, ids_ref[line : line + 1, :], 0), axis=1, keepdims=True)
+        pick = ones_where(lanes == column.astype(i16))
+        out_ref[line * step : (line + 1) * step, :] = jnp.dot(
+            pick, rel_ref[...], preferred_element_type=f32
+        )
 
 
 def pool(counts_ref, fetched_ref, scaling_ref, query_ref, tails_ref, positive_ref, negs_ref):
@@ -113,7 +151,12 @@
         jnp.exp(scores - highest), axis=1, keepdims=True
     )
     log_total = highest + jnp.log(total)
-    loss_ref[...] = log_total - positive
+    loss = log_total - positive
+    step = loss_ref.shape[1]
+    eye = lax.broadcasted_iota(i32, (step, step), 0) == lax.broadcasted_iota(i32, (step, step), 1)
+    for line in range(loss_ref.shape[0]):
+        part = loss[line * step : (line + 1) * step]
+        loss_ref[line : line + 1, :] = jnp.sum(jnp.where(eye, part, 0.0), axis=0, keepdims=True)
     p_pos = jnp.exp(positive - log_total)
     p_neg_f = jnp.exp(scores - log_total)
     p_neg = p_neg_f.astype(bf16)
@@ -143,21 +186,16 @@
                 ]
 
 
-def collect(place_ref, own_ref, other_ref, grads_ref, kept_ref, up_ref, down_ref, acc_ref):
+def collect(place_ref, asked_ref, grads_ref, kept_ref, up_ref, down_ref, acc_ref):
     blocks, cap, half = grads_ref.shape
     rows = acc_ref.shape[0]
     chunk = rows // 8
     place = place_ref[0]
-    even = (place & 1) == 0
-    asked = (
-        jnp.where(even, own_ref[...], other_ref[...]),
-        jnp.where(even, other_ref[...], own_ref[...]),
-    )
     sub = narrow_iota((rows, cap), 0)
     group = 8
     for first in range(0, blocks, group):
         picks = [
-            ones_where(sub == asked[b % 2][b // 2 : b // 2 + 1, :].astype(i16))
+            ones_where(sub == asked_ref[b : b + 1, :].astype(i16))
             for b in range(first, first + group)
         ]
         part = jnp.dot(
@@ -226,36 +264,51 @@
     half = width // 2
     place = lax.axis_index("dp").astype(i32).reshape(1)
 
-    def swap(value):
-        return lax.ppermute(value, "dp", [(i, i ^ 1) for i in range(n_dp)])
-
     def shift(value, by):
         return lax.ppermute(value, "dp", [(i, (i + by) % n_dp) for i in range(n_dp)])
 
-    asked = lax.all_to_all(slot_rows[0], "feat", split_axis=0, concat_axis=0, tiled=True)
-    asked_other = swap(asked)
+    pairs = [
+        [f * n_dp + 2 * p + h for f in range(n_feat) for h in range(2)] for p in range(n_dp // 2)
+    ]
+
+    def across_pairs(value):
+        return lax.all_to_all(
+            value,
+            ("feat", "dp"),
+            split_axis=0,
+            concat_axis=0,
+            tiled=True,
+            axis_index_groups=pairs,
+        )
+
+    place, slot_rows = lax.optimization_barrier((place, slot_rows))
+    twice = jnp.broadcast_to(slot_rows[0][:, None], (n_feat, 2, cap)).reshape(2 * n_feat, cap)
+    asked = across_pairs(twice)
     served = call(
         gather_rows,
         shape((n_feat, cap, width), bf16),
-        [VM, VM],
+        [SM, VM, VM],
         flops=2 * slots * rows * width,
         moved=rows * width * 2 + slots * width * 2,
-    )(asked, feature_table)
+    )(place, asked, feature_table)
     fetched = lax.all_to_all(served, "feat", split_axis=0, concat_axis=0, tiled=True)
     fetched = fetched.reshape(slots, width)
 
-    bags = jnp.concatenate([head_bags.T, tail_bags.T, negative_bags.T], axis=1)
+    bags = jnp.concatenate([head_bags.T, tail_bags.T], axis=1)
     by_item, by_slot = call(
         count_entries,
         (shape((items, slots), bf16), shape((slots, items), bf16)),
-        [SM, VM],
+        [SM, VM, VM],
         flops=8 * items * slots * 32,
         moved=4 * items * slots,
-    )(slot_counts, bags)
-    rel_pick = (
-        relation_ids[:, None] == lax.broadcasted_iota(i32, (trip, rel_diag.shape[0]), 1)
-    ).astype(bf16)
-    scaling = jnp.dot(rel_pick, rel_diag, preferred_element_type=f32)
+    )(slot_counts, bags, negative_bags)
+    scaling = call(
+        pick_relations,
+        shape((trip, width), f32),
+        [VM, VM],
+        flops=2 * trip * rel_diag.shape[0] * width,
+        moved=2 * rel_diag.shape[0] * width,
+    )(relation_ids.reshape(trip // cap, cap), rel_diag)
 
     query, tails, positive, own_negs = call(
         pool,
@@ -273,7 +326,7 @@
     loss, gneg, grads = call(
         score,
         (
-            shape((trip, 1), f32),
+            shape((trip // cap, cap), f32),
             shape((n_feat, n_neg, width), bf16),
             shape((2 * trip, width), bf16),
         ),
@@ -287,17 +340,7 @@
         [VM, VM, VM],
         flops=2 * items * slots * width,
     )(by_slot, grads, gneg)
-    pairs = [
-        [f * n_dp + 2 * p + h for f in range(n_feat) for h in range(2)] for p in range(n_dp // 2)
-    ]
-    arrived = lax.all_to_all(
-        slot_grad,
-        ("feat", "dp"),
-        split_axis=0,
-        concat_axis=0,
-        tiled=True,
-        axis_index_groups=pairs,
-    )
+    arrived = across_pairs(slot_grad)
     chunk = rows // 8
     kept, up, down = call(
         collect,
@@ -306,10 +349,10 @@
             shape((2, chunk, half), bf16),
             shape((2, chunk, half), bf16),
         ),
-        [SM, VM, VM, VM],
+        [SM, VM, VM],
         scratch=[pltpu.VMEM((rows, half), f32)],
         flops=4 * slots * rows * half,
-    )(place, asked, asked_other, arrived)
+    )(place, asked, arrived)
     nearby = jnp.concatenate([shift(up, 2), shift(down, -2)], axis=0)
     kept = (kept.astype(f32) + nearby.astype(f32)).astype(bf16)
     apart = [[h + 4 * j for j in range(4)] for h in range(4)]

time: 234 us -> 228 us (0.974)
  the two profiles are of different devices: /device:TPU:4 before, /device:TPU:2 now
where the time goes in v4:
time: 228 us; the launch traced here: 227 us
  blocking collectives  150 us (66%)
  Pallas kernels  43.2 us (19%)
  starting transfers between devices  18 us (8%)
  waiting for transfers between devices  7.94 us (3%)
  local copies, waits for them, and re-layouts  7.16 us (3%)
    all_to_all x2, blocking collectives, across_pairs(): lax.all_to_all(value, ('feat', 'dp'), split_axis=0, concat_axis=0, tiled=...  49.9 us
    all_to_all x1, blocking collectives, on_device(): lax.all_to_all(kept, 'dp', split_axis=0, concat_axis=0, tiled=True, axis_...  28.7 us
    all_to_all x1, blocking collectives, on_device(): lax.all_to_all(jnp.broadcast_to(quad[None], (4,) + quad.shape), 'dp', spl...  25.8 us
    all_gather x1, blocking collectives, on_device(): quad = lax.all_gather(summed, 'dp', axis=0, axis_index_groups=apart)  19.1 us
    pallas_call x1, Pallas kernels, on_device(): call(count_entries, (shape((items, slots), bf16), shape((slots, items), b...  17.5 us
    all_to_all x1, blocking collectives, on_device(): lax.all_to_all(own_negs, 'feat', split_axis=0, concat_axis=0, tiled=True)  13.7 us
    ppermute x2, starting transfers between devices, shift(): lax.ppermute(value, 'dp', [(i, (i + by) % n_dp) for i in range(n_dp)])  12.8 us
    all_to_all x1, blocking collectives, on_device(): gneg = lax.all_to_all(gneg, 'feat', split_axis=0, concat_axis=0, tiled=True)  12.4 us
  transfers between devices with their start and end apart: 3, of which 3 were waited for; matrix products, arithmetic and copies ran while one was open for 0% of the time, Pallas kernels for 8%

profile of v4, /device:TPU:2, one launch (start us, length us, event | category | flops | bytes accessed | tf_op | source)
XLA Modules:
  0.0 227.0 jit_solution(6944702227393252620)
XLA Ops:
  0.6 0.7 broadcast_in_dim.14
  1.4 16.3 %all_to_all.41 = s32[64,1,128]{2,1,0:T(1,128)S(1)} all-to-all(s32[64,1,128]{2,1,0:T(1,128)S(1)} %bitcast.18), channel_id=1, replica_groups={{0,1,16,17,32,33,48,49,64,65,80,81,96,97,112,113,128,129,144,145,160,16..., dimensions={0} | all-to-all | bytes 65536 | tf_op jit(solution)/shard_map/all_to_all | solution.py:275
  17.7 1.2 copy-done.3
  18.9 4.7 %shard_map.113 = bf16[32,128,256]{2,1,0:T(8,128)(2,1)S(1)} custom-call(s32[1]{0:T(128)} %bitcast.2.place_ref, s32[64,128]{1,0:T(8,128)S(1)} %bitcast.13, bf16[2048,256]{1,0:T(8,128)(2,1)S(1)} %copy-done.3), custom_call_target="tpu_custom_call" | custom-call | flops 4294967296 | bytes 3145728 | tf_op jit(solution)/shard_map/pallas_call | solution.py:287
  23.6 1.3 copy-done.2
  24.9 5.2 %all-to-all-start.1 = ((bf16[32,128,256]{2,1,0:T(8,128)(2,1)}), bf16[32,128,256]{2,1,0:T(8,128)(2,1)S(1)}, u32[]{:S(2)}, u32[]{:S(2)}) async-start(bf16[32,128,256]{2,1,0:T(8,128)(2,1)} %copy-done.2), calls=%async_computation.1 | async-start | bytes 4194304 | tf_op jit(solution)/shard_map/all_to_all | solution.py:294
  30.1 0.0 copy-start.8
  30.1 0.0 copy-start.1
  30.1 1.6 copy-done.1
  31.7 0.8 shard_map.114.scaling_ref
  32.5 0.0 copy-done.9
  32.5 0.0 copy-done.10
  32.6 17.5 %shard_map.112 = (bf16[528,4096]{1,0:T(8,128)(2,1)S(1)}, bf16[4096,528]{1,0:T(8,128)(2,1)}) custom-call(s32[1,32]{1,0:T(1,128)S(1)} %copy-done.8, s32[16,512]{1,0:T(8,128)S(1)} %pad_add_fusion.bags_ref, s32[16,16]{1,0:T(8,128)S(1)} %copy-done.7), custom_call_target="tpu_custom_call" | custom-call | flops 553648128 | bytes 8650752 | tf_op jit(solution)/shard_map/pallas_call | solution.py:298
  50.1 2.1 copy-done
  52.2 3.9 %all-to-all-done.1 = bf16[32,128,256]{2,1,0:T(8,128)(2,1)S(1)} async-done(((bf16[32,128,256]{2,1,0:T(8,128)(2,1)}), bf16[32,128,256]{2,1,0:T(8,128)(2,1)S(1)}, u32[]{:S(2)}, u32[]{:S(2)}) %all-to-all-start.1) | async-done | bytes 2097184 | tf_op jit(solution)/shard_map/all_to_all | solution.py:294
  56.1 3.6 %shard_map.115 = (bf16[256,256]{1,0:T(8,128)(2,1)S(1)}, bf16[256,256]{1,0:T(8,128)(2,1)S(1)}, f32[256,1]{1,0:T(8,128)S(1)}, bf16[32,16,256]{2,1,0:T(8,128)(2,1)S(1)}) custom-call(bf16[528,4096]{1,0:T(8,128)(2,1)} %copy-done, bf16[4096,256]{1,0:T(8,128)(2,1)S(1)} %bitcast.12, f32[256,256]{1,0:T(8,128)S(1)} %shard_map.114.scaling_ref), custom_call_target="tpu_custom_call" | custom-call | flops 1107296256 | bytes 6422528 | tf_op jit(solution)/shard_map/pallas_call | solution.py:313
  59.6 13.7 %all_to_all.42.negs_ref = bf16[32,16,256]{2,1,0:T(8,128)(2,1)S(1)} all-to-all(bf16[32,16,256]{2,1,0:T(8,128)(2,1)S(1)} %get-tuple-element.25), channel_id=1, replica_groups=mesh['feat'=32,'dp'=16] {'feat'}, dimensions={0} | all-to-all | bytes 524288 | tf_op jit(solution)/shard_map/all_to_all | solution.py:325
  73.4 1.2 shard_map.116
  74.6 12.4 %all_to_all.43.gneg_ref = bf16[32,16,256]{2,1,0:T(8,128)(2,1)S(1)} all-to-all(bf16[32,16,256]{2,1,0:T(8,128)(2,1)S(1)} %get-tuple-element.29), channel_id=1, replica_groups=mesh['feat'=32,'dp'=16] {'feat'}, dimensions={0} | all-to-all | bytes 524288 | tf_op jit(solution)/shard_map/all_to_all | solution.py:336
  87.0 4.3 %shard_map.117 = bf16[64,128,128]{2,1,0:T(8,128)(2,1)S(1)} custom-call(bf16[4096,528]{1,0:T(8,128)(2,1)} %get-tuple-element.27.counts_ref, bf16[512,256]{1,0:T(8,128)(2,1)S(1)} %get-tuple-element.28.grads_ref, bf16[32,16,256]{2,1,0:T(8,128)(2,1)S(1)} %all_to_all.43.gneg_ref), custom_call_target="tpu_custom_call" | custom-call | flops 1107296256 | tf_op jit(solution)/shard_map/pallas_call | solution.py:337
  91.3 33.6 %all_to_all.44.grads_ref = bf16[64,128,128]{2,1,0:T(8,128)(2,1)S(1)} all-to-all(bf16[64,128,128]{2,1,0:T(8,128)(2,1)S(1)} %shard_map.117), channel_id=1, replica_groups={{0,1,16,17,32,33,48,49,64,65,80,81,96,97,112,113,128,129,144,145,160,16..., dimensions={0} | all-to-all | bytes 4194304 | tf_op jit(solution)/shard_map/all_to_all | solution.py:275
  124.9 9.2 %shard_map.118 = (bf16[4,256,128]{2,1,0:T(8,128)(2,1)S(1)}, bf16[2,256,128]{2,1,0:T(8,128)(2,1)S(1)}, bf16[2,256,128]{2,1,0:T(8,128)(2,1)S(1)}) custom-call(s32[1]{0:T(128)} %bitcast.2.place_ref, s32[64,128]{1,0:T(8,128)S(1)} %bitcast.14, bf16[64,128,128]{2,1,0:T(8,128)(2,1)S(1)} %all_to_all.44.grads_ref), custom_call_target="tpu_custom_call" | custom-call | flops 4294967296 | tf_op jit(solution)/shard_map/pallas_call | solution.py:345
  134.1 5.1 %collective-permute-start = (bf16[2,256,128]{2,1,0:T(8,128)(2,1)S(1)}, bf16[2,256,128]{2,1,0:T(8,128)(2,1)S(1)}, u32[]{:S(2)}, u32[]{:S(2)}) collective-permute-start(bf16[2,256,128]{2,1,0:T(8,128)(2,1)S(1)} %get-tuple-element.31), channel_id=1, source_target_pairs={{0,2},{1,3},{2,4},{3,5},{4,6},{5,7},{6,8},{7,9},{8,10},{9,11},{10,... | collective-permute-start | bytes 393224 | tf_op jit(solution)/shard_map/ppermute | solution.py:268
  139.2 7.7 %collective-permute-start.1 = (bf16[2,256,128]{2,1,0:T(8,128)(2,1)S(1)}, bf16[2,256,128]{2,1,0:T(8,128)(2,1)S(1)}, u32[]{:S(2)}, u32[]{:S(2)}) collective-permute-start(bf16[2,256,128]{2,1,0:T(8,128)(2,1)S(1)} %get-tuple-element.32), channel_id=1, source_target_pairs={{0,14},{1,15},{2,0},{3,1},{4,2},{5,3},{6,4},{7,5},{8,6},{9,7},{10,... | collective-permute-start | bytes 393224 | tf_op jit(solution)/shard_map/ppermute | solution.py:268
  146.9 1.7 collective-permute-done
  148.6 2.4 %collective-permute-done.1 = bf16[2,256,128]{2,1,0:T(8,128)(2,1)S(1)} collective-permute-done((bf16[2,256,128]{2,1,0:T(8,128)(2,1)S(1)}, bf16[2,256,128]{2,1,0:T(8,128)(2,1)S(1)}, u32[]{:S(2)}, u32[]{:S(2)}) %collective-permute-start.1) | collective-permute-done | bytes 131104 | tf_op jit(solution)/shard_map/ppermute | solution.py:268
  151.0 0.1 add_convert_fusion
  151.1 28.7 %all_to_all.45 = bf16[4,256,128]{2,1,0:T(8,128)(2,1)S(1)} all-to-all(bf16[4,256,128]{2,1,0:T(8,128)(2,1)S(1)} %add_convert_fusion), channel_id=1, replica_groups={{0,4,8,12},{1,5,9,13},{2,6,10,14},{3,7,11,15},{16,20,24,28},{17,21,25,2..., dimensions={0} | all-to-all | bytes 524288 | tf_op jit(solution)/shard_map/all_to_all | solution.py:359
  179.8 19.1 %all-gather = bf16[1024,128]{1,0:T(8,128)(2,1)S(1)} all-gather(bf16[256,128]{1,0:T(8,128)(2,1)S(1)} %reduce_sum.12), channel_id=2, replica_groups={{0,4,8,12},{1,5,9,13},{2,6,10,14},{3,7,11,15},{16,20,24,28},{17,21,25,2..., dimensions={0}, use_global_device_ids=true | all-gather | bytes 327680 | tf_op jit(solution)/shard_map/all_gather | solution.py:368
  198.9 0.2 broadcast_in_dim.15
  199.1 25.8 %all_to_all.46.sums_ref = bf16[4,4,256,128]{3,2,1,0:T(8,128)(2,1)S(1)} all-to-all(bf16[4,4,256,128]{3,2,1,0:T(8,128)(2,1)S(1)} %broadcast_in_dim.15), channel_id=1, replica_groups={{0,1,2,3},{4,5,6,7},{8,9,10,11},{12,13,14,15},{16,17,18,19},{20,21,22,2..., dimensions={0} | all-to-all | bytes 2097152 | tf_op jit(solution)/shard_map/all_to_all | solution.py:369
  225.0 2.0 shard_map.119
  (16 shorter events, 0.1 us)
Async XLA Ops:
  17.7 1.2 copy-start.3
  23.6 1.3 copy-start.2
  24.9 5.2 %copy-start.6 = (s32[256]{0:T(256)S(1)}, s32[256]{0:T(256)}, u32[]{:S(2)}) copy-start(s32[256]{0:T(256)} %param.17) | copy-start | bytes 3076
  24.9 31.1 %all-to-all-start.1 = ((bf16[32,128,256]{2,1,0:T(8,128)(2,1)}), bf16[32,128,256]{2,1,0:T(8,128)(2,1)S(1)}, u32[]{:S(2)}, u32[]{:S(2)}) async-start(bf16[32,128,256]{2,1,0:T(8,128)(2,1)} %copy-done.2), calls=%async_computation.1 | async-start | bytes 4194304 | tf_op jit(solution)/shard_map/all_to_all | solution.py:294
  30.1 2.4 %copy-start.8 = (s32[1,32]{1,0:T(1,128)S(1)}, s32[1,32]{1,0:T(1,128)}, u32[]{:S(2)}) copy-start(s32[1,32]{1,0:T(1,128)} %counts_ref.1) | copy-start | bytes 388
  30.1 1.6 copy-start.1
  31.7 0.8 copy-start.9
  31.7 0.8 copy-start.10
  31.7 0.8 copy-start.7
  50.1 2.1 copy-start
  134.1 14.5 %collective-permute-start = (bf16[2,256,128]{2,1,0:T(8,128)(2,1)S(1)}, bf16[2,256,128]{2,1,0:T(8,128)(2,1)S(1)}, u32[]{:S(2)}, u32[]{:S(2)}) collective-permute-start(bf16[2,256,128]{2,1,0:T(8,128)(2,1)S(1)} %get-tuple-element.31), channel_id=1, source_target_pairs={{0,2},{1,3},{2,4},{3,5},{4,6},{5,7},{6,8},{7,9},{8,10},{9,11},{10,... | collective-permute-start | bytes 393224 | tf_op jit(solution)/shard_map/ppermute | solution.py:268
  139.2 11.8 %collective-permute-start.1 = (bf16[2,256,128]{2,1,0:T(8,128)(2,1)S(1)}, bf16[2,256,128]{2,1,0:T(8,128)(2,1)S(1)}, u32[]{:S(2)}, u32[]{:S(2)}) collective-permute-start(bf16[2,256,128]{2,1,0:T(8,128)(2,1)S(1)} %get-tuple-element.32), channel_id=1, source_target_pairs={{0,14},{1,15},{2,0},{3,1},{4,2},{5,3},{6,4},{7,5},{8,6},{9,7},{10,... | collective-permute-start | bytes 393224 | tf_op jit(solution)/shard_map/ppermute | solution.py:268
  179.8 45.2 %copy-start.4 = (bf16[2048,256]{1,0:T(8,128)(2,1)S(1)}, bf16[2048,256]{1,0:T(8,128)(2,1)}, u32[]{:S(2)}) copy-start(bf16[2048,256]{1,0:T(8,128)(2,1)} %table_ref.3) | copy-start | bytes 3145732
  179.8 45.2 %copy-start.5 = (f32[2048]{0:T(1024)S(1)}, f32[2048]{0:T(1024)}, u32[]{:S(2)}) copy-start(f32[2048]{0:T(1024)} %param.10) | copy-start | bytes 24580

commit v5 on v4

--- a/solution.py
+++ b/solution.py
@@ -216,8 +216,27 @@
         down_ref[j] = take(2 * j + 5 - parity)
 
 
-def update(table_ref, state_ref, sums_ref, table_out_ref, state_out_ref):
-    chunk, half = sums_ref.shape[2:]
+def update(
+    place_ref,
+    table_ref,
+    state_ref,
+    own_ref,
+    below_ref,
+    above_ref,
+    low_ref,
+    high_ref,
+    table_out_ref,
+    state_out_ref,
+    sums_ref,
+):
+    half = own_ref.shape[2]
+    chunk = own_ref.shape[1]
+    kind = place_ref[0] & 3
+    sums_ref[kind] = own_ref[...]
+    sums_ref[(kind + 3) & 3] = below_ref[...]
+    sums_ref[(kind + 1) & 3] = above_ref[...]
+    sums_ref[(kind + 2) & 3, :2] = low_ref[...]
+    sums_ref[(kind + 2) & 3, 2:] = high_ref[...]
     step = state_ref.shape[1]
     eye = lax.broadcasted_iota(i32, (step, step), 0) == lax.broadcasted_iota(i32, (step, step), 1)
     for c in range(8):
@@ -331,6 +350,7 @@
             shape((2 * trip, width), bf16),
         ),
         [VM] * 5,
+        limit=24,
         flops=6 * trip * n_feat * n_neg * width,
     )(query, tails, positive, scaling, negs)
     gneg = lax.all_to_all(gneg, "feat", split_axis=0, concat_axis=0, tiled=True)
@@ -338,6 +358,7 @@
         spread,
         shape((2 * n_feat, cap, half), bf16),
         [VM, VM, VM],
+        limit=24,
         flops=2 * items * slots * width,
     )(by_slot, grads, gneg)
     arrived = across_pairs(slot_grad)
@@ -366,19 +387,14 @@
     )
     summed = jnp.sum(quarter.astype(f32), axis=0).astype(bf16)
     quad = lax.all_gather(summed, "dp", axis=0, axis_index_groups=apart)
-    whole = lax.all_to_all(
-        jnp.broadcast_to(quad[None], (4,) + quad.shape),
-        "dp",
-        split_axis=0,
-        concat_axis=0,
-        tiled=True,
-        axis_index_groups=[[4 * j + h for h in range(4)] for j in range(4)],
-    )
+    below, above = shift(quad, 1), shift(quad, -1)
+    low, high = shift(quad[:2], 2), shift(quad[2:], -2)
     new_table, new_state = call(
         update,
         (shape((rows, width), bf16), shape((rows // 128, 128), f32)),
-        [VM] * 3,
-    )(feature_table, row_state.reshape(rows // 128, 128), whole)
+        [SM] + [VM] * 7,
+        scratch=[pltpu.VMEM((4, 4, chunk, half), bf16)],
+    )(place, feature_table, row_state.reshape(rows // 128, 128), quad, below, above, low, high)
     return (loss.reshape(trip), new_table, new_state.reshape(rows))
 
 

time: 228 us -> 219 us (0.961)
  blocking collectives: 150 us -> 124 us
  starting transfers between devices: 18 us -> 31.9 us
  waiting for transfers between devices: 7.94 us -> 13.8 us
    all_to_all x1 -> x0, blocking collectives: 25.8 us -> none  [on_device(): lax.all_to_all(jnp.broadcast_to(quad[None], (4,) + quad.shape), 'dp', spl...]
    ppermute x2 -> x6, starting transfers between devices: 12.8 us -> 26.7 us  [shift(): lax.ppermute(value, 'dp', [(i, (i + by) % n_dp) for i in range(n_dp)])]
    ppermute x2 -> x6, waiting for transfers between devices: 4.08 us -> 9.91 us  [shift(): lax.ppermute(value, 'dp', [(i, (i + by) % n_dp) for i in range(n_dp)])]
    pallas_call x1, Pallas kernels: 4.27 us -> 1.78 us  [on_device(): call(spread, shape((2 * n_feat, cap, half), bf16), [VM, VM, VM], limit=24...]
    unnamed x22 -> x24, local copies, waits for them, and re-layouts: 6.24 us -> 6.21 us
  transfers between devices with their start and end apart: 3 -> 7, of which waited for: 3 -> 5; matrix products, arithmetic and copies ran while one was open for 0% -> 0% of each run, Pallas kernels for 8% -> 8%
where the time goes in v5:
time: 219 us; the launch traced here: 218 us
  blocking collectives  124 us (57%)
  Pallas kernels  41 us (19%)
  starting transfers between devices  31.9 us (15%)
  waiting for transfers between devices  13.8 us (6%)
  local copies, waits for them, and re-layouts  6.96 us (3%)
    all_to_all x2, blocking collectives, across_pairs(): lax.all_to_all(value, ('feat', 'dp'), split_axis=0, concat_axis=0, tiled=...  49.9 us
    all_to_all x1, blocking collectives, on_device(): lax.all_to_all(kept, 'dp', split_axis=0, concat_axis=0, tiled=True, axis_...  28.7 us
    ppermute x6, starting transfers between devices, shift(): lax.ppermute(value, 'dp', [(i, (i + by) % n_dp) for i in range(n_dp)])  26.7 us
    all_gather x1, blocking collectives, on_device(): quad = lax.all_gather(summed, 'dp', axis=0, axis_index_groups=apart)  19 us
    pallas_call x1, Pallas kernels, on_device(): call(count_entries, (shape((items, slots), bf16), shape((slots, items), b...  17.6 us
    all_to_all x1, blocking collectives, on_device(): lax.all_to_all(own_negs, 'feat', split_axis=0, concat_axis=0, tiled=True)  13.7 us
    all_to_all x1, blocking collectives, on_device(): gneg = lax.all_to_all(gneg, 'feat', split_axis=0, concat_axis=0, tiled=True)  12.4 us
    ppermute x6, waiting for transfers between devices, shift(): lax.ppermute(value, 'dp', [(i, (i + by) % n_dp) for i in range(n_dp)])  9.91 us
  transfers between devices with their start and end apart: 7, of which 5 were waited for; matrix products, arithmetic and copies ran while one was open for 0% of the time, Pallas kernels for 8%

profile of v5, /device:TPU:2, one launch (start us, length us, event | category | flops | bytes accessed | tf_op | source)
XLA Modules:
  0.0 218.4 jit_solution(3186450948094329792)
XLA Ops:
  0.6 0.7 broadcast_in_dim.8
  1.4 16.3 %all_to_all.36 = s32[64,1,128]{2,1,0:T(1,128)S(1)} all-to-all(s32[64,1,128]{2,1,0:T(1,128)S(1)} %bitcast.22), channel_id=1, replica_groups={{0,1,16,17,32,33,48,49,64,65,80,81,96,97,112,113,128,129,144,145,160,16..., dimensions={0} | all-to-all | bytes 65536 | tf_op jit(solution)/shard_map/all_to_all | solution.py:294
  17.7 1.2 copy-done.4
  18.9 4.7 %shard_map.113 = bf16[32,128,256]{2,1,0:T(8,128)(2,1)S(1)} custom-call(s32[1]{0:T(128)} %bitcast.2.place_ref, s32[64,128]{1,0:T(8,128)S(1)} %bitcast.18, bf16[2048,256]{1,0:T(8,128)(2,1)S(1)} %copy-done.4), custom_call_target="tpu_custom_call" | custom-call | flops 4294967296 | bytes 3145728 | tf_op jit(solution)/shard_map/pallas_call | solution.py:306
  23.6 1.3 copy-done.3
  24.9 5.2 %all-to-all-start.1 = ((bf16[32,128,256]{2,1,0:T(8,128)(2,1)}), bf16[32,128,256]{2,1,0:T(8,128)(2,1)S(1)}, u32[]{:S(2)}, u32[]{:S(2)}) async-start(bf16[32,128,256]{2,1,0:T(8,128)(2,1)} %copy-done.3), calls=%async_computation.1 | async-start | bytes 4194304 | tf_op jit(solution)/shard_map/all_to_all | solution.py:313
  30.1 1.6 copy-done.2
  31.7 0.8 shard_map.114.scaling_ref
  32.6 17.6 %shard_map.112 = (bf16[528,4096]{1,0:T(8,128)(2,1)S(1)}, bf16[4096,528]{1,0:T(8,128)(2,1)}) custom-call(s32[1,32]{1,0:T(1,128)S(1)} %copy-done.9, s32[16,512]{1,0:T(8,128)S(1)} %pad_add_fusion.bags_ref, s32[16,16]{1,0:T(8,128)S(1)} %copy-done.8), custom_call_target="tpu_custom_call" | custom-call | flops 553648128 | bytes 8650752 | tf_op jit(solution)/shard_map/pallas_call | solution.py:317
  50.1 2.1 copy-done.1
  52.2 3.9 %all-to-all-done.1 = bf16[32,128,256]{2,1,0:T(8,128)(2,1)S(1)} async-done(((bf16[32,128,256]{2,1,0:T(8,128)(2,1)}), bf16[32,128,256]{2,1,0:T(8,128)(2,1)S(1)}, u32[]{:S(2)}, u32[]{:S(2)}) %all-to-all-start.1) | async-done | bytes 2097184 | tf_op jit(solution)/shard_map/all_to_all | solution.py:313
  56.1 3.7 %shard_map.115 = (bf16[256,256]{1,0:T(8,128)(2,1)S(1)}, bf16[256,256]{1,0:T(8,128)(2,1)S(1)}, f32[256,1]{1,0:T(8,128)S(1)}, bf16[32,16,256]{2,1,0:T(8,128)(2,1)S(1)}) custom-call(bf16[528,4096]{1,0:T(8,128)(2,1)} %copy-done.1, bf16[4096,256]{1,0:T(8,128)(2,1)S(1)} %bitcast.14, f32[256,256]{1,0:T(8,128)S(1)} %shard_map.114.scaling_ref), custom_call_target="tpu_custom_call" | custom-call | flops 1107296256 | bytes 6422528 | tf_op jit(solution)/shard_map/pallas_call | solution.py:332
  59.8 13.7 %all_to_all.37.negs_ref = bf16[32,16,256]{2,1,0:T(8,128)(2,1)S(1)} all-to-all(bf16[32,16,256]{2,1,0:T(8,128)(2,1)S(1)} %get-tuple-element.25), channel_id=1, replica_groups=mesh['feat'=32,'dp'=16] {'feat'}, dimensions={0} | all-to-all | bytes 524288 | tf_op jit(solution)/shard_map/all_to_all | solution.py:344
  73.5 1.2 shard_map.116
  74.7 12.4 %all_to_all.38.gneg_ref = bf16[32,16,256]{2,1,0:T(8,128)(2,1)S(1)} all-to-all(bf16[32,16,256]{2,1,0:T(8,128)(2,1)S(1)} %get-tuple-element.29), channel_id=1, replica_groups=mesh['feat'=32,'dp'=16] {'feat'}, dimensions={0} | all-to-all | bytes 524288 | tf_op jit(solution)/shard_map/all_to_all | solution.py:356
  87.2 1.8 shard_map.117
  88.9 33.6 %all_to_all.39.grads_ref = bf16[64,128,128]{2,1,0:T(8,128)(2,1)S(1)} all-to-all(bf16[64,128,128]{2,1,0:T(8,128)(2,1)S(1)} %shard_map.117), channel_id=1, replica_groups={{0,1,16,17,32,33,48,49,64,65,80,81,96,97,112,113,128,129,144,145,160,16..., dimensions={0} | all-to-all | bytes 4194304 | tf_op jit(solution)/shard_map/all_to_all | solution.py:294
  122.6 9.2 %shard_map.118 = (bf16[4,256,128]{2,1,0:T(8,128)(2,1)S(1)}, bf16[2,256,128]{2,1,0:T(8,128)(2,1)S(1)}, bf16[2,256,128]{2,1,0:T(8,128)(2,1)S(1)}) custom-call(s32[1]{0:T(128)} %bitcast.2.place_ref, s32[64,128]{1,0:T(8,128)S(1)} %bitcast.19, bf16[64,128,128]{2,1,0:T(8,128)(2,1)S(1)} %all_to_all.39.grads_ref), custom_call_target="tpu_custom_call" | custom-call | flops 4294967296 | tf_op jit(solution)/shard_map/pallas_call | solution.py:366
  131.8 5.2 %collective-permute-start = (bf16[2,256,128]{2,1,0:T(8,128)(2,1)S(1)}, bf16[2,256,128]{2,1,0:T(8,128)(2,1)S(1)}, u32[]{:S(2)}, u32[]{:S(2)}) collective-permute-start(bf16[2,256,128]{2,1,0:T(8,128)(2,1)S(1)} %get-tuple-element.31), channel_id=1, source_target_pairs={{0,2},{1,3},{2,4},{3,5},{4,6},{5,7},{6,8},{7,9},{8,10},{9,11},{10,... | collective-permute-start | bytes 393224 | tf_op jit(solution)/shard_map/ppermute | solution.py:287
  137.0 7.7 %collective-permute-start.1 = (bf16[2,256,128]{2,1,0:T(8,128)(2,1)S(1)}, bf16[2,256,128]{2,1,0:T(8,128)(2,1)S(1)}, u32[]{:S(2)}, u32[]{:S(2)}) collective-permute-start(bf16[2,256,128]{2,1,0:T(8,128)(2,1)S(1)} %get-tuple-element.32), channel_id=1, source_target_pairs={{0,14},{1,15},{2,0},{3,1},{4,2},{5,3},{6,4},{7,5},{8,6},{9,7},{10,... | collective-permute-start | bytes 393224 | tf_op jit(solution)/shard_map/ppermute | solution.py:287
  144.7 1.7 collective-permute-done
  146.4 2.4 %collective-permute-done.1 = bf16[2,256,128]{2,1,0:T(8,128)(2,1)S(1)} collective-permute-done((bf16[2,256,128]{2,1,0:T(8,128)(2,1)S(1)}, bf16[2,256,128]{2,1,0:T(8,128)(2,1)S(1)}, u32[]{:S(2)}, u32[]{:S(2)}) %collective-permute-start.1) | collective-permute-done | bytes 131104 | tf_op jit(solution)/shard_map/ppermute | solution.py:287
  148.8 0.1 add_convert_fusion
  148.9 28.7 %all_to_all.40 = bf16[4,256,128]{2,1,0:T(8,128)(2,1)S(1)} all-to-all(bf16[4,256,128]{2,1,0:T(8,128)(2,1)S(1)} %add_convert_fusion), channel_id=1, replica_groups={{0,4,8,12},{1,5,9,13},{2,6,10,14},{3,7,11,15},{16,20,24,28},{17,21,25,2..., dimensions={0} | all-to-all | bytes 524288 | tf_op jit(solution)/shard_map/all_to_all | solution.py:380
  177.6 19.0 %all-gather = bf16[1024,128]{1,0:T(8,128)(2,1)S(1)} all-gather(bf16[256,128]{1,0:T(8,128)(2,1)S(1)} %reduce_sum.12), channel_id=2, replica_groups={{0,4,8,12},{1,5,9,13},{2,6,10,14},{3,7,11,15},{16,20,24,28},{17,21,25,2..., dimensions={0}, use_global_device_ids=true | all-gather | bytes 327680 | tf_op jit(solution)/shard_map/all_gather | solution.py:389
  196.6 3.0 %collective-permute-start.3 = (bf16[4,256,128]{2,1,0:T(8,128)(2,1)S(1)}, bf16[4,256,128]{2,1,0:T(8,128)(2,1)S(1)}, u32[]{:S(2)}, u32[]{:S(2)}) collective-permute-start(bf16[4,256,128]{2,1,0:T(8,128)(2,1)S(1)} %bitcast.15), channel_id=1, source_target_pairs={{0,15},{1,0},{2,1},{3,2},{4,3},{5,4},{6,5},{7,6},{8,7},{9,8},{10,9... | collective-permute-start | bytes 786440 | tf_op jit(solution)/shard_map/ppermute | solution.py:287
  199.6 2.9 %collective-permute-start.2 = (bf16[4,256,128]{2,1,0:T(8,128)(2,1)S(1)}, bf16[4,256,128]{2,1,0:T(8,128)(2,1)S(1)}, u32[]{:S(2)}, u32[]{:S(2)}) collective-permute-start(bf16[4,256,128]{2,1,0:T(8,128)(2,1)S(1)} %bitcast.16), channel_id=1, source_target_pairs={{0,1},{1,2},{2,3},{3,4},{4,5},{5,6},{6,7},{7,8},{8,9},{9,10},{10,1... | collective-permute-start | bytes 786440 | tf_op jit(solution)/shard_map/ppermute | solution.py:287
  202.5 5.2 %collective-permute-start.4 = (bf16[2,256,128]{2,1,0:T(8,128)(2,1)S(1)}, bf16[2,256,128]{2,1,0:T(8,128)(2,1)S(1)}, u32[]{:S(2)}, u32[]{:S(2)}) collective-permute-start(bf16[2,256,128]{2,1,0:T(8,128)(2,1)S(1)} %bitcast.24), channel_id=1, source_target_pairs={{0,2},{1,3},{2,4},{3,5},{4,6},{5,7},{6,8},{7,9},{8,10},{9,11},{10,... | collective-permute-start | bytes 393224 | tf_op jit(solution)/shard_map/ppermute | solution.py:287
  207.7 2.8 %collective-permute-start.5 = (bf16[2,256,128]{2,1,0:T(8,128)(2,1)S(1)}, bf16[2,256,128]{2,1,0:T(8,128)(2,1)S(1)}, u32[]{:S(2)}, u32[]{:S(2)}) collective-permute-start(bf16[2,256,128]{2,1,0:T(8,128)(2,1)S(1)} %bitcast.23), channel_id=1, source_target_pairs={{0,14},{1,15},{2,0},{3,1},{4,2},{5,3},{6,4},{7,5},{8,6},{9,7},{10,... | collective-permute-start | bytes 393224 | tf_op jit(solution)/shard_map/ppermute | solution.py:287
  210.5 1.9 collective-permute-done.4.low_ref
  212.4 3.9 %collective-permute-done.5.high_ref = bf16[2,256,128]{2,1,0:T(8,128)(2,1)S(1)} collective-permute-done((bf16[2,256,128]{2,1,0:T(8,128)(2,1)S(1)}, bf16[2,256,128]{2,1,0:T(8,128)(2,1)S(1)}, u32[]{:S(2)}, u32[]{:S(2)}) %collective-permute-start.5) | collective-permute-done | bytes 131104 | tf_op jit(solution)/shard_map/ppermute | solution.py:287
  216.3 2.1 shard_map.119
  (25 shorter events, 0.1 us)
Async XLA Ops:
  17.7 1.2 copy-start.4
  23.6 1.3 copy-start.3
  24.9 5.2 %copy-start.7 = (s32[256]{0:T(256)S(1)}, s32[256]{0:T(256)}, u32[]{:S(2)}) copy-start(s32[256]{0:T(256)} %param.17) | copy-start | bytes 3076
  24.9 31.1 %all-to-all-start.1 = ((bf16[32,128,256]{2,1,0:T(8,128)(2,1)}), bf16[32,128,256]{2,1,0:T(8,128)(2,1)S(1)}, u32[]{:S(2)}, u32[]{:S(2)}) async-start(bf16[32,128,256]{2,1,0:T(8,128)(2,1)} %copy-done.3), calls=%async_computation.1 | async-start | bytes 4194304 | tf_op jit(solution)/shard_map/all_to_all | solution.py:313
  30.1 2.4 %copy-start.9 = (s32[1,32]{1,0:T(1,128)S(1)}, s32[1,32]{1,0:T(1,128)}, u32[]{:S(2)}) copy-start(s32[1,32]{1,0:T(1,128)} %counts_ref.1) | copy-start | bytes 388
  30.1 1.6 copy-start.2
  31.7 0.8 copy-start.10
  31.7 0.8 copy-start.11
  31.7 0.8 copy-start.8
  50.1 2.1 copy-start.1
  56.1 31.1 %copy-start = (bf16[4096,528]{1,0:T(8,128)(2,1)S(1)}, bf16[4096,528]{1,0:T(8,128)(2,1)}, u32[]{:S(2)}) copy-start(bf16[4096,528]{1,0:T(8,128)(2,1)} %get-tuple-element.27.counts_ref) | copy-start | bytes 12976132
  131.7 84.6 %copy-start.5 = (bf16[2048,256]{1,0:T(8,128)(2,1)S(1)}, bf16[2048,256]{1,0:T(8,128)(2,1)}, u32[]{:S(2)}) copy-start(bf16[2048,256]{1,0:T(8,128)(2,1)} %table_ref.3) | copy-start | bytes 3145732
  131.8 84.6 %copy-start.6 = (f32[2048]{0:T(1024)S(1)}, f32[2048]{0:T(1024)}, u32[]{:S(2)}) copy-start(f32[2048]{0:T(1024)} %param.10) | copy-start | bytes 24580
  131.8 14.7 %collective-permute-start = (bf16[2,256,128]{2,1,0:T(8,128)(2,1)S(1)}, bf16[2,256,128]{2,1,0:T(8,128)(2,1)S(1)}, u32[]{:S(2)}, u32[]{:S(2)}) collective-permute-start(bf16[2,256,128]{2,1,0:T(8,128)(2,1)S(1)} %get-tuple-element.31), channel_id=1, source_target_pairs={{0,2},{1,3},{2,4},{3,5},{4,6},{5,7},{6,8},{7,9},{8,10},{9,11},{10,... | collective-permute-start | bytes 393224 | tf_op jit(solution)/shard_map/ppermute | solution.py:287
  137.0 11.8 %collective-permute-start.1 = (bf16[2,256,128]{2,1,0:T(8,128)(2,1)S(1)}, bf16[2,256,128]{2,1,0:T(8,128)(2,1)S(1)}, u32[]{:S(2)}, u32[]{:S(2)}) collective-permute-start(bf16[2,256,128]{2,1,0:T(8,128)(2,1)S(1)} %get-tuple-element.32), channel_id=1, source_target_pairs={{0,14},{1,15},{2,0},{3,1},{4,2},{5,3},{6,4},{7,5},{8,6},{9,7},{10,... | collective-permute-start | bytes 393224 | tf_op jit(solution)/shard_map/ppermute | solution.py:287
  196.6 19.7 %collective-permute-start.3 = (bf16[4,256,128]{2,1,0:T(8,128)(2,1)S(1)}, bf16[4,256,128]{2,1,0:T(8,128)(2,1)S(1)}, u32[]{:S(2)}, u32[]{:S(2)}) collective-permute-start(bf16[4,256,128]{2,1,0:T(8,128)(2,1)S(1)} %bitcast.15), channel_id=1, source_target_pairs={{0,15},{1,0},{2,1},{3,2},{4,3},{5,4},{6,5},{7,6},{8,7},{9,8},{10,9... | collective-permute-start | bytes 786440 | tf_op jit(solution)/shard_map/ppermute | solution.py:287
  199.6 16.7 %collective-permute-start.2 = (bf16[4,256,128]{2,1,0:T(8,128)(2,1)S(1)}, bf16[4,256,128]{2,1,0:T(8,128)(2,1)S(1)}, u32[]{:S(2)}, u32[]{:S(2)}) collective-permute-start(bf16[4,256,128]{2,1,0:T(8,128)(2,1)S(1)} %bitcast.16), channel_id=1, source_target_pairs={{0,1},{1,2},{2,3},{3,4},{4,5},{5,6},{6,7},{7,8},{8,9},{9,10},{10,1... | collective-permute-start | bytes 786440 | tf_op jit(solution)/shard_map/ppermute | solution.py:287
  202.5 9.9 %collective-permute-start.4 = (bf16[2,256,128]{2,1,0:T(8,128)(2,1)S(1)}, bf16[2,256,128]{2,1,0:T(8,128)(2,1)S(1)}, u32[]{:S(2)}, u32[]{:S(2)}) collective-permute-start(bf16[2,256,128]{2,1,0:T(8,128)(2,1)S(1)} %bitcast.24), channel_id=1, source_target_pairs={{0,2},{1,3},{2,4},{3,5},{4,6},{5,7},{6,8},{7,9},{8,10},{9,11},{10,... | collective-permute-start | bytes 393224 | tf_op jit(solution)/shard_map/ppermute | solution.py:287
  207.7 8.6 %collective-permute-start.5 = (bf16[2,256,128]{2,1,0:T(8,128)(2,1)S(1)}, bf16[2,256,128]{2,1,0:T(8,128)(2,1)S(1)}, u32[]{:S(2)}, u32[]{:S(2)}) collective-permute-start(bf16[2,256,128]{2,1,0:T(8,128)(2,1)S(1)} %bitcast.23), channel_id=1, source_target_pairs={{0,14},{1,15},{2,0},{3,1},{4,2},{5,3},{6,4},{7,5},{8,6},{9,7},{10,... | collective-permute-start | bytes 393224 | tf_op jit(solution)/shard_map/ppermute | solution.py:287

commit v6 on v5

--- a/solution.py
+++ b/solution.py
@@ -1,3 +1,5 @@
+import functools
+
 import jax
 import jax.numpy as jnp
 from jax import lax
@@ -186,34 +188,32 @@
                 ]
 
 
-def collect(place_ref, asked_ref, grads_ref, kept_ref, up_ref, down_ref, acc_ref):
+def collect(turn, place_ref, asked_ref, grads_ref, *refs):
+    out_refs, acc_ref = refs[:-1], refs[-1]
     blocks, cap, half = grads_ref.shape
-    rows = acc_ref.shape[0]
-    chunk = rows // 8
-    place = place_ref[0]
-    sub = narrow_iota((rows, cap), 0)
+    chunk = acc_ref.shape[1] // 4
+    parity = (place_ref[0] >> 1) & 1
+    parity = 1 - parity if turn else parity
+    lane = lax.broadcasted_iota(i32, (cap, 4 * chunk), 1)
+    row = (lane + (lane // chunk + parity) * chunk).astype(i16)
+    columns = asked_ref[...].T
     group = 8
     for first in range(0, blocks, group):
         picks = [
-            ones_where(sub == asked_ref[b : b + 1, :].astype(i16))
+            ones_where(row == columns[:, b : b + 1].astype(i16))
             for b in range(first, first + group)
         ]
         part = jnp.dot(
-            jnp.concatenate(picks, axis=1),
-            grads_ref[first : first + group].reshape(group * cap, half),
+            grads_ref[first : first + group].reshape(group * cap, half).T,
+            jnp.concatenate(picks, axis=0),
             preferred_element_type=f32,
         )
         acc_ref[...] = part if first == 0 else acc_ref[...] + part
-    parity = (place >> 1) & 1
-
-    def take(c):
-        return acc_ref[pl.ds(pl.multiple_of(c * chunk, chunk), chunk), :].astype(bf16)
-
-    for j in range(4):
-        kept_ref[j] = take(2 * j + parity)
-    for j in range(2):
-        up_ref[j] = take(2 * j + 1 - parity)
-        down_ref[j] = take(2 * j + 5 - parity)
+    j = 0
+    for ref in out_refs:
+        for k in range(ref.shape[0]):
+            ref[k] = acc_ref[:, j * chunk : (j + 1) * chunk].T.astype(bf16)
+            j += 1
 
 
 def update(
@@ -363,16 +363,21 @@
     )(by_slot, grads, gneg)
     arrived = across_pairs(slot_grad)
     chunk = rows // 8
-    kept, up, down = call(
-        collect,
-        (
-            shape((4, chunk, half), bf16),
-            shape((2, chunk, half), bf16),
-            shape((2, chunk, half), bf16),
-        ),
+    scratch = [pltpu.VMEM((half, 4 * chunk), f32)]
+    up, down = call(
+        functools.partial(collect, 1),
+        (shape((2, chunk, half), bf16), shape((2, chunk, half), bf16)),
         [SM, VM, VM],
-        scratch=[pltpu.VMEM((rows, half), f32)],
-        flops=4 * slots * rows * half,
+        scratch=scratch,
+        flops=2 * slots * rows * half,
+    )(place, asked, arrived)
+    kept = call(
+        functools.partial(collect, 0),
+        shape((4, chunk, half), bf16),
+        [SM, VM, VM],
+        scratch=scratch,
+        flops=2 * slots * rows * half,
+        moved=2 * slots * width,
     )(place, asked, arrived)
     nearby = jnp.concatenate([shift(up, 2), shift(down, -2)], axis=0)
     kept = (kept.astype(f32) + nearby.astype(f32)).astype(bf16)

time: 219 us -> 213 us (0.973)
  Pallas kernels: 41 us -> 37.1 us
  waiting for transfers between devices: 13.8 us -> 11.1 us
    pallas_call x1 -> x2, Pallas kernels: 9.19 us -> 5.37 us  [the longest x1 2.69 us: on_device(): call(functools.partial(collect, 1), (shape((2, chunk, half), bf16), shape...]
    ppermute x6, waiting for transfers between devices: 9.91 us -> 7.28 us  [shift(): lax.ppermute(value, 'dp', [(i, (i + by) % n_dp) for i in range(n_dp)])]
  transfers between devices with their start and end apart: 7 -> 7, of which waited for: 5 -> 4; matrix products, arithmetic and copies ran while one was open for 0% -> 0% of each run, Pallas kernels for 8% -> 10%
where the time goes in v6:
time: 213 us; the launch traced here: 212 us
  blocking collectives  124 us (58%)
  Pallas kernels  37.1 us (17%)
  starting transfers between devices  31.8 us (15%)
  waiting for transfers between devices  11.1 us (5%)
  local copies, waits for them, and re-layouts  6.96 us (3%)
    all_to_all x2, blocking collectives, across_pairs(): lax.all_to_all(value, ('feat', 'dp'), split_axis=0, concat_axis=0, tiled=...  49.9 us
    all_to_all x1, blocking collectives, on_device(): lax.all_to_all(kept, 'dp', split_axis=0, concat_axis=0, tiled=True, axis_...  28.7 us
    ppermute x6, starting transfers between devices, shift(): lax.ppermute(value, 'dp', [(i, (i + by) % n_dp) for i in range(n_dp)])  26.6 us
    all_gather x1, blocking collectives, on_device(): quad = lax.all_gather(summed, 'dp', axis=0, axis_index_groups=apart)  19.2 us
    pallas_call x1, Pallas kernels, on_device(): call(count_entries, (shape((items, slots), bf16), shape((slots, items), b...  17.6 us
    all_to_all x1, blocking collectives, on_device(): lax.all_to_all(own_negs, 'feat', split_axis=0, concat_axis=0, tiled=True)  13.7 us
    all_to_all x1, blocking collectives, on_device(): gneg = lax.all_to_all(gneg, 'feat', split_axis=0, concat_axis=0, tiled=True)  12.4 us
    ppermute x6, waiting for transfers between devices, shift(): lax.ppermute(value, 'dp', [(i, (i + by) % n_dp) for i in range(n_dp)])  7.28 us
  transfers between devices with their start and end apart: 7, of which 4 were waited for; matrix products, arithmetic and copies ran while one was open for 0% of the time, Pallas kernels for 10%

profile of v6, /device:TPU:2, one launch (start us, length us, event | category | flops | bytes accessed | tf_op | source)
XLA Modules:
  0.0 212.0 jit_solution(5098020934854052812)
XLA Ops:
  0.6 0.7 broadcast_in_dim.8
  1.4 16.3 %all_to_all.36 = s32[64,1,128]{2,1,0:T(1,128)S(1)} all-to-all(s32[64,1,128]{2,1,0:T(1,128)S(1)} %bitcast.23), channel_id=1, replica_groups={{0,1,16,17,32,33,48,49,64,65,80,81,96,97,112,113,128,129,144,145,160,16..., dimensions={0} | all-to-all | bytes 65536 | tf_op jit(solution)/shard_map/all_to_all | solution.py:294
  17.7 1.2 copy-done.4
  18.9 4.7 %shard_map.113 = bf16[32,128,256]{2,1,0:T(8,128)(2,1)S(1)} custom-call(s32[1]{0:T(128)} %bitcast.2.place_ref, s32[64,128]{1,0:T(8,128)S(1)} %bitcast.18, bf16[2048,256]{1,0:T(8,128)(2,1)S(1)} %copy-done.4), custom_call_target="tpu_custom_call" | custom-call | flops 4294967296 | bytes 3145728 | tf_op jit(solution)/shard_map/pallas_call | solution.py:306
  23.6 1.3 copy-done.3
  24.9 5.2 %all-to-all-start.1 = ((bf16[32,128,256]{2,1,0:T(8,128)(2,1)}), bf16[32,128,256]{2,1,0:T(8,128)(2,1)S(1)}, u32[]{:S(2)}, u32[]{:S(2)}) async-start(bf16[32,128,256]{2,1,0:T(8,128)(2,1)} %copy-done.3), calls=%async_computation.1 | async-start | bytes 4194304 | tf_op jit(solution)/shard_map/all_to_all | solution.py:313
  30.1 1.6 copy-done.2
  31.7 0.8 shard_map.114.scaling_ref
  32.6 17.6 %shard_map.112 = (bf16[528,4096]{1,0:T(8,128)(2,1)S(1)}, bf16[4096,528]{1,0:T(8,128)(2,1)}) custom-call(s32[1,32]{1,0:T(1,128)S(1)} %copy-done.9, s32[16,512]{1,0:T(8,128)S(1)} %pad_add_fusion.bags_ref, s32[16,16]{1,0:T(8,128)S(1)} %copy-done.8), custom_call_target="tpu_custom_call" | custom-call | flops 553648128 | bytes 8650752 | tf_op jit(solution)/shard_map/pallas_call | solution.py:317
  50.1 2.1 copy-done.1
  52.2 3.9 %all-to-all-done.1 = bf16[32,128,256]{2,1,0:T(8,128)(2,1)S(1)} async-done(((bf16[32,128,256]{2,1,0:T(8,128)(2,1)}), bf16[32,128,256]{2,1,0:T(8,128)(2,1)S(1)}, u32[]{:S(2)}, u32[]{:S(2)}) %all-to-all-start.1) | async-done | bytes 2097184 | tf_op jit(solution)/shard_map/all_to_all | solution.py:313
  56.1 3.7 %shard_map.115 = (bf16[256,256]{1,0:T(8,128)(2,1)S(1)}, bf16[256,256]{1,0:T(8,128)(2,1)S(1)}, f32[256,1]{1,0:T(8,128)S(1)}, bf16[32,16,256]{2,1,0:T(8,128)(2,1)S(1)}) custom-call(bf16[528,4096]{1,0:T(8,128)(2,1)} %copy-done.1, bf16[4096,256]{1,0:T(8,128)(2,1)S(1)} %bitcast.14, f32[256,256]{1,0:T(8,128)S(1)} %shard_map.114.scaling_ref), custom_call_target="tpu_custom_call" | custom-call | flops 1107296256 | bytes 6422528 | tf_op jit(solution)/shard_map/pallas_call | solution.py:332
  59.8 13.7 %all_to_all.37.negs_ref = bf16[32,16,256]{2,1,0:T(8,128)(2,1)S(1)} all-to-all(bf16[32,16,256]{2,1,0:T(8,128)(2,1)S(1)} %get-tuple-element.24), channel_id=1, replica_groups=mesh['feat'=32,'dp'=16] {'feat'}, dimensions={0} | all-to-all | bytes 524288 | tf_op jit(solution)/shard_map/all_to_all | solution.py:344
  73.5 1.2 shard_map.116
  74.7 12.4 %all_to_all.38.gneg_ref = bf16[32,16,256]{2,1,0:T(8,128)(2,1)S(1)} all-to-all(bf16[32,16,256]{2,1,0:T(8,128)(2,1)S(1)} %get-tuple-element.28), channel_id=1, replica_groups=mesh['feat'=32,'dp'=16] {'feat'}, dimensions={0} | all-to-all | bytes 524288 | tf_op jit(solution)/shard_map/all_to_all | solution.py:356
  87.2 1.8 shard_map.117
  88.9 33.6 %all_to_all.39.grads_ref = bf16[64,128,128]{2,1,0:T(8,128)(2,1)S(1)} all-to-all(bf16[64,128,128]{2,1,0:T(8,128)(2,1)S(1)} %shard_map.117), channel_id=1, replica_groups={{0,1,16,17,32,33,48,49,64,65,80,81,96,97,112,113,128,129,144,145,160,16..., dimensions={0} | all-to-all | bytes 4194304 | tf_op jit(solution)/shard_map/all_to_all | solution.py:294
  122.6 2.7 %shard_map.119 = (bf16[2,256,128]{2,1,0:T(8,128)(2,1)S(1)}, bf16[2,256,128]{2,1,0:T(8,128)(2,1)S(1)}) custom-call(s32[1]{0:T(128)} %bitcast.2.place_ref, s32[64,128]{1,0:T(8,128)S(1)} %bitcast.19, bf16[64,128,128]{2,1,0:T(8,128)(2,1)S(1)} %all_to_all.39.grads_ref), custom_call_target="tpu_custom_call" | custom-call | flops 2147483648 | tf_op jit(solution)/shard_map/pallas_call | solution.py:367
  125.2 5.1 %collective-permute-start = (bf16[2,256,128]{2,1,0:T(8,128)(2,1)S(1)}, bf16[2,256,128]{2,1,0:T(8,128)(2,1)S(1)}, u32[]{:S(2)}, u32[]{:S(2)}) collective-permute-start(bf16[2,256,128]{2,1,0:T(8,128)(2,1)S(1)} %get-tuple-element.29), channel_id=1, source_target_pairs={{0,2},{1,3},{2,4},{3,5},{4,6},{5,7},{6,8},{7,9},{8,10},{9,11},{10,... | collective-permute-start | bytes 393224 | tf_op jit(solution)/shard_map/ppermute | solution.py:287
  130.4 7.7 %collective-permute-start.1 = (bf16[2,256,128]{2,1,0:T(8,128)(2,1)S(1)}, bf16[2,256,128]{2,1,0:T(8,128)(2,1)S(1)}, u32[]{:S(2)}, u32[]{:S(2)}) collective-permute-start(bf16[2,256,128]{2,1,0:T(8,128)(2,1)S(1)} %get-tuple-element.30), channel_id=1, source_target_pairs={{0,14},{1,15},{2,0},{3,1},{4,2},{5,3},{6,4},{7,5},{8,6},{9,7},{10,... | collective-permute-start | bytes 393224 | tf_op jit(solution)/shard_map/ppermute | solution.py:287
  138.1 2.7 %shard_map.118 = bf16[4,256,128]{2,1,0:T(8,128)(2,1)S(1)} custom-call(s32[1]{0:T(128)} %bitcast.2.place_ref, s32[64,128]{1,0:T(8,128)S(1)} %bitcast.20, bf16[64,128,128]{2,1,0:T(8,128)(2,1)S(1)} %all_to_all.39.grads_ref), custom_call_target="tpu_custom_call" | custom-call | flops 2147483648 | bytes 2097152 | tf_op jit(solution)/shard_map/pallas_call | solution.py:374
  140.8 1.4 collective-permute-done.1
  142.1 0.1 add_convert_fusion
  142.2 28.7 %all_to_all.40 = bf16[4,256,128]{2,1,0:T(8,128)(2,1)S(1)} all-to-all(bf16[4,256,128]{2,1,0:T(8,128)(2,1)S(1)} %add_convert_fusion), channel_id=1, replica_groups={{0,4,8,12},{1,5,9,13},{2,6,10,14},{3,7,11,15},{16,20,24,28},{17,21,25,2..., dimensions={0} | all-to-all | bytes 524288 | tf_op jit(solution)/shard_map/all_to_all | solution.py:385
  171.0 19.2 %all-gather = bf16[1024,128]{1,0:T(8,128)(2,1)S(1)} all-gather(bf16[256,128]{1,0:T(8,128)(2,1)S(1)} %reduce_sum.12), channel_id=2, replica_groups={{0,4,8,12},{1,5,9,13},{2,6,10,14},{3,7,11,15},{16,20,24,28},{17,21,25,2..., dimensions={0}, use_global_device_ids=true | all-gather | bytes 327680 | tf_op jit(solution)/shard_map/all_gather | solution.py:394
  190.1 3.2 %collective-permute-start.3 = (bf16[4,256,128]{2,1,0:T(8,128)(2,1)S(1)}, bf16[4,256,128]{2,1,0:T(8,128)(2,1)S(1)}, u32[]{:S(2)}, u32[]{:S(2)}) collective-permute-start(bf16[4,256,128]{2,1,0:T(8,128)(2,1)S(1)} %bitcast.15), channel_id=1, source_target_pairs={{0,15},{1,0},{2,1},{3,2},{4,3},{5,4},{6,5},{7,6},{8,7},{9,8},{10,9... | collective-permute-start | bytes 786440 | tf_op jit(solution)/shard_map/ppermute | solution.py:287
  193.4 2.6 %collective-permute-start.2 = (bf16[4,256,128]{2,1,0:T(8,128)(2,1)S(1)}, bf16[4,256,128]{2,1,0:T(8,128)(2,1)S(1)}, u32[]{:S(2)}, u32[]{:S(2)}) collective-permute-start(bf16[4,256,128]{2,1,0:T(8,128)(2,1)S(1)} %bitcast.16), channel_id=1, source_target_pairs={{0,1},{1,2},{2,3},{3,4},{4,5},{5,6},{6,7},{7,8},{8,9},{9,10},{10,1... | collective-permute-start | bytes 786440 | tf_op jit(solution)/shard_map/ppermute | solution.py:287
  196.0 5.2 %collective-permute-start.4 = (bf16[2,256,128]{2,1,0:T(8,128)(2,1)S(1)}, bf16[2,256,128]{2,1,0:T(8,128)(2,1)S(1)}, u32[]{:S(2)}, u32[]{:S(2)}) collective-permute-start(bf16[2,256,128]{2,1,0:T(8,128)(2,1)S(1)} %bitcast.25), channel_id=1, source_target_pairs={{0,2},{1,3},{2,4},{3,5},{4,6},{5,7},{6,8},{7,9},{8,10},{9,11},{10,... | collective-permute-start | bytes 393224 | tf_op jit(solution)/shard_map/ppermute | solution.py:287
  201.3 2.7 %collective-permute-start.5 = (bf16[2,256,128]{2,1,0:T(8,128)(2,1)S(1)}, bf16[2,256,128]{2,1,0:T(8,128)(2,1)S(1)}, u32[]{:S(2)}, u32[]{:S(2)}) collective-permute-start(bf16[2,256,128]{2,1,0:T(8,128)(2,1)S(1)} %bitcast.24), channel_id=1, source_target_pairs={{0,14},{1,15},{2,0},{3,1},{4,2},{5,3},{6,4},{7,5},{8,6},{9,7},{10,... | collective-permute-start | bytes 393224 | tf_op jit(solution)/shard_map/ppermute | solution.py:287
  204.0 1.4 collective-permute-done.4.low_ref
  205.4 4.5 %collective-permute-done.5.high_ref = bf16[2,256,128]{2,1,0:T(8,128)(2,1)S(1)} collective-permute-done((bf16[2,256,128]{2,1,0:T(8,128)(2,1)S(1)}, bf16[2,256,128]{2,1,0:T(8,128)(2,1)S(1)}, u32[]{:S(2)}, u32[]{:S(2)}) %collective-permute-start.5) | collective-permute-done | bytes 131104 | tf_op jit(solution)/shard_map/ppermute | solution.py:287
  209.9 2.1 shard_map.120
  (26 shorter events, 0.1 us)
Async XLA Ops:
  17.7 1.2 copy-start.4
  23.6 1.3 copy-start.3
  24.9 5.2 %copy-start.7 = (s32[256]{0:T(256)S(1)}, s32[256]{0:T(256)}, u32[]{:S(2)}) copy-start(s32[256]{0:T(256)} %param.17) | copy-start | bytes 3076
  24.9 31.1 %all-to-all-start.1 = ((bf16[32,128,256]{2,1,0:T(8,128)(2,1)}), bf16[32,128,256]{2,1,0:T(8,128)(2,1)S(1)}, u32[]{:S(2)}, u32[]{:S(2)}) async-start(bf16[32,128,256]{2,1,0:T(8,128)(2,1)} %copy-done.3), calls=%async_computation.1 | async-start | bytes 4194304 | tf_op jit(solution)/shard_map/all_to_all | solution.py:313
  30.1 2.4 %copy-start.9 = (s32[1,32]{1,0:T(1,128)S(1)}, s32[1,32]{1,0:T(1,128)}, u32[]{:S(2)}) copy-start(s32[1,32]{1,0:T(1,128)} %counts_ref.1) | copy-start | bytes 388
  30.1 1.6 copy-start.2
  31.7 0.8 copy-start.10
  31.7 0.8 copy-start.11
  31.7 0.8 copy-start.8
  50.1 2.1 copy-start.1
  56.1 31.1 %copy-start = (bf16[4096,528]{1,0:T(8,128)(2,1)S(1)}, bf16[4096,528]{1,0:T(8,128)(2,1)}, u32[]{:S(2)}) copy-start(bf16[4096,528]{1,0:T(8,128)(2,1)} %get-tuple-element.26.counts_ref) | copy-start | bytes 12976132
  125.2 15.5 %collective-permute-start = (bf16[2,256,128]{2,1,0:T(8,128)(2,1)S(1)}, bf16[2,256,128]{2,1,0:T(8,128)(2,1)S(1)}, u32[]{:S(2)}, u32[]{:S(2)}) collective-permute-start(bf16[2,256,128]{2,1,0:T(8,128)(2,1)S(1)} %get-tuple-element.29), channel_id=1, source_target_pairs={{0,2},{1,3},{2,4},{3,5},{4,6},{5,7},{6,8},{7,9},{8,10},{9,11},{10,... | collective-permute-start | bytes 393224 | tf_op jit(solution)/shard_map/ppermute | solution.py:287
  130.4 11.8 %collective-permute-start.1 = (bf16[2,256,128]{2,1,0:T(8,128)(2,1)S(1)}, bf16[2,256,128]{2,1,0:T(8,128)(2,1)S(1)}, u32[]{:S(2)}, u32[]{:S(2)}) collective-permute-start(bf16[2,256,128]{2,1,0:T(8,128)(2,1)S(1)} %get-tuple-element.30), channel_id=1, source_target_pairs={{0,14},{1,15},{2,0},{3,1},{4,2},{5,3},{6,4},{7,5},{8,6},{9,7},{10,... | collective-permute-start | bytes 393224 | tf_op jit(solution)/shard_map/ppermute | solution.py:287
  140.8 69.1 %copy-start.5 = (bf16[2048,256]{1,0:T(8,128)(2,1)S(1)}, bf16[2048,256]{1,0:T(8,128)(2,1)}, u32[]{:S(2)}) copy-start(bf16[2048,256]{1,0:T(8,128)(2,1)} %table_ref.3) | copy-start | bytes 3145732
  140.8 69.1 %copy-start.6 = (f32[2048]{0:T(1024)S(1)}, f32[2048]{0:T(1024)}, u32[]{:S(2)}) copy-start(f32[2048]{0:T(1024)} %param.10) | copy-start | bytes 24580
  190.1 19.8 %collective-permute-start.3 = (bf16[4,256,128]{2,1,0:T(8,128)(2,1)S(1)}, bf16[4,256,128]{2,1,0:T(8,128)(2,1)S(1)}, u32[]{:S(2)}, u32[]{:S(2)}) collective-permute-start(bf16[4,256,128]{2,1,0:T(8,128)(2,1)S(1)} %bitcast.15), channel_id=1, source_target_pairs={{0,15},{1,0},{2,1},{3,2},{4,3},{5,4},{6,5},{7,6},{8,7},{9,8},{10,9... | collective-permute-start | bytes 786440 | tf_op jit(solution)/shard_map/ppermute | solution.py:287
  193.4 16.5 %collective-permute-start.2 = (bf16[4,256,128]{2,1,0:T(8,128)(2,1)S(1)}, bf16[4,256,128]{2,1,0:T(8,128)(2,1)S(1)}, u32[]{:S(2)}, u32[]{:S(2)}) collective-permute-start(bf16[4,256,128]{2,1,0:T(8,128)(2,1)S(1)} %bitcast.16), channel_id=1, source_target_pairs={{0,1},{1,2},{2,3},{3,4},{4,5},{5,6},{6,7},{7,8},{8,9},{9,10},{10,1... | collective-permute-start | bytes 786440 | tf_op jit(solution)/shard_map/ppermute | solution.py:287
  196.0 9.4 %collective-permute-start.4 = (bf16[2,256,128]{2,1,0:T(8,128)(2,1)S(1)}, bf16[2,256,128]{2,1,0:T(8,128)(2,1)S(1)}, u32[]{:S(2)}, u32[]{:S(2)}) collective-permute-start(bf16[2,256,128]{2,1,0:T(8,128)(2,1)S(1)} %bitcast.25), channel_id=1, source_target_pairs={{0,2},{1,3},{2,4},{3,5},{4,6},{5,7},{6,8},{7,9},{8,10},{9,11},{10,... | collective-permute-start | bytes 393224 | tf_op jit(solution)/shard_map/ppermute | solution.py:287
  201.3 8.6 %collective-permute-start.5 = (bf16[2,256,128]{2,1,0:T(8,128)(2,1)S(1)}, bf16[2,256,128]{2,1,0:T(8,128)(2,1)S(1)}, u32[]{:S(2)}, u32[]{:S(2)}) collective-permute-start(bf16[2,256,128]{2,1,0:T(8,128)(2,1)S(1)} %bitcast.24), channel_id=1, source_target_pairs={{0,14},{1,15},{2,0},{3,1},{4,2},{5,3},{6,4},{7,5},{8,6},{9,7},{10,... | collective-permute-start | bytes 393224 | tf_op jit(solution)/shard_map/ppermute | solution.py:287

commit v7 on v6

--- a/solution.py
+++ b/solution.py
@@ -122,10 +122,33 @@
         )
 
 
-def pool(counts_ref, fetched_ref, scaling_ref, query_ref, tails_ref, positive_ref, negs_ref):
+def pool(
+    counts_ref,
+    fetched_ref,
+    scaling_ref,
+    query_ref,
+    tails_ref,
+    positive_ref,
+    negs_ref,
+    held_ref,
+    sems,
+):
     bag = 16
     trip = query_ref.shape[0]
-    pooled = jnp.dot(counts_ref[...], fetched_ref[...], preferred_element_type=f32)
+    pieces = sems.shape[0]
+    wide = fetched_ref.shape[0] // pieces
+    spans = [slice(k * wide, (k + 1) * wide) for k in range(pieces)]
+    copies = [
+        pltpu.make_async_copy(counts_ref.at[:, span], held_ref.at[:, span], sems.at[k])
+        for k, span in enumerate(spans)
+    ]
+    for copy in copies:
+        copy.start()
+    pooled = None
+    for copy, span in zip(copies, spans):
+        copy.wait()
+        part = jnp.dot(held_ref[:, span], fetched_ref[span, :], preferred_element_type=f32)
+        pooled = part if pooled is None else pooled + part
     entity = (pooled * (1.0 / bag)).astype(bf16)
     negs_ref[...] = jnp.broadcast_to(entity[None, 2 * trip :], negs_ref.shape)
     tails = entity[trip : 2 * trip]
@@ -188,8 +211,7 @@
                 ]
 
 
-def collect(turn, place_ref, asked_ref, grads_ref, *refs):
-    out_refs, acc_ref = refs[:-1], refs[-1]
+def collect(turn, place_ref, asked_ref, grads_ref, out_ref, acc_ref):
     blocks, cap, half = grads_ref.shape
     chunk = acc_ref.shape[1] // 4
     parity = (place_ref[0] >> 1) & 1
@@ -209,11 +231,8 @@
             preferred_element_type=f32,
         )
         acc_ref[...] = part if first == 0 else acc_ref[...] + part
-    j = 0
-    for ref in out_refs:
-        for k in range(ref.shape[0]):
-            ref[k] = acc_ref[:, j * chunk : (j + 1) * chunk].T.astype(bf16)
-            j += 1
+    for j in range(4):
+        out_ref[j] = acc_ref[:, j * chunk : (j + 1) * chunk].T.astype(bf16)
 
 
 def update(
@@ -223,8 +242,7 @@
     own_ref,
     below_ref,
     above_ref,
-    low_ref,
-    high_ref,
+    beyond_ref,
     table_out_ref,
     state_out_ref,
     sums_ref,
@@ -235,8 +253,7 @@
     sums_ref[kind] = own_ref[...]
     sums_ref[(kind + 3) & 3] = below_ref[...]
     sums_ref[(kind + 1) & 3] = above_ref[...]
-    sums_ref[(kind + 2) & 3, :2] = low_ref[...]
-    sums_ref[(kind + 2) & 3, 2:] = high_ref[...]
+    sums_ref[(kind + 2) & 3] = beyond_ref[...]
     step = state_ref.shape[1]
     eye = lax.broadcasted_iota(i32, (step, step), 0) == lax.broadcasted_iota(i32, (step, step), 1)
     for c in range(8):
@@ -337,7 +354,8 @@
             shape((trip, 1), f32),
             shape((n_feat, n_neg, width), bf16),
         ),
-        [VM, VM, VM],
+        [pl.BlockSpec(memory_space=pl.ANY), VM, VM],
+        scratch=[pltpu.VMEM((items, slots), bf16), pltpu.SemaphoreType.DMA((4,))],
         flops=2 * items * slots * width,
         moved=2 * slots * (width + items),
     )(by_item, fetched, scaling)
@@ -364,9 +382,9 @@
     arrived = across_pairs(slot_grad)
     chunk = rows // 8
     scratch = [pltpu.VMEM((half, 4 * chunk), f32)]
-    up, down = call(
+    sent = call(
         functools.partial(collect, 1),
-        (shape((2, chunk, half), bf16), shape((2, chunk, half), bf16)),
+        shape((4, chunk, half), bf16),
         [SM, VM, VM],
         scratch=scratch,
         flops=2 * slots * rows * half,
@@ -379,7 +397,7 @@
         flops=2 * slots * rows * half,
         moved=2 * slots * width,
     )(place, asked, arrived)
-    nearby = jnp.concatenate([shift(up, 2), shift(down, -2)], axis=0)
+    nearby = lax.ppermute(sent, "dp", [(i, i ^ 2) for i in range(n_dp)])
     kept = (kept.astype(f32) + nearby.astype(f32)).astype(bf16)
     apart = [[h + 4 * j for j in range(4)] for h in range(4)]
     quarter = lax.all_to_all(
@@ -393,13 +411,13 @@
     summed = jnp.sum(quarter.astype(f32), axis=0).astype(bf16)
     quad = lax.all_gather(summed, "dp", axis=0, axis_index_groups=apart)
     below, above = shift(quad, 1), shift(quad, -1)
-    low, high = shift(quad[:2], 2), shift(quad[2:], -2)
+    beyond = shift(quad, 2)
     new_table, new_state = call(
         update,
         (shape((rows, width), bf16), shape((rows // 128, 128), f32)),
-        [SM] + [VM] * 7,
+        [SM] + [VM] * 6,
         scratch=[pltpu.VMEM((4, 4, chunk, half), bf16)],
-    )(place, feature_table, row_state.reshape(rows // 128, 128), quad, below, above, low, high)
+    )(place, feature_table, row_state.reshape(rows // 128, 128), quad, below, above, beyond)
     return (loss.reshape(trip), new_table, new_state.reshape(rows))
 
 

time: 213 us -> 215 us (level)
  the two profiles are of different devices: /device:TPU:2 before, /device:TPU:4 now
where the time goes in v7:
time: 215 us
  blocking collectives  125 us (58%)
  Pallas kernels  37.8 us (18%)
  starting transfers between devices  22.1 us (10%)
  waiting for transfers between devices  21.7 us (10%)
  local copies, waits for them, and re-layouts  6.96 us (3%)
    all_to_all x2, blocking collectives, across_pairs(): lax.all_to_all(value, ('feat', 'dp'), split_axis=0, concat_axis=0, tiled=...  47.9 us
    all_to_all x1, blocking collectives, on_device(): lax.all_to_all(kept, 'dp', split_axis=0, concat_axis=0, tiled=True, axis_...  31.6 us
    all_gather x1, blocking collectives, on_device(): quad = lax.all_gather(summed, 'dp', axis=0, axis_index_groups=apart)  20.3 us
    pallas_call x1, Pallas kernels, on_device(): call(count_entries, (shape((items, slots), bf16), shape((slots, items), b...  17.5 us
    all_to_all x1, blocking collectives, on_device(): lax.all_to_all(own_negs, 'feat', split_axis=0, concat_axis=0, tiled=True)  13.1 us
    all_to_all x1, blocking collectives, on_device(): gneg = lax.all_to_all(gneg, 'feat', split_axis=0, concat_axis=0, tiled=True)  12.4 us
    ppermute x3, starting transfers between devices, shift(): lax.ppermute(value, 'dp', [(i, (i + by) % n_dp) for i in range(n_dp)])  10.9 us
    ppermute x1, waiting for transfers between devices, on_device(): nearby = lax.ppermute(sent, 'dp', [(i, i ^ 2) for i in range(n_dp)])  9.96 us
  transfers between devices with their start and end apart: 5, of which 4 were waited for; matrix products, arithmetic and copies ran while one was open for 0% of the time, Pallas kernels for 10%

profile of v7, /device:TPU:4, one launch (start us, length us, event | category | flops | bytes accessed | tf_op | source)
XLA Modules:
  0.0 214.7 jit_solution(10723155564952360502)
XLA Ops:
  0.6 0.7 broadcast_in_dim.8
  1.4 15.5 %all_to_all.36 = s32[64,1,128]{2,1,0:T(1,128)S(1)} all-to-all(s32[64,1,128]{2,1,0:T(1,128)S(1)} %bitcast.22), channel_id=1, replica_groups={{0,1,16,17,32,33,48,49,64,65,80,81,96,97,112,113,128,129,144,145,160,16..., dimensions={0} | all-to-all | bytes 65536 | tf_op jit(solution)/shard_map/all_to_all | solution.py:311
  16.8 1.2 copy-done.4
  18.1 4.7 %shard_map.113 = bf16[32,128,256]{2,1,0:T(8,128)(2,1)S(1)} custom-call(s32[1]{0:T(128)} %bitcast.2.place_ref, s32[64,128]{1,0:T(8,128)S(1)} %bitcast.17, bf16[2048,256]{1,0:T(8,128)(2,1)S(1)} %copy-done.4), custom_call_target="tpu_custom_call" | custom-call | flops 4294967296 | bytes 3145728 | tf_op jit(solution)/shard_map/pallas_call | solution.py:323
  22.7 1.3 copy-done.3
  24.0 6.1 %all-to-all-start.1 = ((bf16[32,128,256]{2,1,0:T(8,128)(2,1)}), bf16[32,128,256]{2,1,0:T(8,128)(2,1)S(1)}, u32[]{:S(2)}, u32[]{:S(2)}) async-start(bf16[32,128,256]{2,1,0:T(8,128)(2,1)} %copy-done.3), calls=%async_computation.1 | async-start | bytes 4194304 | tf_op jit(solution)/shard_map/all_to_all | solution.py:330
  30.2 1.6 copy-done.2
  31.8 0.8 shard_map.114.scaling_ref
  32.6 17.5 %shard_map.112 = (bf16[528,4096]{1,0:T(8,128)(2,1)S(1)}, bf16[4096,528]{1,0:T(8,128)(2,1)}) custom-call(s32[1,32]{1,0:T(1,128)S(1)} %copy-done.9, s32[16,512]{1,0:T(8,128)S(1)} %pad_add_fusion.bags_ref, s32[16,16]{1,0:T(8,128)S(1)} %copy-done.8), custom_call_target="tpu_custom_call" | custom-call | flops 553648128 | bytes 8650752 | tf_op jit(solution)/shard_map/pallas_call | solution.py:334
  50.1 2.1 copy-done.1
  52.2 3.8 %all-to-all-done.1 = bf16[32,128,256]{2,1,0:T(8,128)(2,1)S(1)} async-done(((bf16[32,128,256]{2,1,0:T(8,128)(2,1)}), bf16[32,128,256]{2,1,0:T(8,128)(2,1)S(1)}, u32[]{:S(2)}, u32[]{:S(2)}) %all-to-all-start.1) | async-done | bytes 2097184 | tf_op jit(solution)/shard_map/all_to_all | solution.py:330
  56.0 4.4 %shard_map.115 = (bf16[256,256]{1,0:T(8,128)(2,1)S(1)}, bf16[256,256]{1,0:T(8,128)(2,1)S(1)}, f32[256,1]{1,0:T(8,128)S(1)}, bf16[32,16,256]{2,1,0:T(8,128)(2,1)S(1)}) custom-call(bf16[528,4096]{1,0:T(8,128)(2,1)} %copy-done.1, bf16[4096,256]{1,0:T(8,128)(2,1)S(1)} %bitcast.12, f32[256,256]{1,0:T(8,128)S(1)} %shard_map.114.scaling_ref), custom_call_target="tpu_custom_call" | custom-call | flops 1107296256 | bytes 6422528 | tf_op jit(solution)/shard_map/pallas_call | solution.py:349
  60.4 13.1 %all_to_all.37.negs_ref = bf16[32,16,256]{2,1,0:T(8,128)(2,1)S(1)} all-to-all(bf16[32,16,256]{2,1,0:T(8,128)(2,1)S(1)} %get-tuple-element.22), channel_id=1, replica_groups=mesh['feat'=32,'dp'=16] {'feat'}, dimensions={0} | all-to-all | bytes 524288 | tf_op jit(solution)/shard_map/all_to_all | solution.py:362
  73.4 1.2 shard_map.116
  74.6 12.4 %all_to_all.38.gneg_ref = bf16[32,16,256]{2,1,0:T(8,128)(2,1)S(1)} all-to-all(bf16[32,16,256]{2,1,0:T(8,128)(2,1)S(1)} %get-tuple-element.26), channel_id=1, replica_groups=mesh['feat'=32,'dp'=16] {'feat'}, dimensions={0} | all-to-all | bytes 524288 | tf_op jit(solution)/shard_map/all_to_all | solution.py:374
  87.1 1.8 shard_map.117
  88.9 32.4 %all_to_all.39.grads_ref = bf16[64,128,128]{2,1,0:T(8,128)(2,1)S(1)} all-to-all(bf16[64,128,128]{2,1,0:T(8,128)(2,1)S(1)} %shard_map.117), channel_id=1, replica_groups={{0,1,16,17,32,33,48,49,64,65,80,81,96,97,112,113,128,129,144,145,160,16..., dimensions={0} | all-to-all | bytes 4194304 | tf_op jit(solution)/shard_map/all_to_all | solution.py:311
  121.3 2.7 %shard_map.119 = bf16[4,256,128]{2,1,0:T(8,128)(2,1)S(1)} custom-call(s32[1]{0:T(128)} %bitcast.2.place_ref, s32[64,128]{1,0:T(8,128)S(1)} %bitcast.18, bf16[64,128,128]{2,1,0:T(8,128)(2,1)S(1)} %all_to_all.39.grads_ref), custom_call_target="tpu_custom_call" | custom-call | flops 2147483648 | tf_op jit(solution)/shard_map/pallas_call | solution.py:385
  124.0 0.0 copy-start.6
  124.0 5.1 %collective-permute-start = (bf16[4,256,128]{2,1,0:T(8,128)(2,1)S(1)}, bf16[4,256,128]{2,1,0:T(8,128)(2,1)S(1)}, u32[]{:S(2)}, u32[]{:S(2)}) collective-permute-start(bf16[4,256,128]{2,1,0:T(8,128)(2,1)S(1)} %shard_map.119), channel_id=1, source_target_pairs={{0,2},{1,3},{2,0},{3,1},{4,6},{5,7},{6,4},{7,5},{8,10},{9,11},{10,... | collective-permute-start | bytes 786440 | tf_op jit(solution)/shard_map/ppermute | solution.py:400
  129.1 2.7 %shard_map.118 = bf16[4,256,128]{2,1,0:T(8,128)(2,1)S(1)} custom-call(s32[1]{0:T(128)} %bitcast.2.place_ref, s32[64,128]{1,0:T(8,128)S(1)} %bitcast.19, bf16[64,128,128]{2,1,0:T(8,128)(2,1)S(1)} %all_to_all.39.grads_ref), custom_call_target="tpu_custom_call" | custom-call | flops 2147483648 | bytes 2097152 | tf_op jit(solution)/shard_map/pallas_call | solution.py:392
  131.8 0.0 copy-start.5
  131.8 10.0 %collective-permute-done = bf16[4,256,128]{2,1,0:T(8,128)(2,1)S(1)} collective-permute-done((bf16[4,256,128]{2,1,0:T(8,128)(2,1)S(1)}, bf16[4,256,128]{2,1,0:T(8,128)(2,1)S(1)}, u32[]{:S(2)}, u32[]{:S(2)}) %collective-permute-start) | collective-permute-done | bytes 262176 | tf_op jit(solution)/shard_map/ppermute | solution.py:400
  141.8 0.1 add_convert_fusion
  141.9 31.6 %all_to_all.40 = bf16[4,256,128]{2,1,0:T(8,128)(2,1)S(1)} all-to-all(bf16[4,256,128]{2,1,0:T(8,128)(2,1)S(1)} %add_convert_fusion), channel_id=1, replica_groups={{0,4,8,12},{1,5,9,13},{2,6,10,14},{3,7,11,15},{16,20,24,28},{17,21,25,2..., dimensions={0} | all-to-all | bytes 524288 | tf_op jit(solution)/shard_map/all_to_all | solution.py:403
  173.5 20.3 %all-gather = bf16[1024,128]{1,0:T(8,128)(2,1)S(1)} all-gather(bf16[256,128]{1,0:T(8,128)(2,1)S(1)} %reduce_sum.12), channel_id=2, replica_groups={{0,4,8,12},{1,5,9,13},{2,6,10,14},{3,7,11,15},{16,20,24,28},{17,21,25,2..., dimensions={0}, use_global_device_ids=true | all-gather | bytes 327680 | tf_op jit(solution)/shard_map/all_gather | solution.py:412
  193.7 5.0 %collective-permute-start.3 = (bf16[4,256,128]{2,1,0:T(8,128)(2,1)S(1)}, bf16[4,256,128]{2,1,0:T(8,128)(2,1)S(1)}, u32[]{:S(2)}, u32[]{:S(2)}) collective-permute-start(bf16[4,256,128]{2,1,0:T(8,128)(2,1)S(1)} %bitcast.13), channel_id=1, source_target_pairs={{0,2},{1,3},{2,4},{3,5},{4,6},{5,7},{6,8},{7,9},{8,10},{9,11},{10,... | collective-permute-start | bytes 786440 | tf_op jit(solution)/shard_map/ppermute | solution.py:304
  198.8 3.5 %collective-permute-start.2 = (bf16[4,256,128]{2,1,0:T(8,128)(2,1)S(1)}, bf16[4,256,128]{2,1,0:T(8,128)(2,1)S(1)}, u32[]{:S(2)}, u32[]{:S(2)}) collective-permute-start(bf16[4,256,128]{2,1,0:T(8,128)(2,1)S(1)} %bitcast.14), channel_id=1, source_target_pairs={{0,15},{1,0},{2,1},{3,2},{4,3},{5,4},{6,5},{7,6},{8,7},{9,8},{10,9... | collective-permute-start | bytes 786440 | tf_op jit(solution)/shard_map/ppermute | solution.py:304
  202.3 2.3 %collective-permute-start.1 = (bf16[4,256,128]{2,1,0:T(8,128)(2,1)S(1)}, bf16[4,256,128]{2,1,0:T(8,128)(2,1)S(1)}, u32[]{:S(2)}, u32[]{:S(2)}) collective-permute-start(bf16[4,256,128]{2,1,0:T(8,128)(2,1)S(1)} %bitcast.15), channel_id=1, source_target_pairs={{0,1},{1,2},{2,3},{3,4},{4,5},{5,6},{6,7},{7,8},{8,9},{9,10},{10,1... | collective-permute-start | bytes 786440 | tf_op jit(solution)/shard_map/ppermute | solution.py:304
  204.6 4.6 %collective-permute-done.3.beyond_ref = bf16[4,256,128]{2,1,0:T(8,128)(2,1)S(1)} collective-permute-done((bf16[4,256,128]{2,1,0:T(8,128)(2,1)S(1)}, bf16[4,256,128]{2,1,0:T(8,128)(2,1)S(1)}, u32[]{:S(2)}, u32[]{:S(2)}) %collective-permute-start.3) | collective-permute-done | bytes 262176 | tf_op jit(solution)/shard_map/ppermute | solution.py:304
  209.2 3.4 %collective-permute-done.1.below_ref = bf16[4,256,128]{2,1,0:T(8,128)(2,1)S(1)} collective-permute-done((bf16[4,256,128]{2,1,0:T(8,128)(2,1)S(1)}, bf16[4,256,128]{2,1,0:T(8,128)(2,1)S(1)}, u32[]{:S(2)}, u32[]{:S(2)}) %collective-permute-start.1) | collective-permute-done | bytes 262176 | tf_op jit(solution)/shard_map/ppermute | solution.py:304
  212.6 2.1 shard_map.120
  (21 shorter events, 0.1 us)
Async XLA Ops:
  16.8 1.2 copy-start.4
  22.7 1.3 copy-start.3
  24.0 6.1 %copy-start.7 = (s32[256]{0:T(256)S(1)}, s32[256]{0:T(256)}, u32[]{:S(2)}) copy-start(s32[256]{0:T(256)} %param.17) | copy-start | bytes 3076
  24.0 31.9 %all-to-all-start.1 = ((bf16[32,128,256]{2,1,0:T(8,128)(2,1)}), bf16[32,128,256]{2,1,0:T(8,128)(2,1)S(1)}, u32[]{:S(2)}, u32[]{:S(2)}) async-start(bf16[32,128,256]{2,1,0:T(8,128)(2,1)} %copy-done.3), calls=%async_computation.1 | async-start | bytes 4194304 | tf_op jit(solution)/shard_map/all_to_all | solution.py:330
  30.1 2.4 %copy-start.9 = (s32[1,32]{1,0:T(1,128)S(1)}, s32[1,32]{1,0:T(1,128)}, u32[]{:S(2)}) copy-start(s32[1,32]{1,0:T(1,128)} %counts_ref.1) | copy-start | bytes 388
  30.2 1.6 copy-start.2
  31.7 0.8 copy-start.10
  31.8 0.8 copy-start.11
  31.8 0.8 copy-start.8
  50.1 2.1 copy-start.1
  56.0 31.1 %copy-start = (bf16[4096,528]{1,0:T(8,128)(2,1)S(1)}, bf16[4096,528]{1,0:T(8,128)(2,1)}, u32[]{:S(2)}) copy-start(bf16[4096,528]{1,0:T(8,128)(2,1)} %get-tuple-element.24.counts_ref) | copy-start | bytes 12976132
  124.0 88.6 %copy-start.6 = (f32[2048]{0:T(1024)S(1)}, f32[2048]{0:T(1024)}, u32[]{:S(2)}) copy-start(f32[2048]{0:T(1024)} %param.10) | copy-start | bytes 24580
  124.0 17.8 %collective-permute-start = (bf16[4,256,128]{2,1,0:T(8,128)(2,1)S(1)}, bf16[4,256,128]{2,1,0:T(8,128)(2,1)S(1)}, u32[]{:S(2)}, u32[]{:S(2)}) collective-permute-start(bf16[4,256,128]{2,1,0:T(8,128)(2,1)S(1)} %shard_map.119), channel_id=1, source_target_pairs={{0,2},{1,3},{2,0},{3,1},{4,6},{5,7},{6,4},{7,5},{8,10},{9,11},{10,... | collective-permute-start | bytes 786440 | tf_op jit(solution)/shard_map/ppermute | solution.py:400
  131.8 80.8 %copy-start.5 = (bf16[2048,256]{1,0:T(8,128)(2,1)S(1)}, bf16[2048,256]{1,0:T(8,128)(2,1)}, u32[]{:S(2)}) copy-start(bf16[2048,256]{1,0:T(8,128)(2,1)} %table_ref.3) | copy-start | bytes 3145732
  193.7 15.5 %collective-permute-start.3 = (bf16[4,256,128]{2,1,0:T(8,128)(2,1)S(1)}, bf16[4,256,128]{2,1,0:T(8,128)(2,1)S(1)}, u32[]{:S(2)}, u32[]{:S(2)}) collective-permute-start(bf16[4,256,128]{2,1,0:T(8,128)(2,1)S(1)} %bitcast.13), channel_id=1, source_target_pairs={{0,2},{1,3},{2,4},{3,5},{4,6},{5,7},{6,8},{7,9},{8,10},{9,11},{10,... | collective-permute-start | bytes 786440 | tf_op jit(solution)/shard_map/ppermute | solution.py:304
  198.8 10.4 %collective-permute-start.2 = (bf16[4,256,128]{2,1,0:T(8,128)(2,1)S(1)}, bf16[4,256,128]{2,1,0:T(8,128)(2,1)S(1)}, u32[]{:S(2)}, u32[]{:S(2)}) collective-permute-start(bf16[4,256,128]{2,1,0:T(8,128)(2,1)S(1)} %bitcast.14), channel_id=1, source_target_pairs={{0,15},{1,0},{2,1},{3,2},{4,3},{5,4},{6,5},{7,6},{8,7},{9,8},{10,9... | collective-permute-start | bytes 786440 | tf_op jit(solution)/shard_map/ppermute | solution.py:304
  202.3 10.3 %collective-permute-start.1 = (bf16[4,256,128]{2,1,0:T(8,128)(2,1)S(1)}, bf16[4,256,128]{2,1,0:T(8,128)(2,1)S(1)}, u32[]{:S(2)}, u32[]{:S(2)}) collective-permute-start(bf16[4,256,128]{2,1,0:T(8,128)(2,1)S(1)} %bitcast.15), channel_id=1, source_target_pairs={{0,1},{1,2},{2,3},{3,4},{4,5},{5,6},{6,7},{7,8},{8,9},{9,10},{10,1... | collective-permute-start | bytes 786440 | tf_op jit(solution)/shard_map/ppermute | solution.py:304

commit v8 on v6

--- a/solution.py
+++ b/solution.py
@@ -16,12 +16,13 @@
 
 VM = pl.BlockSpec(memory_space=pltpu.VMEM)
 SM = pl.BlockSpec(memory_space=pltpu.SMEM)
+ANY = pl.BlockSpec(memory_space=pl.ANY)
 MIB = 1 << 20
 LIMIT = 48
 
 
-def call(body, out_shape, in_specs, scratch=(), flops=0, moved=0, limit=LIMIT):
-    outs = jax.tree.map(lambda _: VM, out_shape)
+def call(body, out_shape, in_specs, outs=None, scratch=(), flops=0, moved=0, limit=LIMIT):
+    outs = jax.tree.map(lambda _: VM, out_shape) if outs is None else outs
     return pl.pallas_call(
         body,
         out_shape=out_shape,
@@ -45,22 +46,27 @@
     return lax.broadcasted_iota(i32, dims, axis).astype(i16)
 
 
-def gather_rows(place_ref, asked_ref, table_ref, out_ref):
-    sources, cap, width = out_ref.shape
-    rows = table_ref.shape[0]
+def gather_rows(place_ref, asked_ref, table_ref, out_ref, held_ref, sems):
+    sources, cap, width = held_ref.shape
     even = (place_ref[0] & 1) == 0
     columns = asked_ref[...].T
-    lanes = narrow_iota((cap, rows), 1)
-    group = 8
-    for first in range(0, sources, group):
+    lanes = narrow_iota((cap, table_ref.shape[0]), 1)
+    group = sources // sems.shape[0]
+    copies = []
+    for k in range(sems.shape[0]):
+        span = slice(k * group, (k + 1) * group)
         picks = []
-        for s in range(first, first + group):
+        for s in range(k * group, (k + 1) * group):
             column = jnp.where(
                 even, columns[:, 2 * s : 2 * s + 1], columns[:, 2 * s + 1 : 2 * s + 2]
             )
             picks.append(ones_where(lanes == column.astype(i16)))
         got = jnp.dot(jnp.concatenate(picks, axis=0), table_ref[...], preferred_element_type=f32)
-        out_ref[first : first + group] = got.astype(bf16).reshape(group, cap, width)
+        held_ref[span] = got.astype(bf16).reshape(group, cap, width)
+        copies.append(pltpu.make_async_copy(held_ref.at[span], out_ref.at[span], sems.at[k]))
+        copies[-1].start()
+    for copy in copies:
+        copy.wait()
 
 
 def count_entries(counts_ref, bags_ref, neg_ref, by_item_ref, by_slot_ref):
@@ -228,6 +234,8 @@
     table_out_ref,
     state_out_ref,
     sums_ref,
+    fresh_ref,
+    sems,
 ):
     half = own_ref.shape[2]
     chunk = own_ref.shape[1]
@@ -239,6 +247,7 @@
     sums_ref[(kind + 2) & 3, 2:] = high_ref[...]
     step = state_ref.shape[1]
     eye = lax.broadcasted_iota(i32, (step, step), 0) == lax.broadcasted_iota(i32, (step, step), 1)
+    copies = []
     for c in range(8):
         at = 2 * (c % 2)
         whole = jnp.concatenate(
@@ -256,9 +265,16 @@
             state_out_ref[line : line + 1, :] = jnp.sum(
                 jnp.where(eye, fresh, 0.0), axis=0, keepdims=True
             )
-            table_out_ref[at, :] = (
+            fresh_ref[at, :] = (
                 table_ref[at, :].astype(f32) - learn_rate * gradient / jnp.sqrt(fresh)
             ).astype(bf16)
+        span = pl.ds(c * chunk, chunk)
+        copies.append(
+            pltpu.make_async_copy(fresh_ref.at[span, :], table_out_ref.at[span, :], sems.at[c])
+        )
+        copies[-1].start()
+    for copy in copies:
+        copy.wait()
 
 
 def on_device(
@@ -307,6 +323,9 @@
         gather_rows,
         shape((n_feat, cap, width), bf16),
         [SM, VM, VM],
+        outs=ANY,
+        scratch=[pltpu.VMEM((n_feat, cap, width), bf16), pltpu.SemaphoreType.DMA((8,))],
+        limit=60,
         flops=2 * slots * rows * width,
         moved=rows * width * 2 + slots * width * 2,
     )(place, asked, feature_table)
@@ -398,7 +417,12 @@
         update,
         (shape((rows, width), bf16), shape((rows // 128, 128), f32)),
         [SM] + [VM] * 7,
-        scratch=[pltpu.VMEM((4, 4, chunk, half), bf16)],
+        outs=(ANY, VM),
+        scratch=[
+            pltpu.VMEM((4, 4, chunk, half), bf16),
+            pltpu.VMEM((rows, width), bf16),
+            pltpu.SemaphoreType.DMA((8,)),
+        ],
     )(place, feature_table, row_state.reshape(rows // 128, 128), quad, below, above, low, high)
     return (loss.reshape(trip), new_table, new_state.reshape(rows))
 

time: 213 us -> 213 us (level)
  Pallas kernels: 37.1 us -> 39.7 us
  local copies, waits for them, and re-layouts: 6.96 us -> 4.44 us
    unnamed x24 -> x22, local copies, waits for them, and re-layouts: 6.21 us -> 3.69 us
    pallas_call x1, Pallas kernels: 4.66 us -> 6.84 us  [on_device(): call(gather_rows, shape((n_feat, cap, width), bf16), [SM, VM, VM], outs=A...]
where the time goes in v8:
time: 213 us; the launch traced here: 212 us
  blocking collectives  125 us (59%)
  Pallas kernels  39.7 us (19%)
  starting transfers between devices  31.2 us (15%)
  waiting for transfers between devices  11 us (5%)
  local copies, waits for them, and re-layouts  4.44 us (2%)
    all_to_all x2, blocking collectives, across_pairs(): lax.all_to_all(value, ('feat', 'dp'), split_axis=0, concat_axis=0, tiled=...  50.6 us
    all_to_all x1, blocking collectives, on_device(): lax.all_to_all(kept, 'dp', split_axis=0, concat_axis=0, tiled=True, axis_...  28.7 us
    ppermute x6, starting transfers between devices, shift(): lax.ppermute(value, 'dp', [(i, (i + by) % n_dp) for i in range(n_dp)])  26 us
    all_gather x1, blocking collectives, on_device(): quad = lax.all_gather(summed, 'dp', axis=0, axis_index_groups=apart)  19.4 us
    pallas_call x1, Pallas kernels, on_device(): call(count_entries, (shape((items, slots), bf16), shape((slots, items), b...  17.6 us
    all_to_all x1, blocking collectives, on_device(): lax.all_to_all(own_negs, 'feat', split_axis=0, concat_axis=0, tiled=True)  13.7 us
    all_to_all x1, blocking collectives, on_device(): gneg = lax.all_to_all(gneg, 'feat', split_axis=0, concat_axis=0, tiled=True)  12.4 us
    ppermute x6, waiting for transfers between devices, shift(): lax.ppermute(value, 'dp', [(i, (i + by) % n_dp) for i in range(n_dp)])  7.13 us
  transfers between devices with their start and end apart: 7, of which 4 were waited for; matrix products, arithmetic and copies ran while one was open for 0% of the time, Pallas kernels for 10%

profile of v8, /device:TPU:2, one launch (start us, length us, event | category | flops | bytes accessed | tf_op | source)
XLA Modules:
  0.0 212.3 jit_solution(7387413077430408052)
XLA Ops:
  0.6 0.7 broadcast_in_dim.8
  1.4 17.0 %all_to_all.36 = s32[64,1,128]{2,1,0:T(1,128)} all-to-all(s32[64,1,128]{2,1,0:T(1,128)S(1)} %bitcast.23), channel_id=1, replica_groups={{0,1,16,17,32,33,48,49,64,65,80,81,96,97,112,113,128,129,144,145,160,16..., dimensions={0} | all-to-all | bytes 65536 | tf_op jit(solution)/shard_map/all_to_all | solution.py:310
  18.4 6.8 %shard_map.113 = bf16[32,128,256]{2,1,0:T(8,128)(2,1)} custom-call(s32[1]{0:T(128)} %bitcast.2.place_ref, s32[64,128]{1,0:T(8,128)} %bitcast.18, bf16[2048,256]{1,0:T(8,128)(2,1)} %table_ref.3), custom_call_target="tpu_custom_call" | custom-call | flops 4294967296 | bytes 3145728 | tf_op jit(solution)/shard_map/pallas_call | solution.py:322
  25.2 0.0 copy-start.6
  25.2 5.2 %all-to-all-start.1 = ((bf16[32,128,256]{2,1,0:T(8,128)(2,1)}), bf16[32,128,256]{2,1,0:T(8,128)(2,1)S(1)}, u32[]{:S(2)}, u32[]{:S(2)}) async-start(bf16[32,128,256]{2,1,0:T(8,128)(2,1)} %shard_map.113), calls=%async_computation.1 | async-start | bytes 4194304 | tf_op jit(solution)/shard_map/all_to_all | solution.py:332
  30.5 0.0 copy-start.8
  30.5 1.6 copy-done.2
  32.1 0.8 shard_map.114.scaling_ref
  32.9 17.6 %shard_map.112 = (bf16[528,4096]{1,0:T(8,128)(2,1)S(1)}, bf16[4096,528]{1,0:T(8,128)(2,1)}) custom-call(s32[1,32]{1,0:T(1,128)S(1)} %copy-done.8, s32[16,512]{1,0:T(8,128)S(1)} %pad_add_fusion.bags_ref, s32[16,16]{1,0:T(8,128)S(1)} %copy-done.7), custom_call_target="tpu_custom_call" | custom-call | flops 553648128 | bytes 8650752 | tf_op jit(solution)/shard_map/pallas_call | solution.py:336
  50.5 2.1 copy-done.1
  52.6 3.9 %all-to-all-done.1 = bf16[32,128,256]{2,1,0:T(8,128)(2,1)S(1)} async-done(((bf16[32,128,256]{2,1,0:T(8,128)(2,1)}), bf16[32,128,256]{2,1,0:T(8,128)(2,1)S(1)}, u32[]{:S(2)}, u32[]{:S(2)}) %all-to-all-start.1) | async-done | bytes 2097184 | tf_op jit(solution)/shard_map/all_to_all | solution.py:332
  56.4 3.7 %shard_map.115 = (bf16[256,256]{1,0:T(8,128)(2,1)S(1)}, bf16[256,256]{1,0:T(8,128)(2,1)S(1)}, f32[256,1]{1,0:T(8,128)S(1)}, bf16[32,16,256]{2,1,0:T(8,128)(2,1)S(1)}) custom-call(bf16[528,4096]{1,0:T(8,128)(2,1)} %copy-done.1, bf16[4096,256]{1,0:T(8,128)(2,1)S(1)} %bitcast.14, f32[256,256]{1,0:T(8,128)S(1)} %shard_map.114.scaling_ref), custom_call_target="tpu_custom_call" | custom-call | flops 1107296256 | bytes 6422528 | tf_op jit(solution)/shard_map/pallas_call | solution.py:351
  60.1 13.7 %all_to_all.37.negs_ref = bf16[32,16,256]{2,1,0:T(8,128)(2,1)S(1)} all-to-all(bf16[32,16,256]{2,1,0:T(8,128)(2,1)S(1)} %get-tuple-element.24), channel_id=1, replica_groups=mesh['feat'=32,'dp'=16] {'feat'}, dimensions={0} | all-to-all | bytes 524288 | tf_op jit(solution)/shard_map/all_to_all | solution.py:363
  73.9 1.2 shard_map.116
  75.1 12.4 %all_to_all.38.gneg_ref = bf16[32,16,256]{2,1,0:T(8,128)(2,1)S(1)} all-to-all(bf16[32,16,256]{2,1,0:T(8,128)(2,1)S(1)} %get-tuple-element.28), channel_id=1, replica_groups=mesh['feat'=32,'dp'=16] {'feat'}, dimensions={0} | all-to-all | bytes 524288 | tf_op jit(solution)/shard_map/all_to_all | solution.py:375
  87.5 1.8 shard_map.117
  89.3 33.6 %all_to_all.39.grads_ref = bf16[64,128,128]{2,1,0:T(8,128)(2,1)S(1)} all-to-all(bf16[64,128,128]{2,1,0:T(8,128)(2,1)S(1)} %shard_map.117), channel_id=1, replica_groups={{0,1,16,17,32,33,48,49,64,65,80,81,96,97,112,113,128,129,144,145,160,16..., dimensions={0} | all-to-all | bytes 4194304 | tf_op jit(solution)/shard_map/all_to_all | solution.py:310
  122.9 2.7 %shard_map.119 = (bf16[2,256,128]{2,1,0:T(8,128)(2,1)S(1)}, bf16[2,256,128]{2,1,0:T(8,128)(2,1)S(1)}) custom-call(s32[1]{0:T(128)} %bitcast.2.place_ref, s32[64,128]{1,0:T(8,128)S(1)} %bitcast.19, bf16[64,128,128]{2,1,0:T(8,128)(2,1)S(1)} %all_to_all.39.grads_ref), custom_call_target="tpu_custom_call" | custom-call | flops 2147483648 | tf_op jit(solution)/shard_map/pallas_call | solution.py:386
  125.6 4.5 %collective-permute-start = (bf16[2,256,128]{2,1,0:T(8,128)(2,1)S(1)}, bf16[2,256,128]{2,1,0:T(8,128)(2,1)S(1)}, u32[]{:S(2)}, u32[]{:S(2)}) collective-permute-start(bf16[2,256,128]{2,1,0:T(8,128)(2,1)S(1)} %get-tuple-element.29), channel_id=1, source_target_pairs={{0,2},{1,3},{2,4},{3,5},{4,6},{5,7},{6,8},{7,9},{8,10},{9,11},{10,... | collective-permute-start | bytes 393224 | tf_op jit(solution)/shard_map/ppermute | solution.py:303
  130.2 7.7 %collective-permute-start.1 = (bf16[2,256,128]{2,1,0:T(8,128)(2,1)S(1)}, bf16[2,256,128]{2,1,0:T(8,128)(2,1)S(1)}, u32[]{:S(2)}, u32[]{:S(2)}) collective-permute-start(bf16[2,256,128]{2,1,0:T(8,128)(2,1)S(1)} %get-tuple-element.30), channel_id=1, source_target_pairs={{0,14},{1,15},{2,0},{3,1},{4,2},{5,3},{6,4},{7,5},{8,6},{9,7},{10,... | collective-permute-start | bytes 393224 | tf_op jit(solution)/shard_map/ppermute | solution.py:303
  137.8 2.7 %shard_map.118 = bf16[4,256,128]{2,1,0:T(8,128)(2,1)S(1)} custom-call(s32[1]{0:T(128)} %bitcast.2.place_ref, s32[64,128]{1,0:T(8,128)S(1)} %bitcast.20, bf16[64,128,128]{2,1,0:T(8,128)(2,1)S(1)} %all_to_all.39.grads_ref), custom_call_target="tpu_custom_call" | custom-call | flops 2147483648 | bytes 2097152 | tf_op jit(solution)/shard_map/pallas_call | solution.py:393
  140.6 1.4 collective-permute-done.1
  141.9 0.1 add_convert_fusion
  142.0 28.7 %all_to_all.40 = bf16[4,256,128]{2,1,0:T(8,128)(2,1)S(1)} all-to-all(bf16[4,256,128]{2,1,0:T(8,128)(2,1)S(1)} %add_convert_fusion), channel_id=1, replica_groups={{0,4,8,12},{1,5,9,13},{2,6,10,14},{3,7,11,15},{16,20,24,28},{17,21,25,2..., dimensions={0} | all-to-all | bytes 524288 | tf_op jit(solution)/shard_map/all_to_all | solution.py:404
  170.7 19.4 %all-gather = bf16[1024,128]{1,0:T(8,128)(2,1)S(1)} all-gather(bf16[256,128]{1,0:T(8,128)(2,1)S(1)} %reduce_sum.12), channel_id=2, replica_groups={{0,4,8,12},{1,5,9,13},{2,6,10,14},{3,7,11,15},{16,20,24,28},{17,21,25,2..., dimensions={0}, use_global_device_ids=true | all-gather | bytes 327680 | tf_op jit(solution)/shard_map/all_gather | solution.py:413
  190.1 3.2 %collective-permute-start.3 = (bf16[4,256,128]{2,1,0:T(8,128)(2,1)S(1)}, bf16[4,256,128]{2,1,0:T(8,128)(2,1)S(1)}, u32[]{:S(2)}, u32[]{:S(2)}) collective-permute-start(bf16[4,256,128]{2,1,0:T(8,128)(2,1)S(1)} %bitcast.15), channel_id=1, source_target_pairs={{0,15},{1,0},{2,1},{3,2},{4,3},{5,4},{6,5},{7,6},{8,7},{9,8},{10,9... | collective-permute-start | bytes 786440 | tf_op jit(solution)/shard_map/ppermute | solution.py:303
  193.3 2.6 %collective-permute-start.2 = (bf16[4,256,128]{2,1,0:T(8,128)(2,1)S(1)}, bf16[4,256,128]{2,1,0:T(8,128)(2,1)S(1)}, u32[]{:S(2)}, u32[]{:S(2)}) collective-permute-start(bf16[4,256,128]{2,1,0:T(8,128)(2,1)S(1)} %bitcast.16), channel_id=1, source_target_pairs={{0,1},{1,2},{2,3},{3,4},{4,5},{5,6},{6,7},{7,8},{8,9},{9,10},{10,1... | collective-permute-start | bytes 786440 | tf_op jit(solution)/shard_map/ppermute | solution.py:303
  196.0 5.1 %collective-permute-start.4 = (bf16[2,256,128]{2,1,0:T(8,128)(2,1)S(1)}, bf16[2,256,128]{2,1,0:T(8,128)(2,1)S(1)}, u32[]{:S(2)}, u32[]{:S(2)}) collective-permute-start(bf16[2,256,128]{2,1,0:T(8,128)(2,1)S(1)} %bitcast.25), channel_id=1, source_target_pairs={{0,2},{1,3},{2,4},{3,5},{4,6},{5,7},{6,8},{7,9},{8,10},{9,11},{10,... | collective-permute-start | bytes 393224 | tf_op jit(solution)/shard_map/ppermute | solution.py:303
  201.1 2.9 %collective-permute-start.5 = (bf16[2,256,128]{2,1,0:T(8,128)(2,1)S(1)}, bf16[2,256,128]{2,1,0:T(8,128)(2,1)S(1)}, u32[]{:S(2)}, u32[]{:S(2)}) collective-permute-start(bf16[2,256,128]{2,1,0:T(8,128)(2,1)S(1)} %bitcast.24), channel_id=1, source_target_pairs={{0,14},{1,15},{2,0},{3,1},{4,2},{5,3},{6,4},{7,5},{8,6},{9,7},{10,... | collective-permute-start | bytes 393224 | tf_op jit(solution)/shard_map/ppermute | solution.py:303
  203.9 1.4 collective-permute-done.4.low_ref
  205.3 4.4 %collective-permute-done.5.high_ref = bf16[2,256,128]{2,1,0:T(8,128)(2,1)S(1)} collective-permute-done((bf16[2,256,128]{2,1,0:T(8,128)(2,1)S(1)}, bf16[2,256,128]{2,1,0:T(8,128)(2,1)S(1)}, u32[]{:S(2)}, u32[]{:S(2)}) %collective-permute-start.5) | collective-permute-done | bytes 131104 | tf_op jit(solution)/shard_map/ppermute | solution.py:303
  209.7 2.4 %shard_map.120 = (bf16[2048,256]{1,0:T(8,128)(2,1)}, f32[16,128]{1,0:T(8,128)}) custom-call(s32[1]{0:T(128)} %bitcast.2.place_ref, bf16[2048,256]{1,0:T(8,128)(2,1)S(1)} %copy-done.3, f32[16,128]{1,0:T(8,128)S(1)} %bitcast.21, bf16[4,256,128]{2,1,0:T(8,128)(2,1)S(1)} %bitcast.17, bf16[4,256,128]{2,1,0:T(8,128)(2,1)S(1)} %collective-permute-done.2.below_ref, ...), custom_call_target="tpu_custom_call" | custom-call | tf_op jit(solution)/shard_map/pallas_call | solution.py:416
  (24 shorter events, 0.1 us)
Async XLA Ops:
  25.2 5.3 %copy-start.6 = (s32[256]{0:T(256)S(1)}, s32[256]{0:T(256)}, u32[]{:S(2)}) copy-start(s32[256]{0:T(256)} %param.17) | copy-start | bytes 3076
  25.2 31.2 %all-to-all-start.1 = ((bf16[32,128,256]{2,1,0:T(8,128)(2,1)}), bf16[32,128,256]{2,1,0:T(8,128)(2,1)S(1)}, u32[]{:S(2)}, u32[]{:S(2)}) async-start(bf16[32,128,256]{2,1,0:T(8,128)(2,1)} %shard_map.113), calls=%async_computation.1 | async-start | bytes 4194304 | tf_op jit(solution)/shard_map/all_to_all | solution.py:332
  30.5 2.4 %copy-start.8 = (s32[1,32]{1,0:T(1,128)S(1)}, s32[1,32]{1,0:T(1,128)}, u32[]{:S(2)}) copy-start(s32[1,32]{1,0:T(1,128)} %counts_ref.1) | copy-start | bytes 388
  30.5 1.6 copy-start.2
  32.1 0.8 copy-start.9
  32.1 0.8 copy-start.10
  32.1 0.8 copy-start.7
  50.5 2.1 copy-start.1
  56.4 31.1 %copy-start = (bf16[4096,528]{1,0:T(8,128)(2,1)S(1)}, bf16[4096,528]{1,0:T(8,128)(2,1)}, u32[]{:S(2)}) copy-start(bf16[4096,528]{1,0:T(8,128)(2,1)} %get-tuple-element.26.counts_ref) | copy-start | bytes 12976132
  89.3 33.6 %copy-start.4 = (s32[64,1,128]{2,1,0:T(1,128)S(1)}, s32[64,1,128]{2,1,0:T(1,128)}, u32[]{:S(2)}) copy-start(s32[64,1,128]{2,1,0:T(1,128)} %all_to_all.36) | copy-start | bytes 98308
  125.6 15.0 %collective-permute-start = (bf16[2,256,128]{2,1,0:T(8,128)(2,1)S(1)}, bf16[2,256,128]{2,1,0:T(8,128)(2,1)S(1)}, u32[]{:S(2)}, u32[]{:S(2)}) collective-permute-start(bf16[2,256,128]{2,1,0:T(8,128)(2,1)S(1)} %get-tuple-element.29), channel_id=1, source_target_pairs={{0,2},{1,3},{2,4},{3,5},{4,6},{5,7},{6,8},{7,9},{8,10},{9,11},{10,... | collective-permute-start | bytes 393224 | tf_op jit(solution)/shard_map/ppermute | solution.py:303
  130.2 11.8 %collective-permute-start.1 = (bf16[2,256,128]{2,1,0:T(8,128)(2,1)S(1)}, bf16[2,256,128]{2,1,0:T(8,128)(2,1)S(1)}, u32[]{:S(2)}, u32[]{:S(2)}) collective-permute-start(bf16[2,256,128]{2,1,0:T(8,128)(2,1)S(1)} %get-tuple-element.30), channel_id=1, source_target_pairs={{0,14},{1,15},{2,0},{3,1},{4,2},{5,3},{6,4},{7,5},{8,6},{9,7},{10,... | collective-permute-start | bytes 393224 | tf_op jit(solution)/shard_map/ppermute | solution.py:303
  140.5 69.2 %copy-start.3 = (bf16[2048,256]{1,0:T(8,128)(2,1)S(1)}, bf16[2048,256]{1,0:T(8,128)(2,1)}, u32[]{:S(2)}) copy-start(bf16[2048,256]{1,0:T(8,128)(2,1)} %table_ref.3) | copy-start | bytes 3145732
  140.6 69.2 %copy-start.5 = (f32[2048]{0:T(1024)S(1)}, f32[2048]{0:T(1024)}, u32[]{:S(2)}) copy-start(f32[2048]{0:T(1024)} %param.10) | copy-start | bytes 24580
  190.1 19.6 %collective-permute-start.3 = (bf16[4,256,128]{2,1,0:T(8,128)(2,1)S(1)}, bf16[4,256,128]{2,1,0:T(8,128)(2,1)S(1)}, u32[]{:S(2)}, u32[]{:S(2)}) collective-permute-start(bf16[4,256,128]{2,1,0:T(8,128)(2,1)S(1)} %bitcast.15), channel_id=1, source_target_pairs={{0,15},{1,0},{2,1},{3,2},{4,3},{5,4},{6,5},{7,6},{8,7},{9,8},{10,9... | collective-permute-start | bytes 786440 | tf_op jit(solution)/shard_map/ppermute | solution.py:303
  193.3 16.4 %collective-permute-start.2 = (bf16[4,256,128]{2,1,0:T(8,128)(2,1)S(1)}, bf16[4,256,128]{2,1,0:T(8,128)(2,1)S(1)}, u32[]{:S(2)}, u32[]{:S(2)}) collective-permute-start(bf16[4,256,128]{2,1,0:T(8,128)(2,1)S(1)} %bitcast.16), channel_id=1, source_target_pairs={{0,1},{1,2},{2,3},{3,4},{4,5},{5,6},{6,7},{7,8},{8,9},{9,10},{10,1... | collective-permute-start | bytes 786440 | tf_op jit(solution)/shard_map/ppermute | solution.py:303
  196.0 9.3 %collective-permute-start.4 = (bf16[2,256,128]{2,1,0:T(8,128)(2,1)S(1)}, bf16[2,256,128]{2,1,0:T(8,128)(2,1)S(1)}, u32[]{:S(2)}, u32[]{:S(2)}) collective-permute-start(bf16[2,256,128]{2,1,0:T(8,128)(2,1)S(1)} %bitcast.25), channel_id=1, source_target_pairs={{0,2},{1,3},{2,4},{3,5},{4,6},{5,7},{6,8},{7,9},{8,10},{9,11},{10,... | collective-permute-start | bytes 393224 | tf_op jit(solution)/shard_map/ppermute | solution.py:303
  201.1 8.6 %collective-permute-start.5 = (bf16[2,256,128]{2,1,0:T(8,128)(2,1)S(1)}, bf16[2,256,128]{2,1,0:T(8,128)(2,1)S(1)}, u32[]{:S(2)}, u32[]{:S(2)}) collective-permute-start(bf16[2,256,128]{2,1,0:T(8,128)(2,1)S(1)} %bitcast.24), channel_id=1, source_target_pairs={{0,14},{1,15},{2,0},{3,1},{4,2},{5,3},{6,4},{7,5},{8,6},{9,7},{10,... | collective-permute-start | bytes 393224 | tf_op jit(solution)/shard_map/ppermute | solution.py:303

commit v9 on v6

--- a/solution.py
+++ b/solution.py
@@ -16,12 +16,13 @@
 
 VM = pl.BlockSpec(memory_space=pltpu.VMEM)
 SM = pl.BlockSpec(memory_space=pltpu.SMEM)
+ANY = pl.BlockSpec(memory_space=pl.ANY)
 MIB = 1 << 20
 LIMIT = 48
 
 
-def call(body, out_shape, in_specs, scratch=(), flops=0, moved=0, limit=LIMIT):
-    outs = jax.tree.map(lambda _: VM, out_shape)
+def call(body, out_shape, in_specs, outs=None, scratch=(), flops=0, moved=0, limit=LIMIT):
+    outs = jax.tree.map(lambda _: VM, out_shape) if outs is None else outs
     return pl.pallas_call(
         body,
         out_shape=out_shape,
@@ -45,20 +46,16 @@
     return lax.broadcasted_iota(i32, dims, axis).astype(i16)
 
 
-def gather_rows(place_ref, asked_ref, table_ref, out_ref):
+def gather_rows(asked_ref, table_ref, out_ref):
     sources, cap, width = out_ref.shape
-    rows = table_ref.shape[0]
-    even = (place_ref[0] & 1) == 0
     columns = asked_ref[...].T
-    lanes = narrow_iota((cap, rows), 1)
+    lanes = narrow_iota((cap, table_ref.shape[0]), 1)
     group = 8
     for first in range(0, sources, group):
-        picks = []
-        for s in range(first, first + group):
-            column = jnp.where(
-                even, columns[:, 2 * s : 2 * s + 1], columns[:, 2 * s + 1 : 2 * s + 2]
-            )
-            picks.append(ones_where(lanes == column.astype(i16)))
+        picks = [
+            ones_where(lanes == columns[:, s : s + 1].astype(i16))
+            for s in range(first, first + group)
+        ]
         got = jnp.dot(jnp.concatenate(picks, axis=0), table_ref[...], preferred_element_type=f32)
         out_ref[first : first + group] = got.astype(bf16).reshape(group, cap, width)
 
@@ -122,7 +119,7 @@
         )
 
 
-def pool(counts_ref, fetched_ref, scaling_ref, query_ref, tails_ref, positive_ref, negs_ref):
+def pool(counts_ref, fetched_ref, scaling_ref, _, query_ref, tails_ref, positive_ref, negs_ref):
     bag = 16
     trip = query_ref.shape[0]
     pooled = jnp.dot(counts_ref[...], fetched_ref[...], preferred_element_type=f32)
@@ -171,24 +168,31 @@
     grads_ref[trip:] = (score_scale * (p_pos - 1.0) * query_f * (1.0 / bag)).astype(bf16)
 
 
-def spread(counts_ref, grads_ref, gneg_ref, out_ref):
+def spread(counts_ref, grads_ref, gneg_ref, out_ref, held_ref, sems):
     bag = 16
     blocks, cap, half = out_ref.shape
+    pieces = sems.shape[0]
+    group = blocks // 2 // pieces
+    spans = [pl.ds(k * group * cap, group * cap) for k in range(pieces)]
+    copies = [
+        pltpu.make_async_copy(counts_ref.at[span, :], held_ref.at[span, :], sems.at[k])
+        for k, span in enumerate(spans)
+    ]
+    for copy in copies:
+        copy.start()
     gneg = jnp.sum(gneg_ref[...].astype(f32), axis=0) * (1.0 / bag)
     grads = jnp.concatenate([grads_ref[...], gneg.astype(bf16)], axis=0)
-    group = 8
-    for first in range(0, blocks // 2, group):
-        slot = jnp.dot(
-            counts_ref[first * cap : (first + group) * cap, :], grads, preferred_element_type=f32
-        ).astype(bf16)
+    for k, (copy, span) in enumerate(zip(copies, spans)):
+        copy.wait()
+        slot = jnp.dot(held_ref[span, :], grads, preferred_element_type=f32).astype(bf16)
         for s in range(group):
             for h in range(2):
-                out_ref[2 * (first + s) + h] = slot[
+                out_ref[2 * (k * group + s) + h] = slot[
                     s * cap : (s + 1) * cap, h * half : (h + 1) * half
                 ]
 
 
-def collect(turn, place_ref, asked_ref, grads_ref, *refs):
+def collect(turn, place_ref, own_ref, other_ref, grads_ref, *refs):
     out_refs, acc_ref = refs[:-1], refs[-1]
     blocks, cap, half = grads_ref.shape
     chunk = acc_ref.shape[1] // 4
@@ -196,11 +200,13 @@
     parity = 1 - parity if turn else parity
     lane = lax.broadcasted_iota(i32, (cap, 4 * chunk), 1)
     row = (lane + (lane // chunk + parity) * chunk).astype(i16)
-    columns = asked_ref[...].T
+    even = (place_ref[0] & 1) == 0
+    own, other = own_ref[...].T, other_ref[...].T
+    columns = (jnp.where(even, own, other), jnp.where(even, other, own))
     group = 8
     for first in range(0, blocks, group):
         picks = [
-            ones_where(row == columns[:, b : b + 1].astype(i16))
+            ones_where(row == columns[b % 2][:, b // 2 : b // 2 + 1].astype(i16))
             for b in range(first, first + group)
         ]
         part = jnp.dot(
@@ -290,26 +296,16 @@
         [f * n_dp + 2 * p + h for f in range(n_feat) for h in range(2)] for p in range(n_dp // 2)
     ]
 
-    def across_pairs(value):
-        return lax.all_to_all(
-            value,
-            ("feat", "dp"),
-            split_axis=0,
-            concat_axis=0,
-            tiled=True,
-            axis_index_groups=pairs,
-        )
-
     place, slot_rows = lax.optimization_barrier((place, slot_rows))
-    twice = jnp.broadcast_to(slot_rows[0][:, None], (n_feat, 2, cap)).reshape(2 * n_feat, cap)
-    asked = across_pairs(twice)
+    asked = lax.all_to_all(slot_rows[0], "feat", split_axis=0, concat_axis=0, tiled=True)
+    asked_other = lax.ppermute(asked, "dp", [(i, i ^ 1) for i in range(n_dp)])
     served = call(
         gather_rows,
         shape((n_feat, cap, width), bf16),
-        [SM, VM, VM],
+        [VM, VM],
         flops=2 * slots * rows * width,
         moved=rows * width * 2 + slots * width * 2,
-    )(place, asked, feature_table)
+    )(asked, feature_table)
     fetched = lax.all_to_all(served, "feat", split_axis=0, concat_axis=0, tiled=True)
     fetched = fetched.reshape(slots, width)
 
@@ -337,10 +333,10 @@
             shape((trip, 1), f32),
             shape((n_feat, n_neg, width), bf16),
         ),
-        [VM, VM, VM],
+        [VM, VM, VM, ANY],
         flops=2 * items * slots * width,
         moved=2 * slots * (width + items),
-    )(by_item, fetched, scaling)
+    )(by_item, fetched, scaling, asked_other)
     negs = lax.all_to_all(own_negs, "feat", split_axis=0, concat_axis=0, tiled=True)
     loss, gneg, grads = call(
         score,
@@ -357,28 +353,35 @@
     slot_grad = call(
         spread,
         shape((2 * n_feat, cap, half), bf16),
-        [VM, VM, VM],
-        limit=24,
+        [ANY, VM, VM],
+        scratch=[pltpu.VMEM((slots, items), bf16), pltpu.SemaphoreType.DMA((8,))],
         flops=2 * items * slots * width,
     )(by_slot, grads, gneg)
-    arrived = across_pairs(slot_grad)
+    arrived = lax.all_to_all(
+        slot_grad,
+        ("feat", "dp"),
+        split_axis=0,
+        concat_axis=0,
+        tiled=True,
+        axis_index_groups=pairs,
+    )
     chunk = rows // 8
     scratch = [pltpu.VMEM((half, 4 * chunk), f32)]
     up, down = call(
         functools.partial(collect, 1),
         (shape((2, chunk, half), bf16), shape((2, chunk, half), bf16)),
-        [SM, VM, VM],
+        [SM, VM, VM, VM],
         scratch=scratch,
         flops=2 * slots * rows * half,
-    )(place, asked, arrived)
+    )(place, asked, asked_other, arrived)
     kept = call(
         functools.partial(collect, 0),
         shape((4, chunk, half), bf16),
-        [SM, VM, VM],
+        [SM, VM, VM, VM],
         scratch=scratch,
         flops=2 * slots * rows * half,
         moved=2 * slots * width,
-    )(place, asked, arrived)
+    )(place, asked, asked_other, arrived)
     nearby = jnp.concatenate([shift(up, 2), shift(down, -2)], axis=0)
     kept = (kept.astype(f32) + nearby.astype(f32)).astype(bf16)
     apart = [[h + 4 * j for j in range(4)] for h in range(4)]

time: 213 us -> 215 us (level)
  Pallas kernels: 37.1 us -> 40.8 us
  local copies, waits for them, and re-layouts: 6.96 us -> 4.64 us
    pallas_call x2, Pallas kernels: 6.45 us -> 10.2 us  [the longest x1 5.6 us: on_device(): call(spread, shape((2 * n_feat, cap, half), bf16), [ANY, VM, VM], scratch...]
    all_to_all x1, waiting for transfers between devices: 3.86 us -> 0.63 us  [on_device(): lax.all_to_all(served, 'feat', split_axis=0, concat_axis=0, tiled=True)]
    ppermute x0 -> x1, waiting for transfers between devices: none -> 2.86 us  [on_device(): asked_other = lax.ppermute(asked, 'dp', [(i, i ^ 1) for i in range(n_dp)])]
    unnamed x24 -> x22, local copies, waits for them, and re-layouts: 6.21 us -> 4.62 us
  transfers between devices with their start and end apart: 7 -> 8, of which waited for: 4 -> 5; matrix products, arithmetic and copies ran while one was open for 0% -> 0% of each run, Pallas kernels for 10% -> 10%
where the time goes in v9:
time: 215 us; the launch traced here: 214 us
  blocking collectives  124 us (58%)
  Pallas kernels  40.8 us (19%)
  starting transfers between devices  33.4 us (16%)
  waiting for transfers between devices  10.6 us (5%)
  local copies, waits for them, and re-layouts  4.64 us (2%)
    all_to_all x1, blocking collectives, on_device(): lax.all_to_all(slot_grad, ('feat', 'dp'), split_axis=0, concat_axis=0, ti...  33.6 us
    all_to_all x1, blocking collectives, on_device(): lax.all_to_all(kept, 'dp', split_axis=0, concat_axis=0, tiled=True, axis_...  28.7 us
    ppermute x6, starting transfers between devices, shift(): lax.ppermute(value, 'dp', [(i, (i + by) % n_dp) for i in range(n_dp)])  26.1 us
    all_gather x1, blocking collectives, on_device(): quad = lax.all_gather(summed, 'dp', axis=0, axis_index_groups=apart)  19.3 us
    pallas_call x1, Pallas kernels, on_device(): call(count_entries, (shape((items, slots), bf16), shape((slots, items), b...  17.6 us
    all_to_all x1, blocking collectives, on_device(): lax.all_to_all(slot_rows[0], 'feat', split_axis=0, concat_axis=0, tiled=T...  15.6 us
    all_to_all x1, blocking collectives, on_device(): lax.all_to_all(own_negs, 'feat', split_axis=0, concat_axis=0, tiled=True)  14.3 us
    all_to_all x1, blocking collectives, on_device(): gneg = lax.all_to_all(gneg, 'feat', split_axis=0, concat_axis=0, tiled=True)  12.4 us
  transfers between devices with their start and end apart: 8, of which 5 were waited for; matrix products, arithmetic and copies ran while one was open for 0% of the time, Pallas kernels for 10%

profile of v9, /device:TPU:2, one launch (start us, length us, event | category | flops | bytes accessed | tf_op | source)
XLA Modules:
  0.0 214.3 jit_solution(13740840274222213906)
XLA Ops:
  0.6 15.6 %all_to_all.36 = s32[32,1,128]{2,1,0:T(1,128)S(1)} all-to-all(s32[32,1,128]{2,1,0:T(1,128)} %bitcast.25), channel_id=1, replica_groups=mesh['feat'=32,'dp'=16] {'feat'}, dimensions={0} | all-to-all | bytes 32768 | tf_op jit(solution)/shard_map/all_to_all | solution.py:300
  16.2 1.2 copy-done.3
  17.5 4.6 %shard_map.113 = bf16[32,128,256]{2,1,0:T(8,128)(2,1)S(1)} custom-call(s32[32,128]{1,0:T(8,128)S(1)} %bitcast.17, bf16[2048,256]{1,0:T(8,128)(2,1)S(1)} %copy-done.3), custom_call_target="tpu_custom_call" | custom-call | flops 4294967296 | bytes 3145728 | tf_op jit(solution)/shard_map/pallas_call | solution.py:302
  22.1 1.3 copy-done.2
  23.4 5.3 %all-to-all-start.1 = ((bf16[32,128,256]{2,1,0:T(8,128)(2,1)}), bf16[32,128,256]{2,1,0:T(8,128)(2,1)S(1)}, u32[]{:S(2)}, u32[]{:S(2)}) async-start(bf16[32,128,256]{2,1,0:T(8,128)(2,1)} %copy-done.2), calls=%async_computation.1 | async-start | bytes 4194304 | tf_op jit(solution)/shard_map/all_to_all | solution.py:309
  28.7 17.6 %shard_map.112 = (bf16[528,4096]{1,0:T(8,128)(2,1)S(1)}, bf16[4096,528]{1,0:T(8,128)(2,1)}) custom-call(s32[1,32]{1,0:T(1,128)S(1)} %copy-done.8, s32[16,512]{1,0:T(8,128)S(1)} %pad_add_fusion.bags_ref, s32[16,16]{1,0:T(8,128)S(1)} %copy-done.7), custom_call_target="tpu_custom_call" | custom-call | flops 553648128 | bytes 8650752 | tf_op jit(solution)/shard_map/pallas_call | solution.py:313
  46.3 2.1 copy-done
  48.4 1.9 collective-permute-start
  50.3 0.8 shard_map.114.scaling_ref
  51.1 2.9 %collective-permute-done._.other_ref = s32[32,128]{1,0:T(8,128)S(1)} collective-permute-done((s32[32,128]{1,0:T(8,128)S(1)}, s32[32,128]{1,0:T(8,128)S(1)}, u32[]{:S(2)}, u32[]{:S(2)}) %collective-permute-start) | collective-permute-done | bytes 16416 | tf_op jit(solution)/shard_map/ppermute | solution.py:301
  54.0 0.6 all-to-all-done.1
  54.6 3.6 %shard_map.115 = (bf16[256,256]{1,0:T(8,128)(2,1)S(1)}, bf16[256,256]{1,0:T(8,128)(2,1)S(1)}, f32[256,1]{1,0:T(8,128)S(1)}, bf16[32,16,256]{2,1,0:T(8,128)(2,1)S(1)}) custom-call(bf16[528,4096]{1,0:T(8,128)(2,1)} %copy-done, bf16[4096,256]{1,0:T(8,128)(2,1)S(1)} %bitcast.13, f32[256,256]{1,0:T(8,128)S(1)} %shard_map.114.scaling_ref, ...), custom_call_target="tpu_custom_call" | custom-call | flops 1107296256 | bytes 6422528 | tf_op jit(solution)/shard_map/pallas_call | solution.py:328
  58.2 14.3 %all_to_all.37.negs_ref = bf16[32,16,256]{2,1,0:T(8,128)(2,1)S(1)} all-to-all(bf16[32,16,256]{2,1,0:T(8,128)(2,1)S(1)} %get-tuple-element.23), channel_id=1, replica_groups=mesh['feat'=32,'dp'=16] {'feat'}, dimensions={0} | all-to-all | bytes 524288 | tf_op jit(solution)/shard_map/all_to_all | solution.py:340
  72.5 1.2 shard_map.116
  73.7 12.4 %all_to_all.38.gneg_ref = bf16[32,16,256]{2,1,0:T(8,128)(2,1)S(1)} all-to-all(bf16[32,16,256]{2,1,0:T(8,128)(2,1)S(1)} %get-tuple-element.28), channel_id=1, replica_groups=mesh['feat'=32,'dp'=16] {'feat'}, dimensions={0} | all-to-all | bytes 524288 | tf_op jit(solution)/shard_map/all_to_all | solution.py:352
  86.2 5.6 %shard_map.117 = bf16[64,128,128]{2,1,0:T(8,128)(2,1)S(1)} custom-call(bf16[4096,528]{1,0:T(8,128)(2,1)} %get-tuple-element.26.counts_ref, bf16[512,256]{1,0:T(8,128)(2,1)S(1)} %get-tuple-element.27.grads_ref, bf16[32,16,256]{2,1,0:T(8,128)(2,1)S(1)} %all_to_all.38.gneg_ref), custom_call_target="tpu_custom_call" | custom-call | flops 1107296256 | tf_op jit(solution)/shard_map/pallas_call | solution.py:353
  91.8 33.6 %all_to_all.39.grads_ref = bf16[64,128,128]{2,1,0:T(8,128)(2,1)S(1)} all-to-all(bf16[64,128,128]{2,1,0:T(8,128)(2,1)S(1)} %shard_map.117), channel_id=1, replica_groups={{0,1,16,17,32,33,48,49,64,65,80,81,96,97,112,113,128,129,144,145,160,16..., dimensions={0} | all-to-all | bytes 4194304 | tf_op jit(solution)/shard_map/all_to_all | solution.py:360
  125.4 2.7 %shard_map.119 = (bf16[2,256,128]{2,1,0:T(8,128)(2,1)S(1)}, bf16[2,256,128]{2,1,0:T(8,128)(2,1)S(1)}) custom-call(s32[1]{0:T(128)} %bitcast.2.place_ref, s32[32,128]{1,0:T(8,128)S(1)} %bitcast.19, s32[32,128]{1,0:T(8,128)S(1)} %collective-permute-done._.other_ref, bf16[64,128,128]{2,1,0:T(8,128)(2,1)S(1)} %all_to_all.39.grads_ref), custom_call_target="tpu_custom_call" | custom-call | flops 2147483648 | tf_op jit(solution)/shard_map/pallas_call | solution.py:370
  128.1 4.7 %collective-permute-start.1 = (bf16[2,256,128]{2,1,0:T(8,128)(2,1)S(1)}, bf16[2,256,128]{2,1,0:T(8,128)(2,1)S(1)}, u32[]{:S(2)}, u32[]{:S(2)}) collective-permute-start(bf16[2,256,128]{2,1,0:T(8,128)(2,1)S(1)} %get-tuple-element.29), channel_id=1, source_target_pairs={{0,2},{1,3},{2,4},{3,5},{4,6},{5,7},{6,8},{7,9},{8,10},{9,11},{10,... | collective-permute-start | bytes 393224 | tf_op jit(solution)/shard_map/ppermute | solution.py:293
  132.8 7.7 %collective-permute-start.2 = (bf16[2,256,128]{2,1,0:T(8,128)(2,1)S(1)}, bf16[2,256,128]{2,1,0:T(8,128)(2,1)S(1)}, u32[]{:S(2)}, u32[]{:S(2)}) collective-permute-start(bf16[2,256,128]{2,1,0:T(8,128)(2,1)S(1)} %get-tuple-element.30), channel_id=1, source_target_pairs={{0,14},{1,15},{2,0},{3,1},{4,2},{5,3},{6,4},{7,5},{8,6},{9,7},{10,... | collective-permute-start | bytes 393224 | tf_op jit(solution)/shard_map/ppermute | solution.py:293
  140.5 2.7 %shard_map.118 = bf16[4,256,128]{2,1,0:T(8,128)(2,1)S(1)} custom-call(s32[1]{0:T(128)} %bitcast.2.place_ref, s32[32,128]{1,0:T(8,128)S(1)} %bitcast.20, s32[32,128]{1,0:T(8,128)S(1)} %collective-permute-done._.other_ref, bf16[64,128,128]{2,1,0:T(8,128)(2,1)S(1)} %all_to_all.39.grads_ref), custom_call_target="tpu_custom_call" | custom-call | flops 2147483648 | bytes 2097152 | tf_op jit(solution)/shard_map/pallas_call | solution.py:377
  143.2 1.3 collective-permute-done.2
  144.5 0.1 add_convert_fusion
  144.6 28.7 %all_to_all.40 = bf16[4,256,128]{2,1,0:T(8,128)(2,1)S(1)} all-to-all(bf16[4,256,128]{2,1,0:T(8,128)(2,1)S(1)} %add_convert_fusion), channel_id=1, replica_groups={{0,4,8,12},{1,5,9,13},{2,6,10,14},{3,7,11,15},{16,20,24,28},{17,21,25,2..., dimensions={0} | all-to-all | bytes 524288 | tf_op jit(solution)/shard_map/all_to_all | solution.py:388
  173.3 19.3 %all-gather = bf16[1024,128]{1,0:T(8,128)(2,1)S(1)} all-gather(bf16[256,128]{1,0:T(8,128)(2,1)S(1)} %reduce_sum.12), channel_id=2, replica_groups={{0,4,8,12},{1,5,9,13},{2,6,10,14},{3,7,11,15},{16,20,24,28},{17,21,25,2..., dimensions={0}, use_global_device_ids=true | all-gather | bytes 327680 | tf_op jit(solution)/shard_map/all_gather | solution.py:397
  192.7 3.2 %collective-permute-start.4 = (bf16[4,256,128]{2,1,0:T(8,128)(2,1)S(1)}, bf16[4,256,128]{2,1,0:T(8,128)(2,1)S(1)}, u32[]{:S(2)}, u32[]{:S(2)}) collective-permute-start(bf16[4,256,128]{2,1,0:T(8,128)(2,1)S(1)} %bitcast.14), channel_id=1, source_target_pairs={{0,15},{1,0},{2,1},{3,2},{4,3},{5,4},{6,5},{7,6},{8,7},{9,8},{10,9... | collective-permute-start | bytes 786440 | tf_op jit(solution)/shard_map/ppermute | solution.py:293
  195.9 2.6 %collective-permute-start.3 = (bf16[4,256,128]{2,1,0:T(8,128)(2,1)S(1)}, bf16[4,256,128]{2,1,0:T(8,128)(2,1)S(1)}, u32[]{:S(2)}, u32[]{:S(2)}) collective-permute-start(bf16[4,256,128]{2,1,0:T(8,128)(2,1)S(1)} %bitcast.15), channel_id=1, source_target_pairs={{0,1},{1,2},{2,3},{3,4},{4,5},{5,6},{6,7},{7,8},{8,9},{9,10},{10,1... | collective-permute-start | bytes 786440 | tf_op jit(solution)/shard_map/ppermute | solution.py:293
  198.5 5.1 %collective-permute-start.5 = (bf16[2,256,128]{2,1,0:T(8,128)(2,1)S(1)}, bf16[2,256,128]{2,1,0:T(8,128)(2,1)S(1)}, u32[]{:S(2)}, u32[]{:S(2)}) collective-permute-start(bf16[2,256,128]{2,1,0:T(8,128)(2,1)S(1)} %bitcast.24), channel_id=1, source_target_pairs={{0,2},{1,3},{2,4},{3,5},{4,6},{5,7},{6,8},{7,9},{8,10},{9,11},{10,... | collective-permute-start | bytes 393224 | tf_op jit(solution)/shard_map/ppermute | solution.py:293
  203.6 2.9 %collective-permute-start.6 = (bf16[2,256,128]{2,1,0:T(8,128)(2,1)S(1)}, bf16[2,256,128]{2,1,0:T(8,128)(2,1)S(1)}, u32[]{:S(2)}, u32[]{:S(2)}) collective-permute-start(bf16[2,256,128]{2,1,0:T(8,128)(2,1)S(1)} %bitcast.23), channel_id=1, source_target_pairs={{0,14},{1,15},{2,0},{3,1},{4,2},{5,3},{6,4},{7,5},{8,6},{9,7},{10,... | collective-permute-start | bytes 393224 | tf_op jit(solution)/shard_map/ppermute | solution.py:293
  206.5 1.2 collective-permute-done.5.low_ref
  207.7 4.5 %collective-permute-done.6.high_ref = bf16[2,256,128]{2,1,0:T(8,128)(2,1)S(1)} collective-permute-done((bf16[2,256,128]{2,1,0:T(8,128)(2,1)S(1)}, bf16[2,256,128]{2,1,0:T(8,128)(2,1)S(1)}, u32[]{:S(2)}, u32[]{:S(2)}) %collective-permute-start.6) | collective-permute-done | bytes 131104 | tf_op jit(solution)/shard_map/ppermute | solution.py:293
  212.3 2.1 shard_map.120
  (25 shorter events, 0.1 us)
Async XLA Ops:
  16.2 1.2 copy-start.3
  22.1 1.3 copy-start.2
  23.4 5.3 %copy-start.9 = (s32[256,16]{0,1:T(8,128)S(1)}, s32[256,16]{0,1:T(8,128)}, u32[]{:S(2)}) copy-start(s32[256,16]{0,1:T(8,128)} %param.15) | copy-start | bytes 49156
  23.4 5.3 %copy-start.10 = (s32[256,16]{0,1:T(8,128)S(1)}, s32[256,16]{0,1:T(8,128)}, u32[]{:S(2)}) copy-start(s32[256,16]{0,1:T(8,128)} %param.14) | copy-start | bytes 49156
  23.4 5.3 %copy-start.7 = (s32[16,16]{1,0:T(8,128)S(1)}, s32[16,16]{1,0:T(8,128)}, u32[]{:S(2)}) copy-start(s32[16,16]{1,0:T(8,128)} %neg_ref.1) | copy-start | bytes 3076
  23.4 5.3 %copy-start.8 = (s32[1,32]{1,0:T(1,128)S(1)}, s32[1,32]{1,0:T(1,128)}, u32[]{:S(2)}) copy-start(s32[1,32]{1,0:T(1,128)} %counts_ref.1) | copy-start | bytes 388
  23.4 31.2 %all-to-all-start.1 = ((bf16[32,128,256]{2,1,0:T(8,128)(2,1)}), bf16[32,128,256]{2,1,0:T(8,128)(2,1)S(1)}, u32[]{:S(2)}, u32[]{:S(2)}) async-start(bf16[32,128,256]{2,1,0:T(8,128)(2,1)} %copy-done.2), calls=%async_computation.1 | async-start | bytes 4194304 | tf_op jit(solution)/shard_map/all_to_all | solution.py:309
  28.7 21.7 %copy-start.1 = (bf16[4096,256]{1,0:T(8,128)(2,1)S(1)}, bf16[4096,256]{1,0:T(8,128)(2,1)}, u32[]{:S(2)}) copy-start(bf16[4096,256]{1,0:T(8,128)(2,1)} %rel_ref.1) | copy-start | bytes 6291460
  28.7 21.6 %copy-start.6 = (s32[256]{0:T(256)S(1)}, s32[256]{0:T(256)}, u32[]{:S(2)}) copy-start(s32[256]{0:T(256)} %param.17) | copy-start | bytes 3076
  46.3 2.1 copy-start
  48.4 5.6 %collective-permute-start = (s32[32,128]{1,0:T(8,128)S(1)}, s32[32,128]{1,0:T(8,128)S(1)}, u32[]{:S(2)}, u32[]{:S(2)}) collective-permute-start(s32[32,128]{1,0:T(8,128)S(1)} %bitcast.18), channel_id=1, source_target_pairs={{0,1},{1,0},{2,3},{3,2},{4,5},{5,4},{6,7},{7,6},{8,9},{9,8},{10,11... | collective-permute-start | bytes 49160 | tf_op jit(solution)/shard_map/ppermute | solution.py:301
  128.1 15.1 %collective-permute-start.1 = (bf16[2,256,128]{2,1,0:T(8,128)(2,1)S(1)}, bf16[2,256,128]{2,1,0:T(8,128)(2,1)S(1)}, u32[]{:S(2)}, u32[]{:S(2)}) collective-permute-start(bf16[2,256,128]{2,1,0:T(8,128)(2,1)S(1)} %get-tuple-element.29), channel_id=1, source_target_pairs={{0,2},{1,3},{2,4},{3,5},{4,6},{5,7},{6,8},{7,9},{8,10},{9,11},{10,... | collective-permute-start | bytes 393224 | tf_op jit(solution)/shard_map/ppermute | solution.py:293
  132.8 11.8 %collective-permute-start.2 = (bf16[2,256,128]{2,1,0:T(8,128)(2,1)S(1)}, bf16[2,256,128]{2,1,0:T(8,128)(2,1)S(1)}, u32[]{:S(2)}, u32[]{:S(2)}) collective-permute-start(bf16[2,256,128]{2,1,0:T(8,128)(2,1)S(1)} %get-tuple-element.30), channel_id=1, source_target_pairs={{0,14},{1,15},{2,0},{3,1},{4,2},{5,3},{6,4},{7,5},{8,6},{9,7},{10,... | collective-permute-start | bytes 393224 | tf_op jit(solution)/shard_map/ppermute | solution.py:293
  143.2 69.1 %copy-start.4 = (bf16[2048,256]{1,0:T(8,128)(2,1)S(1)}, bf16[2048,256]{1,0:T(8,128)(2,1)}, u32[]{:S(2)}) copy-start(bf16[2048,256]{1,0:T(8,128)(2,1)} %table_ref.3) | copy-start | bytes 3145732
  143.2 69.1 %copy-start.5 = (f32[2048]{0:T(1024)S(1)}, f32[2048]{0:T(1024)}, u32[]{:S(2)}) copy-start(f32[2048]{0:T(1024)} %param.10) | copy-start | bytes 24580
  192.7 19.6 %collective-permute-start.4 = (bf16[4,256,128]{2,1,0:T(8,128)(2,1)S(1)}, bf16[4,256,128]{2,1,0:T(8,128)(2,1)S(1)}, u32[]{:S(2)}, u32[]{:S(2)}) collective-permute-start(bf16[4,256,128]{2,1,0:T(8,128)(2,1)S(1)} %bitcast.14), channel_id=1, source_target_pairs={{0,15},{1,0},{2,1},{3,2},{4,3},{5,4},{6,5},{7,6},{8,7},{9,8},{10,9... | collective-permute-start | bytes 786440 | tf_op jit(solution)/shard_map/ppermute | solution.py:293
  195.9 16.3 %collective-permute-start.3 = (bf16[4,256,128]{2,1,0:T(8,128)(2,1)S(1)}, bf16[4,256,128]{2,1,0:T(8,128)(2,1)S(1)}, u32[]{:S(2)}, u32[]{:S(2)}) collective-permute-start(bf16[4,256,128]{2,1,0:T(8,128)(2,1)S(1)} %bitcast.15), channel_id=1, source_target_pairs={{0,1},{1,2},{2,3},{3,4},{4,5},{5,6},{6,7},{7,8},{8,9},{9,10},{10,1... | collective-permute-start | bytes 786440 | tf_op jit(solution)/shard_map/ppermute | solution.py:293
  198.5 9.2 %collective-permute-start.5 = (bf16[2,256,128]{2,1,0:T(8,128)(2,1)S(1)}, bf16[2,256,128]{2,1,0:T(8,128)(2,1)S(1)}, u32[]{:S(2)}, u32[]{:S(2)}) collective-permute-start(bf16[2,256,128]{2,1,0:T(8,128)(2,1)S(1)} %bitcast.24), channel_id=1, source_target_pairs={{0,2},{1,3},{2,4},{3,5},{4,6},{5,7},{6,8},{7,9},{8,10},{9,11},{10,... | collective-permute-start | bytes 393224 | tf_op jit(solution)/shard_map/ppermute | solution.py:293
  203.6 8.6 %collective-permute-start.6 = (bf16[2,256,128]{2,1,0:T(8,128)(2,1)S(1)}, bf16[2,256,128]{2,1,0:T(8,128)(2,1)S(1)}, u32[]{:S(2)}, u32[]{:S(2)}) collective-permute-start(bf16[2,256,128]{2,1,0:T(8,128)(2,1)S(1)} %bitcast.23), channel_id=1, source_target_pairs={{0,14},{1,15},{2,0},{3,1},{4,2},{5,3},{6,4},{7,5},{8,6},{9,7},{10,... | collective-permute-start | bytes 393224 | tf_op jit(solution)/shard_map/ppermute | solution.py:293
